TPU v7x, 32 devices: a whole 2x2x4 slice. The times are simulated.
32 devices in a mesh: img: 2 (over x), row: 16 (over z, y, core).
Axes of the slice: x: 2, y: 2, z: 4, core: 2. Of those that a mesh axis runs over, the one named last changes fastest.
Arguments:
- inputs: bfloat16 [32, 16, 96, 256], P('row', 'img'), may hold values from -6 to 6
- cotangent: bfloat16 [32, 16, 96, 256], P('row', 'img'), may hold values from -6 to 6
- rows_gain: float32 [256], replicated, may hold values from 0.25 to 1.75
- rows_query: bfloat16 [256, 256], replicated, may hold values from -0.5 to 0.5
- rows_keys: bfloat16 [256, 256], replicated, may hold values from -0.5 to 0.5
- rows_values: bfloat16 [256, 256], replicated, may hold values from -0.375 to 0.375
- rows_mixer: bfloat16 [256, 256], replicated, may hold values from -1 to 1
- rows_scale: float32 [256], replicated, may hold values from 0.25 to 1.75
- rows_expand: bfloat16 [256, 1024], replicated, may hold values from -0.375 to 0.375
- rows_shrink: bfloat16 [1024, 256], replicated, may hold values from -0.375 to 0.375
- column_gain: float32 [256], replicated, may hold values from 0.25 to 1.75
- column_query: bfloat16 [256, 256], replicated, may hold values from -0.5 to 0.5
- column_keys: bfloat16 [256, 256], replicated, may hold values from -0.5 to 0.5
- column_values: bfloat16 [256, 256], replicated, may hold values from -0.375 to 0.375
- column_mixer: bfloat16 [256, 256], replicated, may hold values from -1 to 1
- column_scale: float32 [256], replicated, may hold values from 0.25 to 1.75
- column_expand: bfloat16 [256, 1024], replicated, may hold values from -0.375 to 0.375
- column_shrink: bfloat16 [1024, 256], replicated, may hold values from -0.375 to 0.375
Outputs:
- output: bfloat16 [32, 16, 96, 256], P('row', 'img')
- input_grad: float32 [32, 16, 96, 256], P('row', 'img')
- rows_gain_grad: float32 [256], replicated
- rows_query_grad: float32 [256, 256], replicated
- rows_keys_grad: float32 [256, 256], replicated
- rows_values_grad: float32 [256, 256], replicated
- rows_mixer_grad: float32 [256, 256], replicated
- rows_scale_grad: float32 [256], replicated
- rows_expand_grad: float32 [256, 1024], replicated
- rows_shrink_grad: float32 [1024, 256], replicated
- column_gain_grad: float32 [256], replicated
- column_query_grad: float32 [256, 256], replicated
- column_keys_grad: float32 [256, 256], replicated
- column_values_grad: float32 [256, 256], replicated
- column_mixer_grad: float32 [256, 256], replicated
- column_scale_grad: float32 [256], replicated
- column_expand_grad: float32 [256, 1024], replicated
- column_shrink_grad: float32 [1024, 256], replicated
All inputs are finite; a program needn't handle non-finite values.
Results may differ from a plain program's by a relative error of at most 0.023.
The roundings to bfloat16 on the way count: a program that leaves them out, or rounds other values in their place, can miss the bound.
Values may be sent and summed in bfloat16 or wider, within the bound.
No kernel may reach another device: no remote copies, remote signals or barrier semaphores. Data moves between devices by JAX's collectives and lax.ppermute only.
A program may use at most 448 MiB of HBM per device.

v0:
```python
import math

import jax
import jax.numpy as jnp
from jax import lax
from jax.sharding import PartitionSpec as P

HEADS = 2


EPS = 1e-05


def outer_sum(left, right):
    return lax.dot_general(
        left, right, (((0,), (0,)), ((), ())), preferred_element_type=jnp.float32
    )


def times_back(grads, weight):
    return lax.dot_general(
        grads, weight, (((1,), (1,)), ((), ())), preferred_element_type=jnp.float32
    )


def normalize(stream, gain):
    centred = stream - jnp.mean(stream, axis=-1, keepdims=True)
    inverse = lax.rsqrt(jnp.mean(centred * centred, axis=-1, keepdims=True) + EPS)
    normal = centred * inverse
    return (normal * gain, normal, inverse)


def normalize_back(upstream, normal, inverse, gain):
    scaled = upstream * gain
    centred = (
        scaled
        - jnp.mean(scaled, axis=-1, keepdims=True)
        - normal * jnp.mean(scaled * normal, axis=-1, keepdims=True)
    )
    return (inverse * centred, jnp.sum(upstream * normal, axis=0))


def split_heads(tensor):
    return tensor.reshape(tensor.shape[:-1] + (HEADS, tensor.shape[-1] // HEADS))


def head_scaling(tensor):
    return 1.0 / math.sqrt(tensor.shape[-1] // HEADS)


def rows_forward(query_in, key_in, value_in):
    scaling = head_scaling(query_in)
    scores = (
        jnp.einsum(
            "rbihe,rbjhe->rbhij",
            split_heads(query_in),
            split_heads(key_in),
            preferred_element_type=jnp.float32,
        )
        * scaling
    )
    places = jnp.arange(scores.shape[-1])
    visible = places[:, None] >= places[None, :]
    softened = jax.nn.softmax(jnp.where(visible, scores, -jnp.inf), axis=-1)
    attended = jnp.einsum(
        "rbhij,rbjhe->rbihe",
        softened.astype(jnp.bfloat16),
        split_heads(value_in),
        preferred_element_type=jnp.float32,
    )
    return (attended.astype(jnp.bfloat16).reshape(query_in.shape), softened)


def rows_backward(upstream, query_in, key_in, value_in, softened):
    scaling = head_scaling(query_in)
    up_heads = split_heads(upstream)
    query_heads = split_heads(query_in)
    prob_grad = jnp.einsum(
        "rbihe,rbjhe->rbhij", up_heads, split_heads(value_in), preferred_element_type=jnp.float32
    )
    score_grad = (
        softened * (prob_grad - jnp.sum(softened * prob_grad, axis=-1, keepdims=True))
    ).astype(jnp.bfloat16)
    query_grad = (
        jnp.einsum(
            "rbhij,rbjhe->rbihe",
            score_grad,
            split_heads(key_in),
            preferred_element_type=jnp.float32,
        )
        * scaling
    )
    key_grad = (
        jnp.einsum(
            "rbhij,rbihe->rbjhe", score_grad, query_heads, preferred_element_type=jnp.float32
        )
        * scaling
    )
    value_grad = jnp.einsum(
        "rbhij,rbihe->rbjhe",
        softened.astype(jnp.bfloat16),
        up_heads,
        preferred_element_type=jnp.float32,
    )
    return tuple(
        (
            each.astype(jnp.bfloat16).reshape(query_in.shape)
            for each in (query_grad, key_grad, value_grad)
        )
    )


def column_scores(query_heads, key_heads, query_first, scaling):
    scores = (
        jnp.einsum("ibche,jbche->ibchj", query_heads, key_heads, preferred_element_type=jnp.float32)
        * scaling
    )
    query_rows = query_first + jnp.arange(query_heads.shape[0])
    key_rows = jnp.arange(key_heads.shape[0])
    visible = query_rows[:, None, None, None, None] >= key_rows[None, None, None, None, :]
    return jnp.where(visible, scores, -jnp.inf)


def columns_forward(query_in, key_in, value_in):
    height = query_in.shape[0]
    first_row = lax.axis_index("row") * height
    scaling = head_scaling(query_in)
    query_heads = split_heads(query_in)
    section = column_scores(
        query_heads,
        split_heads(lax.all_gather(key_in, "row", axis=0, tiled=True)),
        first_row,
        scaling,
    )
    scores = section
    softened = jax.nn.softmax(scores, axis=-1)
    soft_low = softened.astype(jnp.bfloat16)
    section = soft_low
    attended = jnp.einsum(
        "ibchj,jbche->ibche",
        section,
        split_heads(lax.all_gather(value_in, "row", axis=0, tiled=True)),
        preferred_element_type=jnp.float32,
    )
    return (attended.astype(jnp.bfloat16).reshape(query_in.shape), softened)


def columns_backward(upstream, query_in, key_in, value_in, retained):
    scaling = head_scaling(query_in)
    query_heads = split_heads(query_in)
    up_heads = split_heads(upstream)
    channels = query_in.shape[-1]
    section = jnp.einsum(
        "ibche,jbche->ibchj",
        up_heads,
        split_heads(lax.all_gather(value_in, "row", axis=0, tiled=True)),
        preferred_element_type=jnp.float32,
    )
    prob_grad = section
    score_grad = (
        retained * (prob_grad - jnp.sum(retained * prob_grad, axis=-1, keepdims=True))
    ).astype(jnp.bfloat16)
    soft_low = retained.astype(jnp.bfloat16)
    section = score_grad
    query_grad = (
        jnp.einsum(
            "ibchj,jbche->ibche",
            section,
            split_heads(lax.all_gather(key_in, "row", axis=0, tiled=True)),
            preferred_element_type=jnp.float32,
        )
        * scaling
    )
    key_grad = (
        jnp.einsum(
            "ibchj,ibche->jbche", score_grad, query_heads, preferred_element_type=jnp.float32
        )
        * scaling
    )
    value_grad = jnp.einsum(
        "ibchj,ibche->jbche", soft_low, up_heads, preferred_element_type=jnp.float32
    )
    target = (lax.axis_size("row") * query_in.shape[0],) + query_in.shape[1:]
    combined = lax.psum_scatter(
        jnp.concatenate([key_grad.reshape(target), value_grad.reshape(target)], axis=-1).astype(
            jnp.bfloat16
        ),
        "row",
        scatter_dimension=0,
        tiled=True,
    ).astype(jnp.float32)
    key_grad = combined[..., :channels].astype(jnp.bfloat16)
    value_grad = combined[..., channels:].astype(jnp.bfloat16)
    return (query_grad.astype(jnp.bfloat16).reshape(query_in.shape), key_grad, value_grad)


def block_forward(stream, weights, attend, grid_shape):
    gain_a, query_w, key_w, value_w, mixer_w, gain_b, expand_w, shrink_w = weights
    normed_a, normal_a, inverse_a = normalize(stream, gain_a)
    lowered_a = normed_a.astype(jnp.bfloat16)
    query_in = (
        jnp.dot(lowered_a, query_w, preferred_element_type=jnp.float32)
        .astype(jnp.bfloat16)
        .reshape(grid_shape)
    )
    key_in = (
        jnp.dot(lowered_a, key_w, preferred_element_type=jnp.float32)
        .astype(jnp.bfloat16)
        .reshape(grid_shape)
    )
    value_in = (
        jnp.dot(lowered_a, value_w, preferred_element_type=jnp.float32)
        .astype(jnp.bfloat16)
        .reshape(grid_shape)
    )
    attended, retained = attend(query_in, key_in, value_in)
    attended_flat = attended.reshape(-1, grid_shape[-1])
    middle = stream + jnp.dot(attended_flat, mixer_w, preferred_element_type=jnp.float32)
    normed_b, normal_b, inverse_b = normalize(middle, gain_b)
    lowered_b = normed_b.astype(jnp.bfloat16)
    expanded = jnp.dot(lowered_b, expand_w, preferred_element_type=jnp.float32)
    hidden = jax.nn.gelu(expanded).astype(jnp.bfloat16)
    result = middle + jnp.dot(hidden, shrink_w, preferred_element_type=jnp.float32)
    stored = (
        lowered_a,
        normal_a,
        inverse_a,
        query_in,
        key_in,
        value_in,
        attended_flat,
        retained,
        normal_b,
        inverse_b,
        lowered_b,
        expanded,
        hidden,
    )
    return (result, stored)


def block_backward(upstream, weights, stored, attend_back, grid_shape):
    gain_a, query_w, key_w, value_w, mixer_w, gain_b, expand_w, shrink_w = weights
    (
        lowered_a,
        normal_a,
        inverse_a,
        query_in,
        key_in,
        value_in,
        attended_flat,
        retained,
        normal_b,
        inverse_b,
        lowered_b,
        expanded,
        hidden,
    ) = stored
    branch_low = upstream.astype(jnp.bfloat16)
    shrink_grad = outer_sum(hidden, branch_low)
    hidden_grad = times_back(branch_low, shrink_w)
    expanded_grad = jax.vjp(jax.nn.gelu, expanded)[1](hidden_grad)[0].astype(jnp.bfloat16)
    expand_grad = outer_sum(lowered_b, expanded_grad)
    lowered_b_grad = times_back(expanded_grad, expand_w)
    middle_norm, scale_grad = normalize_back(lowered_b_grad, normal_b, inverse_b, gain_b)
    middle_grad = upstream + middle_norm
    middle_low = middle_grad.astype(jnp.bfloat16)
    mixer_grad = outer_sum(attended_flat, middle_low)
    attended_grad = times_back(middle_low, mixer_w).astype(jnp.bfloat16).reshape(grid_shape)
    query_grad, key_grad, value_grad = attend_back(
        attended_grad, query_in, key_in, value_in, retained
    )
    channels = grid_shape[-1]
    query_flat = query_grad.reshape(-1, channels)
    key_flat = key_grad.reshape(-1, channels)
    value_flat = value_grad.reshape(-1, channels)
    query_w_grad = outer_sum(lowered_a, query_flat)
    key_w_grad = outer_sum(lowered_a, key_flat)
    value_w_grad = outer_sum(lowered_a, value_flat)
    lowered_a_grad = (
        times_back(query_flat, query_w)
        + times_back(key_flat, key_w)
        + times_back(value_flat, value_w)
    )
    stream_norm, gain_grad = normalize_back(lowered_a_grad, normal_a, inverse_a, gain_a)
    return (
        middle_grad + stream_norm,
        (
            gain_grad,
            query_w_grad,
            key_w_grad,
            value_w_grad,
            mixer_grad,
            scale_grad,
            expand_grad,
            shrink_grad,
        ),
    )


def on_device(
    inputs,
    cotangent,
    rows_gain,
    rows_query,
    rows_keys,
    rows_values,
    rows_mixer,
    rows_scale,
    rows_expand,
    rows_shrink,
    column_gain,
    column_query,
    column_keys,
    column_values,
    column_mixer,
    column_scale,
    column_expand,
    column_shrink,
):
    grid_shape = inputs.shape
    channels = grid_shape[-1]
    rows_weights = (
        rows_gain,
        rows_query,
        rows_keys,
        rows_values,
        rows_mixer,
        rows_scale,
        rows_expand,
        rows_shrink,
    )
    column_weights = (
        column_gain,
        column_query,
        column_keys,
        column_values,
        column_mixer,
        column_scale,
        column_expand,
        column_shrink,
    )
    stream = inputs.astype(jnp.float32).reshape(-1, channels)
    between, stored_rows = block_forward(stream, rows_weights, rows_forward, grid_shape)
    final, stored_columns = block_forward(between, column_weights, columns_forward, grid_shape)
    upstream = cotangent.astype(jnp.float32).reshape(-1, channels)
    between_grad, grads_columns = block_backward(
        upstream, column_weights, stored_columns, columns_backward, grid_shape
    )
    stream_grad, grads_rows = block_backward(
        between_grad, rows_weights, stored_rows, rows_backward, grid_shape
    )
    totals = lax.psum(
        (
            grads_rows[0],
            grads_rows[1],
            grads_rows[2],
            grads_rows[3],
            grads_rows[4],
            grads_rows[5],
            grads_rows[6],
            grads_rows[7],
            grads_columns[0],
            grads_columns[1],
            grads_columns[2],
            grads_columns[3],
            grads_columns[4],
            grads_columns[5],
            grads_columns[6],
            grads_columns[7],
        ),
        ("img", "row"),
    )
    return (
        final.astype(jnp.bfloat16).reshape(grid_shape),
        stream_grad.reshape(grid_shape),
    ) + tuple(totals)


def solution(mesh):
    in_specs = (
        P("row", "img", None, None),
        P("row", "img", None, None),
        P(),
        P(),
        P(),
        P(),
        P(),
        P(),
        P(),
        P(),
        P(),
        P(),
        P(),
        P(),
        P(),
        P(),
        P(),
        P(),
    )
    out_specs = (
        P("row", "img", None, None),
        P("row", "img", None, None),
        P(),
        P(),
        P(),
        P(),
        P(),
        P(),
        P(),
        P(),
        P(),
        P(),
        P(),
        P(),
        P(),
        P(),
        P(),
        P(),
    )
    return jax.shard_map(
        on_device, mesh=mesh, in_specs=in_specs, out_specs=out_specs, check_vma=False
    )
```

profile of v0, /device:TPU:0, one launch (start us, length us, event | category | flops | bytes accessed | tf_op | source)
XLA Modules:
  0.0 910.7 jit_solution(12401794550634463029)
XLA Ops:
  46.5 95.8 %all-gather.5.cloned.1.call-done = bf16[32,8,96,256]{3,2,1,0:T(8,128)(2,1)} async-done(((bf16[2,8,96,256]{3,2,1,0:T(8,128)(2,1)}), bf16[32,8,96,256]{3,2,1,0:T(8,128)(2,1)}) %all-gather.5.cloned.1.call-update) | async-done | bytes 12582928 | tf_op jit(solution)/shard_map/all_gather | solution.py:131
  142.3 18.3 %reshape.264 = bf16[32,8,96,2,128]{4,3,2,1,0:T(2,128)(2,1)} reshape(bf16[32,8,96,256]{3,2,1,0:T(8,128)(2,1)} %all-gather.5.cloned.1.call-done) | data formatting | bytes 25165824 | tf_op jit(solution)/shard_map/reshape | solution.py:44
  160.6 17.4 %fusion.115 = (f32[2,8,96,2]{0,3,2,1:T(2,128)}, f32[2,8,96,2,32]{4,0,3,2,1:T(2,128)}) fusion(pred[2,32]{1,0:T(4,128)(4,1)S(1)} %iota_compare_fusion.1, bf16[32,8,96,2,128]{4,3,2,1,0:T(2,128)(2,1)} %reshape.264, bf16[2,8,96,2,128]{4,3,2,1,0:T(2,128)(2,1)} %reshape_reshape.44), kind=kOutput, calls=%fused_computation.192 | convolution fusion | flops 25559072 | bytes 13774912 | tf_op jit(solution)/shard_map/sub | solution.py:136
  178.0 4.6 broadcast_divide_fusion
  182.6 61.5 %all-gather.3.cloned.1.call-done = bf16[32,8,96,256]{3,2,1,0:T(8,128)(2,1)} async-done(((bf16[2,8,96,256]{3,2,1,0:T(8,128)(2,1)}), bf16[32,8,96,256]{3,2,1,0:T(8,128)(2,1)}) %all-gather.3.cloned.1.call-update) | async-done | bytes 12582928 | tf_op jit(solution)/shard_map/all_gather | solution.py:142
  244.1 18.2 %reshape.262 = bf16[32,8,96,2,128]{4,3,2,1,0:T(2,128)(2,1)} reshape(bf16[32,8,96,256]{3,2,1,0:T(8,128)(2,1)} %all-gather.3.cloned.1.call-done) | data formatting | bytes 25165824 | tf_op jit(solution)/shard_map/reshape | solution.py:44
  262.3 13.1 %fusion.43 = bf16[2,8,96,2,128]{4,0,3,2,1:T(2,128)(2,1)S(1)} fusion(bf16[32,8,96,2,128]{4,3,2,1,0:T(2,128)(2,1)} %reshape.262, f32[2,8,96,2,32]{4,0,3,2,1:T(2,128)} %broadcast_divide_fusion), kind=kOutput, calls=%fused_computation.103 | convolution fusion | flops 25657344 | bytes 13762560 | tf_op jit(solution)/shard_map/ibchj,jbche->ibche/dot_general | solution.py:139
  277.6 3.9 multiply_convert_fusion.1
  281.5 4.7 fusion.24
  294.8 19.5 %fusion.28 = (f32[2,8,96,2]{0,3,2,1:T(2,128)}, f32[8,96,2,32,2]{3,4,2,1,0:T(2,128)}) fusion(f32[2,8,96,2,32]{4,0,3,2,1:T(2,128)} %broadcast_divide_fusion, bf16[2,8,96,2,128]{4,3,2,1,0:T(2,128)(2,1)} %reshape_reshape.46, bf16[32,8,96,2,128]{4,3,2,1,0:T(2,128)(2,1)} %reshape.262), kind=kOutput, calls=%fused_computation.55 | convolution fusion | flops 25359360 | bytes 14168064 | tf_op jit(solution)/shard_map/ibche,jbche->ibchj/dot_general | solution.py:153
  314.3 4.1 convert_bitcast_fusion
  318.5 14.7 %copy.92 = bf16[32,8,96,2,128]{4,3,2,1,0:T(2,128)(2,1)} copy(bf16[32,8,96,2,128]{4,0,3,2,1:T(8,128)(2,1)S(1)} %convert_bitcast_fusion) | data formatting | bytes 25165824 | tf_op jit(solution)/shard_map/ibchj,ibche->jbche/transpose | solution.py:180
  333.2 20.5 %reshape.269 = bf16[32,8,96,256]{3,2,1,0:T(8,128)(2,1)} reshape(bf16[32,8,96,2,128]{4,3,2,1,0:T(2,128)(2,1)} %copy.92) | data formatting | bytes 25165824 | tf_op jit(solution)/shard_map/reshape | solution.py:185
  353.7 7.0 fusion.30
  360.8 4.9 fusion.2
  365.7 14.9 %copy.90 = bf16[32,8,96,2,128]{4,3,2,1,0:T(2,128)(2,1)} copy(bf16[32,8,96,2,128]{4,0,3,2,1:T(8,128)(2,1)S(1)} %fusion.2) | data formatting | bytes 25165824 | tf_op jit(solution)/shard_map/mul | solution.py:175
  380.6 20.5 %reshape.268 = bf16[32,8,96,256]{3,2,1,0:T(8,128)(2,1)} reshape(bf16[32,8,96,2,128]{4,3,2,1,0:T(2,128)(2,1)} %copy.90) | data formatting | bytes 25165824 | tf_op jit(solution)/shard_map/reshape | solution.py:185
  401.1 20.8 %pad_maximum_fusion = bf16[32,8,96,512]{3,2,1,0:T(8,128)(2,1)} fusion(bf16[32,8,96,256]{3,2,1,0:T(8,128)(2,1)} %reshape.269, bf16[32,8,96,256]{3,2,1,0:T(8,128)(2,1)} %reshape.268), kind=kLoop, calls=%fused_computation.2 | loop fusion | flops 50331648 | bytes 50331648 | tf_op jit(solution)/shard_map/concatenate | solution.py:185
  424.1 13.8 %fusion.46 = bf16[2,8,96,2,128]{4,0,3,2,1:T(2,128)(2,1)S(1)} fusion(bf16[2,8,96,2,32]{4,0,3,2,1:T(2,128)(2,1)S(1)} %copy-done.43, bf16[32,8,96,2,128]{4,3,2,1,0:T(2,128)(2,1)} %reshape.264), kind=kOutput, calls=%fused_computation.104 | convolution fusion | flops 25952256 | bytes 13565952 | tf_op jit(solution)/shard_map/ibchj,jbche->ibche/dot_general | solution.py:166
  450.3 213.8 %reduce-scatter.2.cloned.1.call-done = bf16[2,8,96,512]{3,2,1,0:T(8,128)(2,1)} async-done(((bf16[32,8,96,512]{3,2,1,0:T(8,128)(2,1)}), bf16[2,8,96,512]{3,2,1,0:T(8,128)(2,1)}) %reduce-scatter.2.cloned.1.call-update) | async-done | bytes 1572880 | tf_op jit(solution)/shard_map/reduce_scatter | solution.py:184
  675.0 4.8 fusion.17
  705.8 4.5 fusion.25
  715.5 40.6 %all-reduce = (f32[256]{0:T(256)}, f32[256]{0:T(256)}, f32[256]{0:T(256)}, f32[256]{0:T(256)}) all-reduce(f32[256]{0:T(256)S(1)} %get-tuple-element.24, f32[256]{0:T(256)S(1)} %get-tuple-element.22, f32[256]{0:T(256)S(1)} %get-tuple-element.20, f32[256]{0:T(256)S(1)} %get-tuple-element.18), channel_id=1, replica_groups=mesh['img'=2,'row'=16] {'img','row'}, use_global_device_ids=true, to_apply=%region_24.25 | all-reduce | flops 1024 | bytes 8192 | tf_op jit(solution)/shard_map/psum | solution.py:353
  759.3 131.7 %all-reduce.4.cloned.1.call-done = (f32[256,256]{1,0:T(8,128)}, f32[256,256]{1,0:T(8,128)}, f32[256,256]{1,0:T(8,128)}, f32[256,256]{1,0:T(8,128)}, f32[256,1024...) async-done(((f32[256,256]{1,0:T(8,128)}, ...) | async-done | bytes 6291472 | tf_op jit(solution)/shard_map/psum | solution.py:353
  (298 shorter events, 121.6 us)
Async XLA Ops:
  7.2 270.3 %copy-start = (bf16[256,1024]{1,0:T(8,128)(2,1)S(1)}, bf16[256,1024]{1,0:T(8,128)(2,1)}, u32[]{:S(2)}) copy-start(bf16[256,1024]{1,0:T(8,128)(2,1)} %param.34) | copy-start | bytes 1572868
  7.2 4.2 copy-start.54
  7.2 135.1 %all-gather.5.cloned.1.call-start = ((), (), s32[]{:S(2)}) async-start(), calls=%async_computation.2 | async-start | bytes 13369344 | tf_op jit(solution)/shard_map/all_gather | solution.py:131
  14.7 7.3 copy-start.24
  14.7 4.0 copy-start.71
  38.6 205.5 %all-gather.3.cloned.1.call-start = ((), (), s32[]{:S(2)}) async-start(), calls=%async_computation.1 | async-start | bytes 13369344 | tf_op jit(solution)/shard_map/all_gather | solution.py:142
  41.1 623.0 %reduce-scatter.2.cloned.1.call-start = ((), (), s32[]{:S(2)}) async-start(), calls=%async_computation.3 | async-start | bytes 26738688 | tf_op jit(solution)/shard_map/reduce_scatter | solution.py:184
  276.9 11.0 %copy-start.9 = (f32[1536,256]{1,0:T(8,128)}, f32[1536,256]{1,0:T(8,128)S(1)}, u32[]{:S(2)}) copy-start(f32[1536,256]{1,0:T(8,128)S(1)} %get-tuple-element.57) | copy-start | bytes 4718596
  294.8 19.5 %copy-start.14 = (f32[2,8,96,2,32]{4,0,3,2,1:T(2,128)S(1)}, f32[2,8,96,2,32]{4,0,3,2,1:T(2,128)}, u32[]{:S(2)}) copy-start(f32[2,8,96,2,32]{4,0,3,2,1:T(2,128)} %broadcast_divide_fusion) | copy-start | bytes 1179652
  294.8 19.5 %copy-start.21 = (bf16[2,8,96,2,128]{4,3,2,1,0:T(2,128)(2,1)S(1)}, bf16[2,8,96,2,128]{4,3,2,1,0:T(2,128)(2,1)}, u32[]{:S(2)}) copy-start(bf16[2,8,96,2,128]{4,3,2,1,0:T(2,128)(2,1)} %reshape_reshape.46) | copy-start | bytes 2359300
  353.7 7.0 copy-start.37
  360.7 5.0 copy-start.42
  422.0 469.1 %all-reduce.4.cloned.1.call-start = ((), (), s32[]{:S(2)}) async-start(), calls=%async_computation.4 | async-start | bytes 12582912 | tf_op jit(solution)/shard_map/psum | solution.py:353
  437.9 6.1 copy-start.91
  667.2 4.3 slice-start
  675.0 4.8 copy-start.3
  675.0 4.8 copy-start.57
  675.0 4.8 copy-start.66
  675.0 4.8 copy-start.86
  686.1 4.2 copy-start.80
  705.7 4.5 copy-start.23
  705.7 4.5 copy-start.53
  891.0 5.2 copy-start.62
  891.0 5.9 copy-start.33
  (76 other events, 139.7 us)
Sparse Core Ops, SparseCore 0:
  38.8 103.4 all-gather.4
  145.1 98.9 all-gather.2
  422.1 241.9 reduce-scatter.1
  705.9 185.1 all-reduce.3
where the time goes:
time: 922 us; the launch traced here: 911 us
  waiting for transfers between devices  503 us (55%)
  local copies, waits for them, and re-layouts  155 us (17%)
  matrix products  148 us (16%)
  other arithmetic  49 us (5%)
  blocking collectives  40.6 us (4%)
  between operations  15.2 us (2%)
    reduce_scatter x1, waiting for transfers between devices, columns_backward(): lax.psum_scatter(jnp.concatenate([key_grad.reshape(target), value_grad.re...  214 us
    psum x1, waiting for transfers between devices, on_device(): lax.psum((grads_rows[0], grads_rows[1], grads_rows[2], grads_rows[3], gra...  132 us
    all_gather x1, waiting for transfers between devices, columns_forward(): lax.all_gather(key_in, 'row', axis=0, tiled=True)  95.8 us
    all_gather x1, waiting for transfers between devices, columns_forward(): lax.all_gather(value_in, 'row', axis=0, tiled=True)  61.5 us
    psum x1, blocking collectives, on_device(): lax.psum((grads_rows[0], grads_rows[1], grads_rows[2], grads_rows[3], gra...  40.6 us
    reshape x2, local copies, waits for them, and re-layouts, split_heads(): tensor.reshape(tensor.shape[:-1] + (HEADS, tensor.shape[-1] // HEADS))  36.4 us
    unnamed x204, local copies, waits for them, and re-layouts  26 us
    dot_general x12, matrix products, times_back(): lax.dot_general(grads, weight, (((1,), (1,)), ((), ())), preferred_elemen...  21.6 us
  transfers between devices with their start and end apart: 4, of which 4 were waited for; matrix products, arithmetic and copies ran while one was open for 9% of the time, Pallas kernels for 0%

commit v1 on v0

v1 whole, which is shorter than its diff:
```python
import functools
import math

import jax
import jax.numpy as jnp
from jax import lax
from jax.experimental import pallas as pl
from jax.experimental.pallas import tpu as pltpu
from jax.sharding import PartitionSpec as P

HEADS = 2
EPS = 1e-05
GROUP = 8
TAIL = 16
HIDDEN_TILE = 256
VMEM_LIMIT = 56 * 1024 * 1024
ALL = ("img", "row")
F32 = jnp.float32
BF16 = jnp.bfloat16


def mm(left, right):
    return lax.dot_general(left, right, (((1,), (0,)), ((), ())), preferred_element_type=F32)


def mm_right_t(left, right):
    return lax.dot_general(left, right, (((1,), (1,)), ((), ())), preferred_element_type=F32)


def mm_left_t(left, right):
    return lax.dot_general(left, right, (((0,), (0,)), ((), ())), preferred_element_type=F32)


def normalize(stream):
    centred = stream - jnp.mean(stream, axis=-1, keepdims=True)
    inverse = lax.rsqrt(jnp.mean(centred * centred, axis=-1, keepdims=True) + EPS)
    return centred * inverse, inverse


def normalize_back(upstream, normal, inverse, gain):
    scaled = upstream * gain
    centred = (
        scaled
        - jnp.mean(scaled, axis=-1, keepdims=True)
        - normal * jnp.mean(scaled * normal, axis=-1, keepdims=True)
    )
    return inverse * centred, jnp.sum(upstream * normal, axis=0, keepdims=True)


ROOT = math.sqrt(2.0 / math.pi)
CUBE = 0.044715


def gelu(value):
    bent = jnp.tanh(ROOT * (value + CUBE * (value * value * value)))
    return 0.5 * value * (1.0 + bent)


def gelu_both(value):
    square = value * value
    bent = jnp.tanh(ROOT * (value + CUBE * (square * value)))
    half = 0.5 * (1.0 + bent)
    slope = half + (0.5 * ROOT) * value * (1.0 - bent * bent) * (1.0 + (3.0 * CUBE) * square)
    return value * half, slope


def softmax(scores):
    risen = jnp.exp(scores - jnp.max(scores, axis=-1, keepdims=True))
    return risen / jnp.sum(risen, axis=-1, keepdims=True)


def causal_bias(size, period):
    row = lax.broadcasted_iota(jnp.int32, (size, size), 0)
    col = lax.broadcasted_iota(jnp.int32, (size, size), 1)
    visible = (row >= col) & (((row ^ col) & (period - 1)) == 0)
    return jnp.where(visible, 0.0, -1e30).astype(F32)


def attend_back(up, query, key, value, probs, scaling):
    prob_grad = mm_right_t(up, value)
    inner = jnp.sum(probs * prob_grad, axis=-1, keepdims=True)
    score_grad = (probs * (prob_grad - inner)).astype(BF16)
    query_grad = (mm(score_grad, key) * scaling).astype(BF16)
    key_grad = (mm_left_t(score_grad, query) * scaling).astype(BF16)
    value_grad = mm_left_t(probs.astype(BF16), up).astype(BF16)
    return query_grad, key_grad, value_grad


def feed_back(normed, up_low, expand_ref, shrink_ref, acc, first, forward):
    width = normed.shape[-1]
    hidden_width = expand_ref.shape[1]
    tile = min(HIDDEN_TILE, hidden_width)
    result = None
    normed_grad = None
    for j in range(hidden_width // tile):
        cut = slice(j * tile, (j + 1) * tile)
        expand = expand_ref[:, cut]
        shrink = shrink_ref[cut, :]
        hidden, slope = gelu_both(mm(normed, expand))
        hidden = hidden.astype(BF16)
        if forward:
            part = mm(hidden, shrink)
            result = part if result is None else result + part
        expanded_grad = (slope * mm_right_t(up_low, shrink)).astype(BF16)
        at = first + j * width
        acc[at : at + width, :] += mm_left_t(normed, expanded_grad)
        at = first + hidden_width // tile * width + j * width
        acc[at : at + width, :] += mm_left_t(up_low, hidden)
        part = mm_right_t(expanded_grad, expand)
        normed_grad = part if normed_grad is None else normed_grad + part
    return result, normed_grad


def project_back(normed_low, grads, weight_refs, acc):
    width = normed_low.shape[-1]
    total = None
    for i, (grad, weight_ref) in enumerate(zip(grads, weight_refs)):
        acc[i * width : (i + 1) * width, :] += mm_left_t(normed_low, grad)
        part = mm_right_t(grad, weight_ref[...])
        total = part if total is None else total + part
    return total


def store_tail(ref, at, gains):
    high = gains.astype(BF16)
    ref[at : at + 8, :] = high
    ref[at + 8 : at + 16, :] = (gains - high.astype(F32)).astype(BF16)


def emit_grads(core, acc, gains, keep_ref, send_ref):
    half = acc.shape[0] // 2
    for which, (mine, other) in enumerate(((keep_ref, send_ref), (send_ref, keep_ref))):

        @pl.when(core == which)
        def _():
            mine[0:half, :] = acc[0:half, :].astype(BF16)
            other[0:half, :] = acc[half:, :].astype(BF16)

    store_tail(keep_ref, half, gains[...])
    store_tail(send_ref, half, gains[...])


def rows_forward_kernel(
    x_ref, ga_ref, wq_ref, wk_ref, wv_ref, wo_ref, gb_ref, w1_ref, w2_ref,
    send_ref, q_ref, k_ref, v_ref, att_ref, mid_ref, p_ref,
):
    rows, images, cols, width = x_ref.shape
    tokens = rows * images * cols
    features = width // HEADS
    scaling = 1.0 / math.sqrt(features)
    stream = x_ref[...].astype(F32).reshape(tokens, width)
    normed = (normalize(stream)[0] * ga_ref[...]).astype(BF16)
    query = mm(normed, wq_ref[...]).astype(BF16)
    key = mm(normed, wk_ref[...]).astype(BF16)
    value = mm(normed, wv_ref[...]).astype(BF16)
    q_ref[...] = query.reshape(q_ref.shape)
    k_ref[...] = key.reshape(q_ref.shape)
    v_ref[...] = value.reshape(q_ref.shape)
    bias = causal_bias(cols, 1)
    groups = []
    for g in range(rows * images):
        span = slice(g * cols, (g + 1) * cols)
        heads = []
        for m in range(HEADS):
            part = slice(m * features, (m + 1) * features)
            probs = softmax(mm_right_t(query[span, part], key[span, part]) * scaling + bias)
            p_ref[g // images, g % images, m] = probs
            heads.append(mm(probs.astype(BF16), value[span, part]))
        groups.append(jnp.concatenate(heads, axis=1))
    attended = jnp.concatenate(groups, axis=0).astype(BF16)
    att_ref[...] = attended.reshape(att_ref.shape)
    middle = stream + mm(attended, wo_ref[...])
    mid_ref[...] = middle.reshape(mid_ref.shape)
    normed_b = (normalize(middle)[0] * gb_ref[...]).astype(BF16)
    hidden_width = w1_ref.shape[1]
    tile = min(HIDDEN_TILE, hidden_width)
    result = middle
    for j in range(hidden_width // tile):
        cut = slice(j * tile, (j + 1) * tile)
        hidden = gelu(mm(normed_b, w1_ref[:, cut])).astype(BF16)
        result = result + mm(hidden, w2_ref[cut, :])
    result = result.reshape(rows, images * cols // GROUP, GROUP, width)
    result = jnp.concatenate([result[r] for r in range(rows)], axis=1)
    send_ref[...] = result.astype(BF16).reshape(send_ref.shape)


def rows_backward_kernel(
    core_ref, x_ref, q_ref, k_ref, v_ref, att_ref, mid_ref, p_ref, up_ref,
    ga_ref, wq_ref, wk_ref, wv_ref, wo_ref, gb_ref, w1_ref, w2_ref,
    grad_ref, keep_ref, send_ref, acc, gains,
):
    rows, images, cols, width = x_ref.shape
    tokens = rows * images * cols
    features = width // HEADS
    scaling = 1.0 / math.sqrt(features)
    step = pl.program_id(0)

    @pl.when(step == 0)
    def _():
        acc[...] = jnp.zeros_like(acc)
        gains[...] = jnp.zeros_like(gains)

    up = up_ref[...].astype(F32).reshape(images * cols // GROUP, rows * GROUP, width)
    up = jnp.concatenate(
        [up[:, r * GROUP : (r + 1) * GROUP].reshape(images * cols, width) for r in range(rows)], axis=0
    )
    up_low = up.astype(BF16)
    middle = mid_ref[...].reshape(tokens, width)
    normal_b, inverse_b = normalize(middle)
    normed_b = (normal_b * gb_ref[...]).astype(BF16)
    _, normed_grad = feed_back(normed_b, up_low, w1_ref, w2_ref, acc, 4 * width, False)
    middle_norm, scale_grad = normalize_back(normed_grad, normal_b, inverse_b, gb_ref[...])
    gains[1:2, :] += scale_grad
    middle_grad = up + middle_norm
    middle_low = middle_grad.astype(BF16)
    acc[3 * width : 4 * width, :] += mm_left_t(att_ref[...].reshape(tokens, width), middle_low)
    up_att = mm_right_t(middle_low, wo_ref[...]).astype(BF16)
    query = q_ref[...].reshape(tokens, width)
    key = k_ref[...].reshape(tokens, width)
    value = v_ref[...].reshape(tokens, width)
    parts = ([], [], [])
    for g in range(rows * images):
        span = slice(g * cols, (g + 1) * cols)
        heads = []
        for m in range(HEADS):
            part = slice(m * features, (m + 1) * features)
            heads.append(
                attend_back(
                    up_att[span, part], query[span, part], key[span, part], value[span, part],
                    p_ref[g // images, g % images, m], scaling,
                )
            )
        for i in range(3):
            parts[i].append(jnp.concatenate([head[i] for head in heads], axis=1))
    grads = tuple(jnp.concatenate(part, axis=0) for part in parts)
    normal_a, inverse_a = normalize(x_ref[...].astype(F32).reshape(tokens, width))
    normed_a = (normal_a * ga_ref[...]).astype(BF16)
    normed_grad = project_back(normed_a, grads, (wq_ref, wk_ref, wv_ref), acc)
    stream_norm, gain_grad = normalize_back(normed_grad, normal_a, inverse_a, ga_ref[...])
    gains[0:1, :] += gain_grad
    grad_ref[...] = (middle_grad + stream_norm).reshape(grad_ref.shape)

    @pl.when(step == pl.num_programs(0) - 1)
    def _():
        emit_grads(core_ref[0], acc, gains, keep_ref, send_ref)


def columns_kernel(
    core_ref, x_ref, up_ref, ga_ref, wq_ref, wk_ref, wv_ref, wo_ref, gb_ref, w1_ref, w2_ref,
    out_ref, grad_ref, keep_ref, send_ref, acc, gains, bias,
):
    width = x_ref.shape[-1]
    tokens = x_ref.shape[0] * x_ref.shape[2]
    features = width // HEADS
    scaling = 1.0 / math.sqrt(features)
    step = pl.program_id(0)

    @pl.when(step == 0)
    def _():
        acc[...] = jnp.zeros_like(acc)
        gains[...] = jnp.zeros_like(gains)
        bias[...] = causal_bias(tokens, GROUP)

    stream = x_ref[...].astype(F32).reshape(tokens, width)
    normal_a, inverse_a = normalize(stream)
    normed_a = (normal_a * ga_ref[...]).astype(BF16)
    query = mm(normed_a, wq_ref[...]).astype(BF16)
    key = mm(normed_a, wk_ref[...]).astype(BF16)
    value = mm(normed_a, wv_ref[...]).astype(BF16)
    probs, heads = [], []
    for m in range(HEADS):
        part = slice(m * features, (m + 1) * features)
        probs.append(softmax(mm_right_t(query[:, part], key[:, part]) * scaling + bias[...]))
        heads.append(mm(probs[m].astype(BF16), value[:, part]))
    attended = jnp.concatenate(heads, axis=1).astype(BF16)
    middle = stream + mm(attended, wo_ref[...])
    normal_b, inverse_b = normalize(middle)
    normed_b = (normal_b * gb_ref[...]).astype(BF16)
    up = up_ref[...].astype(F32).reshape(tokens, width)
    up_low = up.astype(BF16)
    result, normed_grad = feed_back(normed_b, up_low, w1_ref, w2_ref, acc, 4 * width, True)
    out_ref[...] = (middle + result).reshape(out_ref.shape).astype(BF16)
    middle_norm, scale_grad = normalize_back(normed_grad, normal_b, inverse_b, gb_ref[...])
    gains[1:2, :] += scale_grad
    middle_grad = up + middle_norm
    middle_low = middle_grad.astype(BF16)
    acc[3 * width : 4 * width, :] += mm_left_t(attended, middle_low)
    up_att = mm_right_t(middle_low, wo_ref[...]).astype(BF16)
    backs = []
    for m in range(HEADS):
        part = slice(m * features, (m + 1) * features)
        backs.append(
            attend_back(up_att[:, part], query[:, part], key[:, part], value[:, part], probs[m], scaling)
        )
    grads = tuple(jnp.concatenate([back[i] for back in backs], axis=1) for i in range(3))
    normed_grad = project_back(normed_a, grads, (wq_ref, wk_ref, wv_ref), acc)
    stream_norm, gain_grad = normalize_back(normed_grad, normal_a, inverse_a, ga_ref[...])
    gains[0:1, :] += gain_grad
    grad_ref[...] = (middle_grad + stream_norm).reshape(grad_ref.shape).astype(BF16)

    @pl.when(step == pl.num_programs(0) - 1)
    def _():
        emit_grads(core_ref[0], acc, gains, keep_ref, send_ref)


def whole(array):
    zeros = (0,) * array.ndim
    return pl.BlockSpec(array.shape, lambda i: zeros)


def whole_out(shape):
    zeros = (0,) * len(shape)
    return pl.BlockSpec(shape, lambda i: zeros)


SCALAR = pl.BlockSpec(memory_space=pltpu.SMEM)


def params():
    return pltpu.CompilerParams(vmem_limit_bytes=VMEM_LIMIT)


def shape_of(shape, dtype):
    return jax.ShapeDtypeStruct(shape, dtype)


def grad_rows(width, hidden_width):
    tile = min(HIDDEN_TILE, hidden_width)
    return 4 * width + 2 * (hidden_width // tile) * width


def cost(tokens, width, hidden_width, passes, moved):
    flops = 2 * passes * tokens * width * (4 * width + 2 * hidden_width)
    return pl.CostEstimate(flops=flops, bytes_accessed=moved, transcendentals=tokens * hidden_width)


def rows_forward(inputs, weights, images_step):
    rows, images, cols, width = inputs.shape
    groups = cols // GROUP
    block = (rows, images_step, cols, width)
    spec = pl.BlockSpec(block, lambda i: (0, i, 0, 0))
    p_spec = pl.BlockSpec((rows, images_step, HEADS, cols, cols), lambda i: (0, i, 0, 0, 0))
    send_block = (images_step, groups, rows * GROUP, width)
    low = shape_of(inputs.shape, BF16)
    return pl.pallas_call(
        rows_forward_kernel,
        grid=(images // images_step,),
        in_specs=[spec] + [whole(w) for w in weights],
        out_specs=[pl.BlockSpec(send_block, lambda i: (i, 0, 0, 0)), spec, spec, spec, spec, spec, p_spec],
        out_shape=[
            shape_of((images, groups, rows * GROUP, width), BF16),
            low, low, low, low,
            shape_of(inputs.shape, F32),
            shape_of((rows, images, HEADS, cols, cols), F32),
        ],
        compiler_params=params(),
        cost_estimate=cost(rows * images * cols, width, weights[6].shape[1], 1, 12 << 20),
        name="rows_forward",
    )(inputs, *weights)


def rows_backward(core, inputs, stored, up, weights, images_step):
    rows, images, cols, width = inputs.shape
    groups = cols // GROUP
    hidden_width = weights[6].shape[1]
    total = grad_rows(width, hidden_width)
    spec = pl.BlockSpec((rows, images_step, cols, width), lambda i: (0, i, 0, 0))
    p_spec = pl.BlockSpec((rows, images_step, HEADS, cols, cols), lambda i: (0, i, 0, 0, 0))
    up_spec = pl.BlockSpec((images_step, groups, rows * GROUP, width), lambda i: (i, 0, 0, 0))
    part = (total // 2 + TAIL, width)
    return pl.pallas_call(
        rows_backward_kernel,
        grid=(images // images_step,),
        in_specs=[SCALAR, spec, spec, spec, spec, spec, spec, p_spec, up_spec] + [whole(w) for w in weights],
        out_specs=[spec, whole_out(part), whole_out(part)],
        out_shape=[shape_of(inputs.shape, F32), shape_of(part, BF16), shape_of(part, BF16)],
        scratch_shapes=[pltpu.VMEM((total, width), F32), pltpu.VMEM((8, width), F32)],
        compiler_params=params(),
        cost_estimate=cost(rows * images * cols, width, hidden_width, 2, 16 << 20),
        name="rows_backward",
    )(core, inputs, *stored, up, *weights)


def columns_both(core, stream, up, weights):
    sources, groups, height, width = stream.shape
    hidden_width = weights[6].shape[1]
    total = grad_rows(width, hidden_width)
    tokens = sources * height
    spec = pl.BlockSpec((sources, 1, height, width), lambda i: (0, i, 0, 0))
    part = (total // 2 + TAIL, width)
    return pl.pallas_call(
        columns_kernel,
        grid=(groups,),
        in_specs=[SCALAR, spec, spec] + [whole(w) for w in weights],
        out_specs=[spec, spec, whole_out(part), whole_out(part)],
        out_shape=[shape_of(stream.shape, BF16), shape_of(stream.shape, BF16), shape_of(part, BF16), shape_of(part, BF16)],
        scratch_shapes=[
            pltpu.VMEM((total, width), F32),
            pltpu.VMEM((8, width), F32),
            pltpu.VMEM((tokens, tokens), F32),
        ],
        compiler_params=params(),
        cost_estimate=cost(tokens * groups, width, hidden_width, 3, 6 << 20),
        name="columns_both",
    )(core, stream, up, *weights)


def sum_split_kernel(count, ways, at_ref, *refs):
    ins, outs, parts = refs[:count], refs[count : count + ways], refs[-1]
    size = ins[0].shape[0] - TAIL
    total = ins[0][0:size, :].astype(F32)
    gains = ins[0][size : size + 8, :].astype(F32) + ins[0][size + 8 :, :].astype(F32)
    for ref in ins[1:]:
        total = total + ref[0:size, :].astype(F32)
        gains = gains + (ref[size : size + 8, :].astype(F32) + ref[size + 8 :, :].astype(F32))
    total = total.astype(BF16)
    if ways == 1:
        outs[0][0:size, :] = total
        store_tail(outs[0], size, gains)
        return
    step = size // ways
    for j in range(ways):
        parts[j] = total[j * step : (j + 1) * step, :]
    for j in range(ways):
        outs[j][0:step, :] = parts[at_ref[0] ^ j]
        store_tail(outs[j], step, gains)


def sum_split(at, arrays, ways):
    size, width = arrays[0].shape
    step = (size - TAIL) // ways
    shape = (step + TAIL, width)
    return pl.pallas_call(
        functools.partial(sum_split_kernel, len(arrays), ways),
        in_specs=[SCALAR] + [pl.BlockSpec(memory_space=pltpu.VMEM)] * len(arrays),
        out_specs=[pl.BlockSpec(memory_space=pltpu.VMEM)] * ways,
        out_shape=[shape_of(shape, BF16)] * ways,
        scratch_shapes=[pltpu.VMEM((ways, step, width), BF16)],
        compiler_params=params(),
        name="sum_split",
    )(at, *arrays)


def join_kernel(ways, at_ref, *refs):
    ins, out = refs[:ways], refs[-1]
    size = out.shape[1]
    for j in range(ways):
        out[at_ref[0] ^ j] = ins[j][0:size, :]


def join(at, arrays, size):
    ways, width = len(arrays), arrays[0].shape[1]
    joined = pl.pallas_call(
        functools.partial(join_kernel, ways),
        in_specs=[SCALAR] + [pl.BlockSpec(memory_space=pltpu.VMEM)] * ways,
        out_specs=pl.BlockSpec(memory_space=pltpu.VMEM),
        out_shape=shape_of((ways, size, width), BF16),
        compiler_params=params(),
        name="join",
    )(at, *arrays)
    return joined.reshape(ways * size, width)


def finish_kernel(at_ref, own_ref, other_ref, tail_ref, *refs):
    outs, halves = refs[:-1], refs[-1]
    gain, query, keys, values, mixer, scale, expand, shrink = outs
    width = own_ref.shape[1]
    halves[at_ref[0]] = own_ref[...]
    halves[at_ref[0] ^ 1] = other_ref[...]
    per_half = halves.shape[1] // width

    def block(i):
        at = (i % per_half) * width
        return halves[i // per_half, at : at + width, :].astype(F32)

    for i, ref in enumerate((query, keys, values, mixer)):
        ref[...] = block(i)
    tiles = expand.shape[1] // width
    for j in range(tiles):
        expand[:, j * width : (j + 1) * width] = block(4 + j)
        shrink[j * width : (j + 1) * width, :] = block(4 + tiles + j).T
    start = tail_ref.shape[0] - TAIL
    gains = tail_ref[start : start + 8, :].astype(F32) + tail_ref[start + 8 :, :].astype(F32)
    gain[...] = gains[0:1, :]
    scale[...] = gains[1:2, :]


def finish(at, own, other, tail, width, hidden_width):
    half = own.shape[0]
    square = shape_of((width, width), F32)
    row = shape_of((1, width), F32)
    outs = pl.pallas_call(
        finish_kernel,
        in_specs=[SCALAR] + [pl.BlockSpec(memory_space=pltpu.VMEM)] * 3,
        out_specs=[pl.BlockSpec(memory_space=pltpu.VMEM)] * 8,
        out_shape=[
            row, square, square, square, square, row,
            shape_of((width, hidden_width), F32), shape_of((hidden_width, width), F32),
        ],
        scratch_shapes=[pltpu.VMEM((2, half, width), BF16)],
        compiler_params=params(),
        name="finish",
    )(at, own, other, tail)
    return [outs[0].reshape(width)] + list(outs[1:5]) + [outs[5].reshape(width)] + list(outs[6:])


class Exchange:
    def __init__(self, bits, flat, devices):
        self.bits = bits
        self.ways = 1 << len(bits)
        place = sum(((flat >> bit) & 1) << i for i, bit in enumerate(bits))
        self.place = jnp.reshape(place, (1,)).astype(jnp.int32)
        self.devices = devices

    def swap(self, array, member):
        mask = sum(1 << bit for i, bit in enumerate(self.bits) if (member >> i) & 1)
        return lax.ppermute(array, ALL, [(i, i ^ mask) for i in range(self.devices)])


def sum_over_devices(exchanges, keep, send, width, hidden_width):
    arrays = [keep, exchanges[0].swap(send, 1)]
    spread = [exchanges[0]]
    for exchange in exchanges[1:]:
        size = arrays[0].shape[0] - TAIL
        if size % (exchange.ways * TAIL) == 0:
            parts = sum_split(exchange.place, arrays, exchange.ways)
            arrays = [parts[0]] + [exchange.swap(parts[j], j) for j in range(1, exchange.ways)]
            spread.append(exchange)
        else:
            (part,) = sum_split(exchange.place, arrays, 1)
            arrays = [part] + [exchange.swap(part, j) for j in range(1, exchange.ways)]
    (tail,) = sum_split(exchanges[0].place, arrays, 1)
    part = tail
    size = tail.shape[0] - TAIL
    for exchange in reversed(spread[1:]):
        part = part if part.shape[0] == size else part[:size]
        pieces = [part] + [exchange.swap(part, j) for j in range(1, exchange.ways)]
        part = join(exchange.place, pieces, size)
        size = part.shape[0]
    other = spread[0].swap(part, 1)
    return finish(spread[0].place, part, other, tail, width, hidden_width)


def on_device(images_step, inputs, cotangent, *weights):
    rows, images, cols, width = inputs.shape
    groups = cols // GROUP
    height = lax.axis_size("row")
    devices = height * lax.axis_size("img")
    flat = lax.axis_index("img") * height + lax.axis_index("row")
    bits = list(range(1, devices.bit_length() - 1))
    exchanges = [Exchange([0], flat, devices)]
    while bits:
        pair = [bits.pop()]
        if bits:
            pair.append(bits.pop(0))
        exchanges.append(Exchange(pair, flat, devices))
    core = exchanges[0].place
    weights = [w.reshape(1, -1) if w.ndim == 1 else w for w in weights]
    rows_weights, column_weights = weights[:8], weights[8:]
    hidden_width = rows_weights[6].shape[1]
    owned = images * groups // height

    def to_columns(array):
        array = array.reshape(height, owned, rows * GROUP, width)
        return lax.all_to_all(array, "row", 0, 0, tiled=True)

    def to_rows(array):
        array = lax.all_to_all(array, "row", 0, 0, tiled=True)
        return array.reshape(images, groups, rows * GROUP, width)

    def gather_rows(array):
        array = array.reshape(rows, images, groups, GROUP, width)
        return array.transpose(1, 2, 0, 3, 4)

    up = to_columns(gather_rows(cotangent))
    sent, *stored = rows_forward(inputs, rows_weights, images_step)
    stream = to_columns(sent)
    final, between_grad, keep, send = columns_both(core, stream, up, column_weights)
    column_grads = sum_over_devices(exchanges, keep, send, width, hidden_width)
    final = to_rows(final).reshape(images, groups, rows, GROUP, width)
    final = final.transpose(2, 0, 1, 3, 4).reshape(inputs.shape)
    stream_grad, keep, send = rows_backward(
        core, inputs, stored, to_rows(between_grad), rows_weights, images_step
    )
    rows_grads = sum_over_devices(exchanges, keep, send, width, hidden_width)
    return (final, stream_grad) + tuple(rows_grads) + tuple(column_grads)


def solution(mesh):
    moved = P("row", "img", None, None)
    return jax.shard_map(
        functools.partial(on_device, 2),
        mesh=mesh,
        in_specs=(moved, moved) + (P(),) * 16,
        out_specs=(moved, moved) + (P(),) * 16,
        check_vma=False,
    )
```

time: 922 us -> 257 us (0.28); the launches traced: 911 us -> 256 us
  waiting for transfers between devices: 503 us -> 82.4 us
  matrix products: 148 us -> 0 us
  local copies, waits for them, and re-layouts: 155 us -> 15.5 us
  Pallas kernels: 0 us -> 100 us
  starting transfers between devices: 0.34 us -> 57 us
  other arithmetic: 49 us -> 0 us
  blocking collectives: 40.6 us -> 0 us
  between operations: 15.2 us -> 0.92 us
    reduce_scatter x1 -> x0, waiting for transfers between devices: 214 us -> none  [columns_backward(): lax.psum_scatter(jnp.concatenate([key_grad.reshape(target), value_grad.re...]
    all_gather x2 -> x0, waiting for transfers between devices: 157 us -> none  [the longest x1 95.8 us: columns_forward(): lax.all_gather(key_in, 'row', axis=0, tiled=True)]
    psum x1 -> x0, waiting for transfers between devices: 132 us -> none  [on_device(): lax.psum((grads_rows[0], grads_rows[1], grads_rows[2], grads_rows[3], gra...]
    dot_general x47 -> x0, matrix products: 131 us -> none  [the longest x12 21.6 us: times_back(): lax.dot_general(grads, weight, (((1,), (1,)), ((), ())), preferred_elemen...]
    pallas_call x0 -> x15, Pallas kernels: none -> 100 us  [the longest x1 30.4 us: columns_both(): pl.pallas_call(columns_kernel, grid=(groups,), in_specs=[SCALAR, spec, sp...]
    reshape x4 -> x1, local copies, waits for them, and re-layouts: 77.4 us -> 0.94 us  [gather_rows(): array = array.reshape(rows, images, groups, GROUP, width)]
    all_to_all x0 -> x4, waiting for transfers between devices: none -> 54.7 us  [the longest x2 36.5 us: to_columns(): return lax.all_to_all(array, 'row', 0, 0, tiled=True)]
    psum x1 -> x0, blocking collectives: 40.6 us -> none  [on_device(): lax.psum((grads_rows[0], grads_rows[1], grads_rows[2], grads_rows[3], gra...]
  transfers between devices with their start and end apart: 4 -> 32, of which waited for: 4 -> 12; matrix products, arithmetic and copies ran while one was open for 9% -> 1% of each run, Pallas kernels for 0% -> 19%
where the time goes in v1:
time: 257 us; the launch traced here: 256 us
  Pallas kernels  100 us (39%)
  waiting for transfers between devices  82.4 us (32%)
  starting transfers between devices  57 us (22%)
  local copies, waits for them, and re-layouts  15.5 us (6%)
    all_to_all x2, waiting for transfers between devices, to_columns(): return lax.all_to_all(array, 'row', 0, 0, tiled=True)  36.5 us
    ppermute x28, starting transfers between devices, swap(): lax.ppermute(array, ALL, [(i, i ^ mask) for i in range(self.devices)])  32.8 us
    pallas_call x1, Pallas kernels, columns_both(): pl.pallas_call(columns_kernel, grid=(groups,), in_specs=[SCALAR, spec, sp...  30.4 us
    ppermute x28, waiting for transfers between devices, swap(): lax.ppermute(array, ALL, [(i, i ^ mask) for i in range(self.devices)])  27.7 us
    pallas_call x1, Pallas kernels, rows_backward(): pl.pallas_call(rows_backward_kernel, grid=(images // images_step,), in_sp...  26 us
    all_to_all x2, waiting for transfers between devices, to_rows(): array = lax.all_to_all(array, 'row', 0, 0, tiled=True)  18.2 us
    pallas_call x1, Pallas kernels, rows_forward(): pl.pallas_call(rows_forward_kernel, grid=(images // images_step,), in_spe...  17.1 us
    all_to_all x2, starting transfers between devices, to_columns(): return lax.all_to_all(array, 'row', 0, 0, tiled=True)  13 us
  transfers between devices with their start and end apart: 32, of which 12 were waited for; matrix products, arithmetic and copies ran while one was open for 1% of the time, Pallas kernels for 19%

profile of v1, /device:TPU:0, one launch (start us, length us, event | category | flops | bytes accessed | tf_op | source)
XLA Modules:
  0.0 256.0 jit_solution(13508352393882788888)
XLA Ops:
  0.7 17.1 %rows_forward.1 = (bf16[8,12,16,256]{3,2,1,0:T(8,128)(2,1)}, bf16[2,8,96,256]{3,2,1,0:T(8,128)(2,1)}, bf16[2,8,96,256]{3,2,1,0:T(8,128)(2,1)}, bf16[2,8,96,256]{...) custom-call(bf16[2,8,96,256]{3,2,1,0:T(8,128)(2,1)} %x_ref.3, ...), custom_call_target="tpu_custom_call" | custom-call | flops 2415919104 | bytes 12582912 | tf_op jit(solution)/shard_map/rows_forward/pallas_call | solution.py:345
  17.7 7.5 %all-to-all-start = ((bf16[16,6,16,256]{3,2,1,0:T(8,128)(2,1)}), bf16[16,6,16,256]{3,2,1,0:T(8,128)(2,1)S(1)}, u32[]{:S(2)}, u32[]{:S(2)}) async-start(bf16[16,6,16,256]{3,2,1,0:T(8,128)(2,1)} %bitcast.35), calls=%async_computation | async-start | bytes 1572864 | tf_op jit(solution)/shard_map/all_to_all | solution.py:565
  26.2 17.8 %all-to-all-done.x_ref = bf16[16,6,16,256]{3,2,1,0:T(8,128)(2,1)S(1)} async-done(((bf16[16,6,16,256]{3,2,1,0:T(8,128)(2,1)}), bf16[16,6,16,256]{3,2,1,0:T(8,128)(2,1)S(1)}, u32[]{:S(2)}, u32[]{:S(2)}) %all-to-all-start) | async-done | bytes 786464 | tf_op jit(solution)/shard_map/all_to_all | solution.py:565
  44.0 5.5 %all-to-all-start.1 = ((bf16[16,6,16,256]{3,2,1,0:T(8,128)(2,1)}), bf16[16,6,16,256]{3,2,1,0:T(8,128)(2,1)S(1)}, u32[]{:S(2)}, u32[]{:S(2)}) async-start(bf16[16,6,16,256]{3,2,1,0:T(8,128)(2,1)} %bitcast.6), calls=%async_computation.1 | async-start | bytes 1572864 | tf_op jit(solution)/shard_map/all_to_all | solution.py:565
  49.5 18.7 %all-to-all-done.1.up_ref = bf16[16,6,16,256]{3,2,1,0:T(8,128)(2,1)S(1)} async-done(((bf16[16,6,16,256]{3,2,1,0:T(8,128)(2,1)}), bf16[16,6,16,256]{3,2,1,0:T(8,128)(2,1)S(1)}, u32[]{:S(2)}, u32[]{:S(2)}) %all-to-all-start.1) | async-done | bytes 786464 | tf_op jit(solution)/shard_map/all_to_all | solution.py:565
  69.1 30.4 %columns_both.1 = (bf16[16,6,16,256]{3,2,1,0:T(8,128)(2,1)}, bf16[16,6,16,256]{3,2,1,0:T(8,128)(2,1)}, bf16[1552,256]{1,0:T(8,128)(2,1)}, bf16[1552,256]{1,0:T(8,128)(2,1)}) custom-call(s32[1]{0:T(128)} %bitcast.core_ref.at_ref, bf16[16,6,16,256]{3,2,1,0:T(8,128)(2,1)} %copy-done.3, bf16[16,6,16,256]{3,2,1,0:T(8,128)(2,1)} %copy-done.5, f32[1,256]{1,0:T(1,128)} %bitcast.44, ...), custom_call_target="tpu_custom_call" | custom-call | flops 7247757312 | bytes 6291456 | tf_op jit(solution)/shard_map/columns_both/pallas_call | solution.py:391
  99.5 5.6 %all-to-all-start.3 = ((bf16[16,6,16,256]{3,2,1,0:T(8,128)(2,1)}), bf16[16,6,16,256]{3,2,1,0:T(8,128)(2,1)S(1)}, u32[]{:S(2)}, u32[]{:S(2)}) async-start(bf16[16,6,16,256]{3,2,1,0:T(8,128)(2,1)} %get-tuple-element.72), calls=%async_computation.3 | async-start | bytes 1572864 | tf_op jit(solution)/shard_map/all_to_all | solution.py:568
  105.6 18.2 %all-to-all-done.3 = bf16[16,6,16,256]{3,2,1,0:T(8,128)(2,1)S(1)} async-done(((bf16[16,6,16,256]{3,2,1,0:T(8,128)(2,1)}), bf16[16,6,16,256]{3,2,1,0:T(8,128)(2,1)S(1)}, u32[]{:S(2)}, u32[]{:S(2)}) %all-to-all-start.3) | async-done | bytes 786464 | tf_op jit(solution)/shard_map/all_to_all | solution.py:568
  124.7 26.0 %rows_backward.1 = (f32[2,8,96,256]{3,2,1,0:T(8,128)}, bf16[1552,256]{1,0:T(8,128)(2,1)}, bf16[1552,256]{1,0:T(8,128)(2,1)}) custom-call(s32[1]{0:T(128)} %bitcast.core_ref.at_ref, bf16[2,8,96,256]{3,2,1,0:T(8,128)(2,1)} %x_ref.3, bf16[2,8,96,256]{3,2,1,0:T(8,128)(2,1)} %get-tuple-element.66.q_ref, bf16[2,8,96,256]{3,2,1,0:T(8,128)(2,1)} %get-tuple-element.67.k_ref, ...), custom_call_target="tpu_custom_call" | custom-call | flops 4831838208 | bytes 16777216 | tf_op jit(solution)/shard_map/rows_backward/pallas_call | solution.py:371
  151.9 2.7 %sum_split.9 = (bf16[400,256]{1,0:T(8,128)(2,1)}, bf16[400,256]{1,0:T(8,128)(2,1)}, bf16[400,256]{1,0:T(8,128)(2,1)}, bf16[400,256]{1,0:T(8,128)(2,1)}) custom-call(s32[1]{0:T(128)} %bitcast.13.at_ref, bf16[1552,256]{1,0:T(8,128)(2,1)} %get-tuple-element.92.refs_0_, bf16[1552,256]{1,0:T(8,128)(2,1)} %copy-done.1), custom_call_target="tpu_custom_call" | custom-call | tf_op jit(solution)/shard_map/sum_split/pallas_call | solution.py:433
  158.1 5.5 %all-to-all-start.2 = ((bf16[16,6,16,256]{3,2,1,0:T(8,128)(2,1)}), bf16[16,6,16,256]{3,2,1,0:T(8,128)(2,1)S(1)}, u32[]{:S(2)}, u32[]{:S(2)}) async-start(bf16[16,6,16,256]{3,2,1,0:T(8,128)(2,1)} %get-tuple-element.65), calls=%async_computation.2 | async-start | bytes 1572864 | tf_op jit(solution)/shard_map/all_to_all | solution.py:568
  163.6 5.1 %collective-permute-done.16.refs_2_ = bf16[400,256]{1,0:T(8,128)(2,1)S(1)} collective-permute-done((bf16[400,256]{1,0:T(8,128)(2,1)}, bf16[400,256]{1,0:T(8,128)(2,1)S(1)}, u32[]{:S(2)}, u32[]{:S(2)}) %collective-permute-start.16) | collective-permute-done | bytes 204832 | tf_op jit(solution)/shard_map/ppermute | solution.py:517
  171.6 4.7 %collective-permute-start.18 = (bf16[112,256]{1,0:T(8,128)(2,1)}, bf16[112,256]{1,0:T(8,128)(2,1)S(1)}, u32[]{:S(2)}, u32[]{:S(2)}) collective-permute-start(bf16[112,256]{1,0:T(8,128)(2,1)} %get-tuple-element.99), channel_id=1, source_target_pairs={{0,8},{1,9},{2,10},{3,11},{4,12},{5,13},{6,14},{7,15},{8,0},{9,1},... | collective-permute-start | bytes 172040 | tf_op jit(solution)/shard_map/ppermute | solution.py:517
  178.6 2.7 %sum_split.6 = (bf16[400,256]{1,0:T(8,128)(2,1)}, bf16[400,256]{1,0:T(8,128)(2,1)}, bf16[400,256]{1,0:T(8,128)(2,1)}, bf16[400,256]{1,0:T(8,128)(2,1)}) custom-call(s32[1]{0:T(128)} %bitcast.13.at_ref, bf16[1552,256]{1,0:T(8,128)(2,1)} %get-tuple-element.74.refs_0_, bf16[1552,256]{1,0:T(8,128)(2,1)} %copy-done), custom_call_target="tpu_custom_call" | custom-call | tf_op jit(solution)/shard_map/sum_split/pallas_call | solution.py:433
  182.2 6.5 %collective-permute-done.18.refs_1_ = bf16[112,256]{1,0:T(8,128)(2,1)S(1)} collective-permute-done((bf16[112,256]{1,0:T(8,128)(2,1)}, bf16[112,256]{1,0:T(8,128)(2,1)S(1)}, u32[]{:S(2)}, u32[]{:S(2)}) %collective-permute-start.18) | collective-permute-done | bytes 57376 | tf_op jit(solution)/shard_map/ppermute | solution.py:517
  188.7 2.4 collective-permute-start.3
  196.1 3.4 %collective-permute-done.21.refs_1_ = bf16[96,256]{1,0:T(8,128)(2,1)S(1)} collective-permute-done((bf16[96,256]{1,0:T(8,128)(2,1)S(1)}, bf16[96,256]{1,0:T(8,128)(2,1)S(1)}, u32[]{:S(2)}, u32[]{:S(2)}) %collective-permute-start.21) | collective-permute-done | bytes 49184 | tf_op jit(solution)/shard_map/ppermute | solution.py:517
  200.9 4.5 %collective-permute-done.23.refs_3_ = bf16[96,256]{1,0:T(8,128)(2,1)S(1)} collective-permute-done((bf16[96,256]{1,0:T(8,128)(2,1)S(1)}, bf16[96,256]{1,0:T(8,128)(2,1)S(1)}, u32[]{:S(2)}, u32[]{:S(2)}) %collective-permute-start.23) | collective-permute-done | bytes 49184 | tf_op jit(solution)/shard_map/ppermute | solution.py:517
  212.9 2.3 collective-permute-start.6
  216.1 3.0 %collective-permute-done.6.refs_3_ = bf16[112,256]{1,0:T(8,128)(2,1)S(1)} collective-permute-done((bf16[112,256]{1,0:T(8,128)(2,1)}, bf16[112,256]{1,0:T(8,128)(2,1)S(1)}, u32[]{:S(2)}, u32[]{:S(2)}) %collective-permute-start.6) | collective-permute-done | bytes 57376 | tf_op jit(solution)/shard_map/ppermute | solution.py:517
  222.0 2.9 %collective-permute-start.8 = (bf16[96,256]{1,0:T(8,128)(2,1)S(1)}, bf16[96,256]{1,0:T(8,128)(2,1)S(1)}, u32[]{:S(2)}, u32[]{:S(2)}) collective-permute-start(bf16[96,256]{1,0:T(8,128)(2,1)S(1)} %slice.8.refs_0_), channel_id=1, source_target_pairs={{0,4},{1,5},{2,6},{3,7},{4,0},{5,1},{6,2},{7,3},{8,12},{9,13},{10,... | collective-permute-start | bytes 147464 | tf_op jit(solution)/shard_map/ppermute | solution.py:517
  244.4 2.2 join.5
  248.5 3.3 %finish.3 = (f32[1,256]{1,0:T(1,128)}, f32[256,256]{1,0:T(8,128)}, f32[256,256]{1,0:T(8,128)}, f32[256,256]{1,0:T(8,128)}, f32[256,256]{1,0:T(8,128)}, /*index=5...) custom-call(s32[1]{0:T(128)} %bitcast.core_ref.at_ref, bf16[1536,256]{1,0:T(8,128)(2,1)} %bitcast.29, ...), custom_call_target="tpu_custom_call" | custom-call | tf_op jit(solution)/shard_map/finish/pallas_call | solution.py:492
  252.7 3.3 %finish.2 = (f32[1,256]{1,0:T(1,128)}, f32[256,256]{1,0:T(8,128)}, f32[256,256]{1,0:T(8,128)}, f32[256,256]{1,0:T(8,128)}, f32[256,256]{1,0:T(8,128)}, /*index=5...) custom-call(s32[1]{0:T(128)} %bitcast.core_ref.at_ref, bf16[1536,256]{1,0:T(8,128)(2,1)} %bitcast.31, ...), custom_call_target="tpu_custom_call" | custom-call | tf_op jit(solution)/shard_map/finish/pallas_call | solution.py:492
  (129 shorter events, 53.9 us)
Async XLA Ops:
  17.7 26.2 %all-to-all-start = ((bf16[16,6,16,256]{3,2,1,0:T(8,128)(2,1)}), bf16[16,6,16,256]{3,2,1,0:T(8,128)(2,1)S(1)}, u32[]{:S(2)}, u32[]{:S(2)}) async-start(bf16[16,6,16,256]{3,2,1,0:T(8,128)(2,1)} %bitcast.35), calls=%async_computation | async-start | bytes 1572864 | tf_op jit(solution)/shard_map/all_to_all | solution.py:565
  44.0 24.2 %all-to-all-start.1 = ((bf16[16,6,16,256]{3,2,1,0:T(8,128)(2,1)}), bf16[16,6,16,256]{3,2,1,0:T(8,128)(2,1)S(1)}, u32[]{:S(2)}, u32[]{:S(2)}) async-start(bf16[16,6,16,256]{3,2,1,0:T(8,128)(2,1)} %bitcast.6), calls=%async_computation.1 | async-start | bytes 1572864 | tf_op jit(solution)/shard_map/all_to_all | solution.py:565
  99.5 24.3 %all-to-all-start.3 = ((bf16[16,6,16,256]{3,2,1,0:T(8,128)(2,1)}), bf16[16,6,16,256]{3,2,1,0:T(8,128)(2,1)S(1)}, u32[]{:S(2)}, u32[]{:S(2)}) async-start(bf16[16,6,16,256]{3,2,1,0:T(8,128)(2,1)} %get-tuple-element.72), calls=%async_computation.3 | async-start | bytes 1572864 | tf_op jit(solution)/shard_map/all_to_all | solution.py:568
  105.1 45.9 %collective-permute-start.14 = (bf16[1552,256]{1,0:T(8,128)(2,1)S(1)}, bf16[1552,256]{1,0:T(8,128)(2,1)S(1)}, u32[]{:S(2)}, u32[]{:S(2)}) collective-permute-start(bf16[1552,256]{1,0:T(8,128)(2,1)S(1)} %copy-done.34), channel_id=1, source_target_pairs={{0,1},{1,0},{2,3},{3,2},{4,5},{5,4},{6,7},{7,6},{8,9},{9,8},{10,11... | collective-permute-start | bytes 2383880 | tf_op jit(solution)/shard_map/ppermute | solution.py:517
  150.7 27.0 %collective-permute-start = (bf16[1552,256]{1,0:T(8,128)(2,1)}, bf16[1552,256]{1,0:T(8,128)(2,1)S(1)}, u32[]{:S(2)}, u32[]{:S(2)}) collective-permute-start(bf16[1552,256]{1,0:T(8,128)(2,1)} %get-tuple-element.75), channel_id=1, source_target_pairs={{0,1},{1,0},{2,3},{3,2},{4,5},{5,4},{6,7},{7,6},{8,9},{9,8},{10,11... | collective-permute-start | bytes 2383880 | tf_op jit(solution)/shard_map/ppermute | solution.py:517
  154.6 9.0 %collective-permute-start.15 = (bf16[400,256]{1,0:T(8,128)(2,1)}, bf16[400,256]{1,0:T(8,128)(2,1)S(1)}, u32[]{:S(2)}, u32[]{:S(2)}) collective-permute-start(bf16[400,256]{1,0:T(8,128)(2,1)} %get-tuple-element.95), channel_id=1, source_target_pairs={{0,16},{1,17},{2,18},{3,19},{4,20},{5,21},{6,22},{7,23},{8,24},{9,... | collective-permute-start | bytes 614408 | tf_op jit(solution)/shard_map/ppermute | solution.py:517
  156.1 12.7 %collective-permute-start.16 = (bf16[400,256]{1,0:T(8,128)(2,1)}, bf16[400,256]{1,0:T(8,128)(2,1)S(1)}, u32[]{:S(2)}, u32[]{:S(2)}) collective-permute-start(bf16[400,256]{1,0:T(8,128)(2,1)} %get-tuple-element.96), channel_id=1, source_target_pairs={{0,2},{1,3},{2,0},{3,1},{4,6},{5,7},{6,4},{7,5},{8,10},{9,11},{10,... | collective-permute-start | bytes 614408 | tf_op jit(solution)/shard_map/ppermute | solution.py:517
  157.7 11.1 %collective-permute-start.17 = (bf16[400,256]{1,0:T(8,128)(2,1)}, bf16[400,256]{1,0:T(8,128)(2,1)S(1)}, u32[]{:S(2)}, u32[]{:S(2)}) collective-permute-start(bf16[400,256]{1,0:T(8,128)(2,1)} %get-tuple-element.97), channel_id=1, source_target_pairs={{0,18},{1,19},{2,16},{3,17},{4,22},{5,23},{6,20},{7,21},{8,26},{9,... | collective-permute-start | bytes 614408 | tf_op jit(solution)/shard_map/ppermute | solution.py:517
  158.1 88.6 %all-to-all-start.2 = ((bf16[16,6,16,256]{3,2,1,0:T(8,128)(2,1)}), bf16[16,6,16,256]{3,2,1,0:T(8,128)(2,1)S(1)}, u32[]{:S(2)}, u32[]{:S(2)}) async-start(bf16[16,6,16,256]{3,2,1,0:T(8,128)(2,1)} %get-tuple-element.65), calls=%async_computation.2 | async-start | bytes 1572864 | tf_op jit(solution)/shard_map/all_to_all | solution.py:568
  171.6 17.1 %collective-permute-start.18 = (bf16[112,256]{1,0:T(8,128)(2,1)}, bf16[112,256]{1,0:T(8,128)(2,1)S(1)}, u32[]{:S(2)}, u32[]{:S(2)}) collective-permute-start(bf16[112,256]{1,0:T(8,128)(2,1)} %get-tuple-element.99), channel_id=1, source_target_pairs={{0,8},{1,9},{2,10},{3,11},{4,12},{5,13},{6,14},{7,15},{8,0},{9,1},... | collective-permute-start | bytes 172040 | tf_op jit(solution)/shard_map/ppermute | solution.py:517
  176.2 14.8 %collective-permute-start.19 = (bf16[112,256]{1,0:T(8,128)(2,1)}, bf16[112,256]{1,0:T(8,128)(2,1)S(1)}, u32[]{:S(2)}, u32[]{:S(2)}) collective-permute-start(bf16[112,256]{1,0:T(8,128)(2,1)} %get-tuple-element.100), channel_id=1, source_target_pairs={{0,4},{1,5},{2,6},{3,7},{4,0},{5,1},{6,2},{7,3},{8,12},{9,13},{10,... | collective-permute-start | bytes 172040 | tf_op jit(solution)/shard_map/ppermute | solution.py:517
  176.2 14.8 %collective-permute-start.20 = (bf16[112,256]{1,0:T(8,128)(2,1)}, bf16[112,256]{1,0:T(8,128)(2,1)S(1)}, u32[]{:S(2)}, u32[]{:S(2)}) collective-permute-start(bf16[112,256]{1,0:T(8,128)(2,1)} %get-tuple-element.101), channel_id=1, source_target_pairs={{0,12},{1,13},{2,14},{3,15},{4,8},{5,9},{6,10},{7,11},{8,4},{9,5},... | collective-permute-start | bytes 172040 | tf_op jit(solution)/shard_map/ppermute | solution.py:517
  181.3 26.6 %collective-permute-start.1 = (bf16[400,256]{1,0:T(8,128)(2,1)}, bf16[400,256]{1,0:T(8,128)(2,1)S(1)}, u32[]{:S(2)}, u32[]{:S(2)}) collective-permute-start(bf16[400,256]{1,0:T(8,128)(2,1)} %get-tuple-element.77), channel_id=1, source_target_pairs={{0,16},{1,17},{2,18},{3,19},{4,20},{5,21},{6,22},{7,23},{8,24},{9,... | collective-permute-start | bytes 614408 | tf_op jit(solution)/shard_map/ppermute | solution.py:517
  181.5 26.4 %collective-permute-start.2 = (bf16[400,256]{1,0:T(8,128)(2,1)}, bf16[400,256]{1,0:T(8,128)(2,1)S(1)}, u32[]{:S(2)}, u32[]{:S(2)}) collective-permute-start(bf16[400,256]{1,0:T(8,128)(2,1)} %get-tuple-element.78), channel_id=1, source_target_pairs={{0,2},{1,3},{2,0},{3,1},{4,6},{5,7},{6,4},{7,5},{8,10},{9,11},{10,... | collective-permute-start | bytes 614408 | tf_op jit(solution)/shard_map/ppermute | solution.py:517
  188.7 19.2 %collective-permute-start.3 = (bf16[400,256]{1,0:T(8,128)(2,1)}, bf16[400,256]{1,0:T(8,128)(2,1)S(1)}, u32[]{:S(2)}, u32[]{:S(2)}) collective-permute-start(bf16[400,256]{1,0:T(8,128)(2,1)} %get-tuple-element.79), channel_id=1, source_target_pairs={{0,18},{1,19},{2,16},{3,17},{4,22},{5,23},{6,20},{7,21},{8,26},{9,... | collective-permute-start | bytes 614408 | tf_op jit(solution)/shard_map/ppermute | solution.py:517
  194.1 6.8 %collective-permute-start.22 = (bf16[96,256]{1,0:T(8,128)(2,1)S(1)}, bf16[96,256]{1,0:T(8,128)(2,1)S(1)}, u32[]{:S(2)}, u32[]{:S(2)}) collective-permute-start(bf16[96,256]{1,0:T(8,128)(2,1)S(1)} %slice.9.refs_0_), channel_id=1, source_target_pairs={{0,4},{1,5},{2,6},{3,7},{4,0},{5,1},{6,2},{7,3},{8,12},{9,13},{10,... | collective-permute-start | bytes 147464 | tf_op jit(solution)/shard_map/ppermute | solution.py:517
  207.6 27.5 %collective-permute-start.24 = (bf16[384,256]{1,0:T(8,128)(2,1)}, bf16[384,256]{1,0:T(8,128)(2,1)S(1)}, u32[]{:S(2)}, u32[]{:S(2)}) collective-permute-start(bf16[384,256]{1,0:T(8,128)(2,1)} %bitcast.36), channel_id=1, source_target_pairs={{0,16},{1,17},{2,18},{3,19},{4,20},{5,21},{6,22},{7,23},{8,24},{9,... | collective-permute-start | bytes 589832 | tf_op jit(solution)/shard_map/ppermute | solution.py:517
  212.9 6.2 %collective-permute-start.6 = (bf16[112,256]{1,0:T(8,128)(2,1)}, bf16[112,256]{1,0:T(8,128)(2,1)S(1)}, u32[]{:S(2)}, u32[]{:S(2)}) collective-permute-start(bf16[112,256]{1,0:T(8,128)(2,1)} %get-tuple-element.83), channel_id=1, source_target_pairs={{0,12},{1,13},{2,14},{3,15},{4,8},{5,9},{6,10},{7,11},{8,4},{9,5},... | collective-permute-start | bytes 172040 | tf_op jit(solution)/shard_map/ppermute | solution.py:517
  222.0 7.5 %collective-permute-start.8 = (bf16[96,256]{1,0:T(8,128)(2,1)S(1)}, bf16[96,256]{1,0:T(8,128)(2,1)S(1)}, u32[]{:S(2)}, u32[]{:S(2)}) collective-permute-start(bf16[96,256]{1,0:T(8,128)(2,1)S(1)} %slice.8.refs_0_), channel_id=1, source_target_pairs={{0,4},{1,5},{2,6},{3,7},{4,0},{5,1},{6,2},{7,3},{8,12},{9,13},{10,... | collective-permute-start | bytes 147464 | tf_op jit(solution)/shard_map/ppermute | solution.py:517
  226.4 11.7 %collective-permute-start.25 = (bf16[384,256]{1,0:T(8,128)(2,1)}, bf16[384,256]{1,0:T(8,128)(2,1)S(1)}, u32[]{:S(2)}, u32[]{:S(2)}) collective-permute-start(bf16[384,256]{1,0:T(8,128)(2,1)} %bitcast.37), channel_id=1, source_target_pairs={{0,2},{1,3},{2,0},{3,1},{4,6},{5,7},{6,4},{7,5},{8,10},{9,11},{10,... | collective-permute-start | bytes 589832 | tf_op jit(solution)/shard_map/ppermute | solution.py:517
  227.4 10.8 %collective-permute-start.26 = (bf16[384,256]{1,0:T(8,128)(2,1)}, bf16[384,256]{1,0:T(8,128)(2,1)S(1)}, u32[]{:S(2)}, u32[]{:S(2)}) collective-permute-start(bf16[384,256]{1,0:T(8,128)(2,1)} %bitcast.38), channel_id=1, source_target_pairs={{0,18},{1,19},{2,16},{3,17},{4,22},{5,23},{6,20},{7,21},{8,26},{9,... | collective-permute-start | bytes 589832 | tf_op jit(solution)/shard_map/ppermute | solution.py:517
  233.0 8.7 %collective-permute-start.10 = (bf16[384,256]{1,0:T(8,128)(2,1)}, bf16[384,256]{1,0:T(8,128)(2,1)S(1)}, u32[]{:S(2)}, u32[]{:S(2)}) collective-permute-start(bf16[384,256]{1,0:T(8,128)(2,1)} %bitcast.40), channel_id=1, source_target_pairs={{0,16},{1,17},{2,18},{3,19},{4,20},{5,21},{6,22},{7,23},{8,24},{9,... | collective-permute-start | bytes 589832 | tf_op jit(solution)/shard_map/ppermute | solution.py:517
  235.1 8.0 %collective-permute-start.11 = (bf16[384,256]{1,0:T(8,128)(2,1)}, bf16[384,256]{1,0:T(8,128)(2,1)S(1)}, u32[]{:S(2)}, u32[]{:S(2)}) collective-permute-start(bf16[384,256]{1,0:T(8,128)(2,1)} %bitcast.41), channel_id=1, source_target_pairs={{0,2},{1,3},{2,0},{3,1},{4,6},{5,7},{6,4},{7,5},{8,10},{9,11},{10,... | collective-permute-start | bytes 589832 | tf_op jit(solution)/shard_map/ppermute | solution.py:517
  235.1 8.0 %collective-permute-start.12 = (bf16[384,256]{1,0:T(8,128)(2,1)}, bf16[384,256]{1,0:T(8,128)(2,1)S(1)}, u32[]{:S(2)}, u32[]{:S(2)}) collective-permute-start(bf16[384,256]{1,0:T(8,128)(2,1)} %bitcast.42), channel_id=1, source_target_pairs={{0,18},{1,19},{2,16},{3,17},{4,22},{5,23},{6,20},{7,21},{8,26},{9,... | collective-permute-start | bytes 589832 | tf_op jit(solution)/shard_map/ppermute | solution.py:517
  (43 other events, 149.7 us)

commit v2 on v1

v2 whole, which is shorter than its diff:
```python
import functools
import math

import jax
import jax.numpy as jnp
from jax import lax
from jax.experimental import pallas as pl
from jax.experimental.pallas import tpu as pltpu
from jax.sharding import PartitionSpec as P

HEADS = 2
EPS = 1e-05
GROUP = 8
TAIL = 16
HIDDEN_TILE = 256
VMEM_LIMIT = 24 * 1024 * 1024
SMALL_LIMIT = 12 * 1024 * 1024
ALL = ("img", "row")
HEAVY = 1 << 25
PLACE = 1
F32 = jnp.float32
BF16 = jnp.bfloat16


def mm(left, right):
    return lax.dot_general(left, right, (((1,), (0,)), ((), ())), preferred_element_type=F32)


def mm_right_t(left, right):
    return lax.dot_general(left, right, (((1,), (1,)), ((), ())), preferred_element_type=F32)


def mm_left_t(left, right):
    return lax.dot_general(left, right, (((0,), (0,)), ((), ())), preferred_element_type=F32)


def normalize(stream):
    centred = stream - jnp.mean(stream, axis=-1, keepdims=True)
    inverse = lax.rsqrt(jnp.mean(centred * centred, axis=-1, keepdims=True) + EPS)
    return centred * inverse, inverse


def normalize_back(upstream, normal, inverse, gain):
    scaled = upstream * gain
    centred = (
        scaled
        - jnp.mean(scaled, axis=-1, keepdims=True)
        - normal * jnp.mean(scaled * normal, axis=-1, keepdims=True)
    )
    return inverse * centred, jnp.sum(upstream * normal, axis=0, keepdims=True)


ROOT = math.sqrt(2.0 / math.pi)
CUBE = 0.044715


def gelu(value):
    bent = jnp.tanh(ROOT * (value + CUBE * (value * value * value)))
    return 0.5 * value * (1.0 + bent)


def gelu_both(value):
    square = value * value
    bent = jnp.tanh(ROOT * (value + CUBE * (square * value)))
    half = 0.5 * (1.0 + bent)
    slope = half + (0.5 * ROOT) * value * (1.0 - bent * bent) * (1.0 + (3.0 * CUBE) * square)
    return value * half, slope


def softmax(scores):
    risen = jnp.exp(scores - jnp.max(scores, axis=-1, keepdims=True))
    return risen * (1.0 / jnp.sum(risen, axis=-1, keepdims=True))


def causal_bias(size, period):
    row = lax.broadcasted_iota(jnp.int32, (size, size), 0)
    col = lax.broadcasted_iota(jnp.int32, (size, size), 1)
    visible = (row >= col) & (((row ^ col) & (period - 1)) == 0)
    return jnp.where(visible, 0.0, -1e30).astype(F32)


def head_places(groups, tokens, features):
    return [
        (slice(i * tokens, (i + 1) * tokens), slice(m * features, (m + 1) * features))
        for i in range(groups)
        for m in range(HEADS)
    ]


def merge_heads(parts):
    pairs = [parts[i : i + HEADS] for i in range(0, len(parts), HEADS)]
    return jnp.concatenate([jnp.concatenate(pair, axis=1) for pair in pairs], axis=0)


def attend_back(up, query, key, value, probs, places, scaling):
    prob_grads = [mm_right_t(up[at], value[at]) for at in places]
    score_grads = []
    for prob, prob_grad in zip(probs, prob_grads):
        inner = jnp.sum(prob * prob_grad, axis=-1, keepdims=True)
        score_grads.append((prob * (prob_grad - inner)).astype(BF16))
    value_grads = [mm_left_t(prob.astype(BF16), up[at]).astype(BF16) for prob, at in zip(probs, places)]
    query_grads = [(mm(grad, key[at]) * scaling).astype(BF16) for grad, at in zip(score_grads, places)]
    key_grads = [(mm_left_t(grad, query[at]) * scaling).astype(BF16) for grad, at in zip(score_grads, places)]
    return tuple(merge_heads(grads) for grads in (query_grads, key_grads, value_grads))


def feed_back(normed, up_low, expand_ref, shrink_ref, acc, first, forward):
    width = normed.shape[-1]
    hidden_width = expand_ref.shape[1]
    tile = min(HIDDEN_TILE, hidden_width)
    result = None
    normed_grad = None
    for j in range(hidden_width // tile):
        cut = slice(j * tile, (j + 1) * tile)
        expand = expand_ref[:, cut]
        shrink = shrink_ref[cut, :]
        hidden, slope = gelu_both(mm(normed, expand))
        hidden = hidden.astype(BF16)
        if forward:
            part = mm(hidden, shrink)
            result = part if result is None else result + part
        expanded_grad = (slope * mm_right_t(up_low, shrink)).astype(BF16)
        at = first + j * width
        acc[at : at + width, :] += mm_left_t(normed, expanded_grad)
        at = first + hidden_width // tile * width + j * width
        acc[at : at + width, :] += mm_left_t(up_low, hidden)
        part = mm_right_t(expanded_grad, expand)
        normed_grad = part if normed_grad is None else normed_grad + part
    return result, normed_grad


def project_back(normed_low, grads, weight_refs, acc):
    width = normed_low.shape[-1]
    total = None
    for i, (grad, weight_ref) in enumerate(zip(grads, weight_refs)):
        acc[i * width : (i + 1) * width, :] += mm_left_t(normed_low, grad)
        part = mm_right_t(grad, weight_ref[...])
        total = part if total is None else total + part
    return total


def store_tail(ref, at, gains):
    high = gains.astype(BF16)
    ref[at : at + 8, :] = high
    ref[at + 8 : at + 16, :] = (gains - high.astype(F32)).astype(BF16)


def emit_grads(core, acc, gains, keep_ref, send_ref):
    half = acc.shape[0] // 2
    for which, (mine, other) in enumerate(((keep_ref, send_ref), (send_ref, keep_ref))):

        @pl.when(core == which)
        def _():
            mine[0:half, :] = acc[0:half, :].astype(BF16)
            other[0:half, :] = acc[half:, :].astype(BF16)

    store_tail(keep_ref, half, gains)
    store_tail(send_ref, half, gains)


def rows_forward_kernel(
    x_ref, ga_ref, wq_ref, wk_ref, wv_ref, wo_ref, gb_ref, w1_ref, w2_ref,
    send_ref, q_ref, k_ref, v_ref, att_ref, mid_ref, p_ref,
):
    rows, images, cols, width = x_ref.shape
    tokens = rows * images * cols
    features = width // HEADS
    scaling = 1.0 / math.sqrt(features)
    stream = x_ref[...].astype(F32).reshape(tokens, width)
    normed = (normalize(stream)[0] * ga_ref[...]).astype(BF16)
    query = mm(normed, wq_ref[...]).astype(BF16)
    key = mm(normed, wk_ref[...]).astype(BF16)
    value = mm(normed, wv_ref[...]).astype(BF16)
    q_ref[...] = query.reshape(q_ref.shape)
    k_ref[...] = key.reshape(q_ref.shape)
    v_ref[...] = value.reshape(q_ref.shape)
    bias = causal_bias(cols, 1)
    places = head_places(rows * images, cols, features)
    probs = [softmax(mm_right_t(query[at], key[at]) * scaling + bias) for at in places]
    heads = [mm(prob.astype(BF16), value[at]) for prob, at in zip(probs, places)]
    for i, prob in enumerate(probs):
        group, m = divmod(i, HEADS)
        p_ref[group // images, group % images, m] = prob
    attended = merge_heads(heads).astype(BF16)
    att_ref[...] = attended.reshape(att_ref.shape)
    middle = stream + mm(attended, wo_ref[...])
    mid_ref[...] = middle.reshape(mid_ref.shape)
    normed_b = (normalize(middle)[0] * gb_ref[...]).astype(BF16)
    hidden_width = w1_ref.shape[1]
    tile = min(HIDDEN_TILE, hidden_width)
    result = middle
    for j in range(hidden_width // tile):
        cut = slice(j * tile, (j + 1) * tile)
        hidden = gelu(mm(normed_b, w1_ref[:, cut])).astype(BF16)
        result = result + mm(hidden, w2_ref[cut, :])
    result = result.reshape(rows, images * cols // GROUP, GROUP, width)
    result = jnp.concatenate([result[r] for r in range(rows)], axis=1)
    send_ref[...] = result.astype(BF16).reshape(send_ref.shape)


def rows_backward_kernel(
    core_ref, up_ref, ga_ref, gb_ref, mid_hbm, w1_hbm, w2_hbm, att_hbm, wo_hbm,
    q_hbm, k_hbm, v_hbm, p_hbm, x_hbm, wq_hbm, wk_hbm, wv_hbm, _,
    grad_ref, keep_ref, send_ref,
    acc, gains, mid_ref, w1_ref, w2_ref, att_ref, wo_ref, q_ref, k_ref, v_ref, p_ref, x_ref, wq_ref, wk_ref, wv_ref, done,
):
    rows, all_images, cols, width = x_ref.shape
    step = pl.program_id(0)
    images = all_images // pl.num_programs(0)
    tokens = rows * images * cols
    here = pl.ds(step * images, images)
    features = width // HEADS
    scaling = 1.0 / math.sqrt(features)
    sources = (mid_hbm, w1_hbm, w2_hbm, att_hbm, wo_hbm, q_hbm, k_hbm, v_hbm, p_hbm, x_hbm, wq_hbm, wk_hbm, wv_hbm)
    targets = (mid_ref, w1_ref, w2_ref, att_ref, wo_ref, q_ref, k_ref, v_ref, p_ref, x_ref, wq_ref, wk_ref, wv_ref)
    copies = [pltpu.make_async_copy(sources[i], targets[i], done.at[i]) for i in range(len(sources))]

    def wait(first, last):
        @pl.when(step == 0)
        def _():
            for copy in copies[first:last]:
                copy.wait()

    @pl.when(step == 0)
    def _():
        for copy in copies:
            copy.start()
        acc[...] = jnp.zeros_like(acc)
        gains[...] = jnp.zeros_like(gains)

    wait(0, 3)
    up = up_ref[here].astype(F32).reshape(images * cols // GROUP, rows * GROUP, width)
    up = jnp.concatenate(
        [up[:, r * GROUP : (r + 1) * GROUP].reshape(images * cols, width) for r in range(rows)], axis=0
    )
    up_low = up.astype(BF16)
    normal_b, inverse_b = normalize(mid_ref[:, here].reshape(tokens, width))
    normed_b = (normal_b * gb_ref[...]).astype(BF16)
    _, normed_grad = feed_back(normed_b, up_low, w1_ref, w2_ref, acc, 4 * width, False)
    middle_norm, scale_grad = normalize_back(normed_grad, normal_b, inverse_b, gb_ref[...])
    gains[1:2, :] += scale_grad
    middle_grad = up + middle_norm
    middle_low = middle_grad.astype(BF16)
    wait(3, len(sources))
    acc[3 * width : 4 * width, :] += mm_left_t(att_ref[:, here].reshape(tokens, width), middle_low)
    up_att = mm_right_t(middle_low, wo_ref[...]).astype(BF16)
    query = q_ref[:, here].reshape(tokens, width)
    key = k_ref[:, here].reshape(tokens, width)
    value = v_ref[:, here].reshape(tokens, width)
    places = head_places(rows * images, cols, features)
    probs = [p_ref[r, step * images + i, m] for r in range(rows) for i in range(images) for m in range(HEADS)]
    grads = attend_back(up_att, query, key, value, probs, places, scaling)
    normal_a, inverse_a = normalize(x_ref[:, here].astype(F32).reshape(tokens, width))
    normed_a = (normal_a * ga_ref[...]).astype(BF16)
    normed_grad = project_back(normed_a, grads, (wq_ref, wk_ref, wv_ref), acc)
    stream_norm, gain_grad = normalize_back(normed_grad, normal_a, inverse_a, ga_ref[...])
    gains[0:1, :] += gain_grad
    grad_ref[...] = (middle_grad + stream_norm).reshape(grad_ref.shape)

    @pl.when(step == pl.num_programs(0) - 1)
    def _():
        emit_grads(core_ref[0], acc, gains[...], keep_ref, send_ref)


def unpack_kernel(in_ref, _, out_ref):
    rows, images, cols, width = out_ref.shape
    array = in_ref[...].astype(F32).reshape(images * cols // GROUP, rows * GROUP, width)
    for r in range(rows):
        part = array[:, r * GROUP : (r + 1) * GROUP].reshape(images, cols, width)
        out_ref[r] = part.astype(BF16)


def load_groups(ref, first, groups):
    sources, _, height, width = ref.shape
    parts = [ref[:, first + i].astype(F32).reshape(sources * height, width) for i in range(groups)]
    return jnp.concatenate(parts, axis=0)


def store_groups(ref, first, groups, value):
    sources, _, height, width = ref.shape
    tokens = sources * height
    for i in range(groups):
        part = value[i * tokens : (i + 1) * tokens].reshape(sources, height, width)
        ref[:, first + i] = part.astype(ref.dtype)


def columns_kernel(
    core_ref, x_ref, up_ref, ga_ref, wq_ref, wk_ref, wv_ref, wo_ref, gb_ref, w1_ref, w2_ref,
    out_ref, grad_ref, keep_ref, send_ref, acc, gains, bias,
):
    width = x_ref.shape[-1]
    groups = x_ref.shape[1] // pl.num_programs(0)
    tokens = x_ref.shape[0] * x_ref.shape[2]
    features = width // HEADS
    scaling = 1.0 / math.sqrt(features)
    step = pl.program_id(0)

    @pl.when(step == 0)
    def _():
        acc[...] = jnp.zeros_like(acc)
        gains[...] = jnp.zeros_like(gains)
        bias[...] = causal_bias(tokens, GROUP)

    first = step * groups
    stream = load_groups(x_ref, first, groups)
    normal_a, inverse_a = normalize(stream)
    normed_a = (normal_a * ga_ref[...]).astype(BF16)
    query = mm(normed_a, wq_ref[...]).astype(BF16)
    key = mm(normed_a, wk_ref[...]).astype(BF16)
    value = mm(normed_a, wv_ref[...]).astype(BF16)
    places = head_places(groups, tokens, features)
    probs = [softmax(mm_right_t(query[at], key[at]) * scaling + bias[...]) for at in places]
    heads = [mm(prob.astype(BF16), value[at]) for prob, at in zip(probs, places)]

    attended = merge_heads(heads).astype(BF16)
    middle = stream + mm(attended, wo_ref[...])
    normal_b, inverse_b = normalize(middle)
    normed_b = (normal_b * gb_ref[...]).astype(BF16)
    up = load_groups(up_ref, first, groups)
    up_low = up.astype(BF16)
    result, normed_grad = feed_back(normed_b, up_low, w1_ref, w2_ref, acc, 4 * width, True)
    store_groups(out_ref, first, groups, middle + result)
    middle_norm, scale_grad = normalize_back(normed_grad, normal_b, inverse_b, gb_ref[...])
    gains[1:2, :] += scale_grad
    middle_grad = up + middle_norm
    middle_low = middle_grad.astype(BF16)
    acc[3 * width : 4 * width, :] += mm_left_t(attended, middle_low)
    up_att = mm_right_t(middle_low, wo_ref[...]).astype(BF16)
    grads = attend_back(up_att, query, key, value, probs, places, scaling)
    normed_grad = project_back(normed_a, grads, (wq_ref, wk_ref, wv_ref), acc)
    stream_norm, gain_grad = normalize_back(normed_grad, normal_a, inverse_a, ga_ref[...])
    gains[0:1, :] += gain_grad
    store_groups(grad_ref, first, groups, middle_grad + stream_norm)

    @pl.when(step == pl.num_programs(0) - 1)
    def _():
        emit_grads(core_ref[0], acc, gains[...], keep_ref, send_ref)


def whole(array):
    zeros = (0,) * array.ndim
    return pl.BlockSpec(array.shape, lambda i: zeros)


def whole_out(shape):
    zeros = (0,) * len(shape)
    return pl.BlockSpec(shape, lambda i: zeros)


SCALAR = pl.BlockSpec(memory_space=pltpu.SMEM)
HELD = pl.BlockSpec(memory_space=pltpu.VMEM)
UNREAD = pl.BlockSpec(memory_space=pl.ANY)


def held(array):
    return pltpu.with_memory_space_constraint(array, pltpu.VMEM)


def params(limit=VMEM_LIMIT):
    return pltpu.CompilerParams(vmem_limit_bytes=limit)


def shape_of(shape, dtype):
    return jax.ShapeDtypeStruct(shape, dtype)


def held_shape(shape, dtype):
    return pltpu.VMEM(shape, dtype)


def stored_shape(shape, dtype):
    return pltpu.HBM(shape, dtype)


def stored(array):
    return pltpu.with_memory_space_constraint(array, pltpu.HBM)


def grad_rows(width, hidden_width):
    tile = min(HIDDEN_TILE, hidden_width)
    return 4 * width + 2 * (hidden_width // tile) * width


def cost(*_):
    return pl.CostEstimate(flops=1, bytes_accessed=1, transcendentals=0)


def rows_forward(inputs, gains, matrices):
    rows, images, cols, width = inputs.shape
    low = stored_shape(inputs.shape, BF16)
    wq, wk, wv, wo, w1, w2 = matrices
    operands = [stored(array) for array in (inputs, gains[0], wq, wk, wv, wo, gains[1], w1, w2)]
    outs = [
        held_shape((images, cols // GROUP, rows * GROUP, width), BF16),
        low, low, low, low,
        stored_shape(inputs.shape, F32),
        stored_shape((rows, images, HEADS, cols, cols), F32),
    ]
    return pl.pallas_call(
        rows_forward_kernel,
        grid=(1,),
        in_specs=[whole(array) for array in operands],
        out_specs=[HELD] + [whole_out(out.shape) for out in outs[1:]],
        out_shape=outs,
        compiler_params=params(),
        cost_estimate=cost(),
        name="rows_forward",
    )(*operands)


def rows_backward(core, up, gains, kept, steps, after):
    rows, images, cols, width = kept[0].shape
    total = grad_rows(width, kept[1].shape[1])
    part = (total // 2 + TAIL, width)
    spec = pl.BlockSpec((rows, images // steps, cols, width), lambda i: (0, i, 0, 0))
    return pl.pallas_call(
        rows_backward_kernel,
        grid=(steps,),
        in_specs=[SCALAR] + [HELD] * 3 + [UNREAD] * (len(kept) + 1),
        out_specs=[spec, HELD, HELD],
        out_shape=[shape_of(kept[0].shape, F32), held_shape(part, BF16), held_shape(part, BF16)],
        scratch_shapes=[pltpu.VMEM((total, width), F32), pltpu.VMEM((8, width), F32)]
        + [pltpu.VMEM(array.shape, array.dtype) for array in kept]
        + [pltpu.SemaphoreType.DMA((len(kept),))],
        compiler_params=params(40 * 1024 * 1024),
        cost_estimate=cost(),
        name="rows_backward",
    )(core, held(up), *gains, *[stored(array) for array in kept], after)


def unpack(array, shape, after):
    return pl.pallas_call(
        unpack_kernel,
        in_specs=[HELD, UNREAD],
        out_specs=pl.BlockSpec(memory_space=pltpu.VMEM),
        out_shape=shape_of(shape, BF16),
        compiler_params=params(SMALL_LIMIT),
        cost_estimate=cost(),
        name="unpack",
    )(held(array), after)


def columns_both(core, stream, up, gains, matrices, steps):
    sources, groups, height, width = stream.shape
    total = grad_rows(width, matrices[4].shape[1])
    tokens = sources * height
    part = (total // 2 + TAIL, width)
    wq, wk, wv, wo, w1, w2 = matrices
    operands = [stored(array) for array in (gains[0], wq, wk, wv, wo, gains[1], w1, w2)]
    return pl.pallas_call(
        columns_kernel,
        grid=(steps,),
        in_specs=[SCALAR, HELD, HELD] + [whole(array) for array in operands],
        out_specs=[HELD] * 4,
        out_shape=[held_shape(stream.shape, BF16)] * 2 + [held_shape(part, BF16)] * 2,
        scratch_shapes=[
            pltpu.VMEM((total, width), F32),
            pltpu.VMEM((8, width), F32),
            pltpu.VMEM((tokens, tokens), F32),
        ],
        compiler_params=params(),
        cost_estimate=cost(),
        name="columns_both",
    )(core, held(stream), held(up), *operands)


def add_parts(refs, size):
    total, gains = None, None
    for ref in refs:
        rows = ref[0:size, :].astype(F32)
        tail = ref[size : size + 8, :].astype(F32) + ref[size + 8 : size + TAIL, :].astype(F32)
        total = rows if total is None else total + rows
        gains = tail if gains is None else gains + tail
    return total.astype(BF16), gains


def sum_split_kernel(count, size, ways, sends, at_ref, *refs):
    ins, rider, outs = refs[:count], refs[count + 1 : -1 - sends], refs[-1 - sends : -1]
    parts = refs[-1]
    total, gains = add_parts(ins, size)
    step = size // ways
    for j in range(ways):
        parts[j] = total[j * step : (j + 1) * step, :]
    for j, out in enumerate(outs):
        out[0:step, :] = parts[(at_ref[0] & (ways - 1)) ^ j]
        store_tail(out, step, gains)
        if rider and j:
            out[step + TAIL :, :] = rider[0][...]


def sum_split(at, arrays, size, ways, sends, after, rider=None, heavy=False):
    width = arrays[0].shape[1]
    step = size // ways
    extra = 0 if rider is None else rider.shape[0]
    shapes = [(step + TAIL + (extra if j else 0), width) for j in range(sends)]
    riders = [] if rider is None else [held(rider)]
    return pl.pallas_call(
        functools.partial(sum_split_kernel, len(arrays), size, ways, sends),
        in_specs=[SCALAR] + [HELD] * len(arrays) + [UNREAD] + [HELD] * len(riders),
        out_specs=[HELD] * sends,
        out_shape=[held_shape(shape, BF16) for shape in shapes],
        scratch_shapes=[pltpu.VMEM((ways, step, width), BF16)],
        compiler_params=params(SMALL_LIMIT),
        cost_estimate=small_cost(arrays, heavy),
        name="sum_split",
    )(at, *[held(array) for array in arrays], after, *riders)


def sum_last_kernel(count, size, *refs):
    ins, (part, tail) = refs[:count], refs[count + 1 :]
    total, gains = add_parts(ins, size)
    part[...] = total
    store_tail(tail, 0, gains)


def sum_last(arrays, size, after, heavy=False):
    width = arrays[0].shape[1]
    return pl.pallas_call(
        functools.partial(sum_last_kernel, len(arrays), size),
        in_specs=[HELD] * len(arrays) + [UNREAD],
        out_specs=[HELD] * 2,
        out_shape=[held_shape((size, width), BF16), held_shape((TAIL, width), BF16)],
        compiler_params=params(SMALL_LIMIT),
        cost_estimate=small_cost(arrays, heavy),
        name="sum_last",
    )(*[held(array) for array in arrays], after)


def join_kernel(ways, first, at_ref, *refs):
    ins, out = refs[:ways], refs[-1]
    size = out.shape[1]
    for j in range(ways):
        start = first if j else 0
        out[at_ref[0] ^ j] = ins[j][start : start + size, :]


def join(at, arrays, first, after):
    ways, (size, width) = len(arrays), arrays[0].shape
    joined = pl.pallas_call(
        functools.partial(join_kernel, ways, first),
        in_specs=[SCALAR] + [HELD] * ways + [UNREAD],
        out_specs=HELD,
        out_shape=held_shape((ways, size, width), BF16),
        compiler_params=params(SMALL_LIMIT),
        cost_estimate=small_cost(arrays),
        name="join",
    )(at, *[held(array) for array in arrays], after)
    return joined.reshape(ways * size, width)


def finish_kernel(buffers, at_ref, own_ref, other_ref, tail_ref, _, *refs):
    outs, halves = list(refs[:-1]), refs[-1]
    width = own_ref.shape[1]
    halves[at_ref[0]] = own_ref[...]
    halves[at_ref[0] ^ 1] = other_ref[...]
    gains = tail_ref[0:8, :].astype(F32) + tail_ref[8:16, :].astype(F32)
    first = 0
    for rows, kinds in buffers:
        at = 0
        for kind in kinds:
            out = outs.pop(0)
            if isinstance(kind, int):
                out[...] = gains[kind : kind + 1, :]
                continue
            for j in range(out.size // (width * width)):
                half, row = divmod(at * width, rows // 2)
                block = halves[half, first + row : first + row + width, :].astype(F32)
                if kind == "rows":
                    out[j * width : (j + 1) * width, :] = block.T
                else:
                    out[:, j * width : (j + 1) * width] = block
                at += 1
        first += rows // 2


def finish(at, own, other, tail, buffers, hidden_width, after):
    half, width = own.shape
    shapes = {"square": (width, width), "columns": (width, hidden_width), "rows": (hidden_width, width)}
    kinds = [kind for _, each in buffers for kind in each]
    outs = [shapes.get(kind, (1, width)) for kind in kinds]
    outs = pl.pallas_call(
        functools.partial(finish_kernel, buffers),
        grid=(1,),
        in_specs=[SCALAR, HELD, HELD, HELD, UNREAD],
        out_specs=[whole_out(shape) for shape in outs],
        out_shape=[shape_of(shape, F32) for shape in outs],
        scratch_shapes=[pltpu.VMEM((2, half, width), BF16)],
        compiler_params=params(24 * 1024 * 1024),
        cost_estimate=cost(),
        name="finish",
    )(at, held(own), held(other), held(tail), after)
    return [out.reshape(width) if isinstance(kind, int) else out for kind, out in zip(kinds, outs)]


def small_cost(arrays, heavy=False):
    moved = HEAVY if heavy else 1
    return pl.CostEstimate(flops=moved, bytes_accessed=moved, transcendentals=0)


class Exchange:
    def __init__(self, bits, scatter, flat, devices):
        self.bits, self.scatter = bits, scatter
        self.ways = 1 << len(bits)
        place = sum(((flat >> bit) & 1) << i for i, bit in enumerate(bits))
        self.place = jnp.reshape(place, (1,)).astype(jnp.int32)
        self.devices = devices

    def swap(self, array, member):
        mask = sum(1 << bit for i, bit in enumerate(self.bits) if (member >> i) & 1)
        return lax.ppermute(array, ALL, [(i, i ^ mask) for i in range(self.devices)])


class Chain:
    def __init__(self, exchanges, buffers, keep, send, hidden_width):
        self.pair, self.four, *self.others = exchanges
        self.rows = sum(rows for rows, _ in buffers) // 2
        self.arrays = [keep, self.pair.swap(send, 1)]
        self.token = keep
        self.buffers, self.hidden_width = buffers, hidden_width

    def cut(self, after, rider=None):
        ways = self.four.ways
        parts = sum_split(self.four.place, self.arrays, self.rows, ways, ways, after, rider)
        self.arrays = [parts[0]] + [self.four.swap(parts[j], j) for j in range(1, ways)]
        self.rows //= ways
        return parts[0]

    def add(self, after, heavy=False):
        exchange = self.others.pop(0)
        (part,) = sum_split(self.pair.place, self.arrays, self.rows, 1, 1, after, heavy=heavy)
        self.arrays = [part, exchange.swap(part, 1)]
        return part

    def last(self, after, heavy=False):
        self.part, self.tail = sum_last(self.arrays, self.rows, after, heavy)
        return self.part

    def spread(self):
        self.pieces = [self.part] + [self.four.swap(self.part, j) for j in range(1, self.four.ways)]
        self.first = 0

    def ride(self, chain):
        self.pieces = [self.part] + chain.arrays[1:]
        self.first = chain.rows + TAIL

    def join(self, after):
        self.own = join(self.four.place, self.pieces, self.first, after)
        self.other = self.pair.swap(self.own, 1)
        return self.own

    def finish(self, after):
        self.results = finish(self.pair.place, self.own, self.other, self.tail, self.buffers, self.hidden_width, after)
        return self.results[0]


def on_device(inputs, cotangent, *weights):
    rows, images, cols, width = inputs.shape
    groups = cols // GROUP
    height = lax.axis_size("row")
    devices = height * lax.axis_size("img")
    flat = lax.axis_index("img") * height + lax.axis_index("row")
    top = devices.bit_length() - 2
    exchanges = [Exchange([0], True, flat, devices), Exchange([top, 1], True, flat, devices)]
    exchanges += [Exchange([bit], False, flat, devices) for bit in range(2, top)]
    core = exchanges[0].place
    rows_gains = [weights[i].reshape(1, width) for i in (0, 5)]
    column_gains = [weights[i].reshape(1, width) for i in (8, 13)]
    matrices = [w for w in weights if w.ndim == 2]
    hidden_width = matrices[4].shape[1]
    owned = images * groups // height

    def to_columns(array):
        array = array.reshape(height, owned, rows * GROUP, width)
        return lax.all_to_all(array, "row", 0, 0, tiled=True)

    def to_rows(array):
        array = lax.all_to_all(array, "row", 0, 0, tiled=True)
        return array.reshape(images, groups, rows * GROUP, width)

    def gather_rows(array):
        array = array.reshape(rows, images, groups, GROUP, width)
        return array.transpose(1, 2, 0, 3, 4)

    squares = ("square",) * 4
    total = grad_rows(width, hidden_width)
    steps = 2 if images % 2 == 0 and owned % 2 == 0 else 1
    up = to_columns(gather_rows(cotangent))
    sent, query, key, value, attended, middle, probs = rows_forward(inputs, rows_gains, matrices[:6])
    sent, up = lax.optimization_barrier((sent, up))
    stream = to_columns(sent)
    final, between_grad, keep, send = columns_both(core, stream, up, column_gains, matrices[6:], steps)
    kinds = (0, *squares, 1, "columns", "rows")
    columns = Chain(exchanges, ((total, kinds),), keep, send, hidden_width)
    token = columns.cut(columns.token)
    token = columns.add(token)
    between_grad = to_rows(between_grad)
    between_grad, final, token = lax.optimization_barrier((between_grad, final, token))
    final = to_rows(final)
    wq, wk, wv, wo, w1, w2 = matrices[:6]
    kept = (middle, w1, w2, attended, wo, query, key, value, probs, inputs, wq, wk, wv)
    stream_grad, keep, send = rows_backward(core, between_grad, rows_gains, kept, steps, token)
    rows_chain = Chain(exchanges, ((total, kinds),), keep, send, hidden_width)
    token = rows_chain.token
    if PLACE == 0:
        token = final = unpack(final, inputs.shape, token)
    while len(columns.others):
        token = columns.add(token)
    token = rows_chain.cut(token)
    if PLACE == 1:
        token = final = unpack(final, inputs.shape, token)
    token = rows_chain.add(token)
    token = columns.last(token)
    columns.spread()
    while rows_chain.others:
        token = rows_chain.add(token)
    token = rows_chain.last(token)
    token = columns.join(token)
    rows_chain.spread()
    token = columns.finish(token)
    token = rows_chain.join(token)
    rows_chain.finish(token)
    c_gain, c_query, c_keys, c_values, c_mixer, c_scale, c_expand, c_shrink = columns.results
    r_gain, r_query, r_keys, r_values, r_mixer, r_scale, r_expand, r_shrink = rows_chain.results
    return (
        final, stream_grad,
        r_gain, r_query, r_keys, r_values, r_mixer, r_scale, r_expand, r_shrink,
        c_gain, c_query, c_keys, c_values, c_mixer, c_scale, c_expand, c_shrink,
    )


def solution(mesh):
    moved = P("row", "img", None, None)
    return jax.shard_map(
        on_device,
        mesh=mesh,
        in_specs=(moved, moved) + (P(),) * 16,
        out_specs=(moved, moved) + (P(),) * 16,
        check_vma=False,
    )
```

time: 257 us -> 175 us (0.68)
  Pallas kernels: 100 us -> 47.7 us
  local copies, waits for them, and re-layouts: 15.5 us -> 3.9 us
  starting transfers between devices: 57 us -> 45.7 us
  waiting for transfers between devices: 82.4 us -> 76.4 us
    pallas_call x15 -> x16, Pallas kernels: 100 us -> 47.7 us  [the longest x1 18.2 us: columns_both(): pl.pallas_call(columns_kernel, grid=(steps,), in_specs=[SCALAR, HELD, HEL...]
    ppermute x28 -> x20, waiting for transfers between devices: 27.7 us -> 47.1 us  [swap(): lax.ppermute(array, ALL, [(i, i ^ mask) for i in range(self.devices)])]
    all_to_all x2, waiting for transfers between devices: 18.2 us -> 0.01 us  [to_rows(): array = lax.all_to_all(array, 'row', 0, 0, tiled=True)]
    ppermute x28 -> x20, starting transfers between devices: 32.8 us -> 21.9 us  [swap(): lax.ppermute(array, ALL, [(i, i ^ mask) for i in range(self.devices)])]
    unnamed x70 -> x8, local copies, waits for them, and re-layouts: 12 us -> 1.83 us
    all_to_all x2, waiting for transfers between devices: 36.5 us -> 29.4 us  [to_columns(): return lax.all_to_all(array, 'row', 0, 0, tiled=True)]
  transfers between devices with their start and end apart: 32 -> 24, of which waited for: 12 -> 16; matrix products, arithmetic and copies ran while one was open for 1% -> 0% of each run, Pallas kernels for 19% -> 16%
where the time goes in v2:
time: 175 us
  waiting for transfers between devices  76.4 us (44%)
  Pallas kernels  47.7 us (27%)
  starting transfers between devices  45.7 us (26%)
  local copies, waits for them, and re-layouts  3.9 us (2%)
    ppermute x20, waiting for transfers between devices, swap(): lax.ppermute(array, ALL, [(i, i ^ mask) for i in range(self.devices)])  47.1 us
    all_to_all x2, waiting for transfers between devices, to_columns(): return lax.all_to_all(array, 'row', 0, 0, tiled=True)  29.4 us
    ppermute x20, starting transfers between devices, swap(): lax.ppermute(array, ALL, [(i, i ^ mask) for i in range(self.devices)])  21.9 us
    pallas_call x1, Pallas kernels, columns_both(): pl.pallas_call(columns_kernel, grid=(steps,), in_specs=[SCALAR, HELD, HEL...  18.2 us
    pallas_call x1, Pallas kernels, rows_backward(): pl.pallas_call(rows_backward_kernel, grid=(steps,), in_specs=[SCALAR] + [...  15.1 us
    all_to_all x2, starting transfers between devices, to_columns(): return lax.all_to_all(array, 'row', 0, 0, tiled=True)  12.9 us
    all_to_all x2, starting transfers between devices, to_rows(): array = lax.all_to_all(array, 'row', 0, 0, tiled=True)  11 us
    pallas_call x1, Pallas kernels, rows_forward(): pl.pallas_call(rows_forward_kernel, grid=(1,), in_specs=[whole(array) for...  8.04 us
  transfers between devices with their start and end apart: 24, of which 16 were waited for; matrix products, arithmetic and copies ran while one was open for 0% of the time, Pallas kernels for 16%

profile of v2, /device:TPU:0, one launch (start us, length us, event | category | flops | bytes accessed | tf_op | source)
XLA Modules:
  0.0 174.5 jit_solution(17693103514091138087)
XLA Ops:
  0.7 2.1 %copy.36 = bf16[2,8,12,8,256]{4,3,0,2,1:T(8,128)(2,1)} copy(bf16[2,8,12,8,256]{4,3,2,1,0:T(8,128)(2,1)} %bitcast.33) | data formatting | bytes 1572864 | tf_op jit(solution)/shard_map/reshape | solution.py:681
  2.7 7.4 %all-to-all-start = ((bf16[16,6,16,256]{3,2,1,0:T(8,128)(2,1)}), bf16[16,6,16,256]{3,2,1,0:T(8,128)(2,1)S(1)}, u32[]{:S(2)}, u32[]{:S(2)}) async-start(bf16[16,6,16,256]{3,2,1,0:T(8,128)(2,1)} %bitcast.5), calls=%async_computation | async-start | bytes 1572864 | tf_op jit(solution)/shard_map/all_to_all | solution.py:674
  10.1 8.0 %rows_forward.1 = (bf16[8,12,16,256]{3,2,1,0:T(8,128)(2,1)}, bf16[2,8,96,256]{3,2,1,0:T(8,128)(2,1)}, bf16[2,8,96,256]{3,2,1,0:T(8,128)(2,1)}, bf16[2,8,96,256]{...) custom-call(bf16[2,8,96,256]{3,2,1,0:T(8,128)(2,1)} %x_hbm.1, ...), custom_call_target="tpu_custom_call" | custom-call | flops 1 | bytes 1 | tf_op jit(solution)/shard_map/rows_forward/pallas_call | solution.py:399
  18.2 10.7 %all-to-all-done.up_ref = bf16[16,6,16,256]{3,2,1,0:T(8,128)(2,1)S(1)} async-done(((bf16[16,6,16,256]{3,2,1,0:T(8,128)(2,1)}), bf16[16,6,16,256]{3,2,1,0:T(8,128)(2,1)S(1)}, u32[]{:S(2)}, u32[]{:S(2)}) %all-to-all-start) | async-done | bytes 786464 | tf_op jit(solution)/shard_map/all_to_all | solution.py:674
  28.8 5.5 %all-to-all-start.1 = ((bf16[16,6,16,256]{3,2,1,0:T(8,128)(2,1)}), bf16[16,6,16,256]{3,2,1,0:T(8,128)(2,1)S(1)}, u32[]{:S(2)}, u32[]{:S(2)}) async-start(bf16[16,6,16,256]{3,2,1,0:T(8,128)(2,1)} %bitcast.6), calls=%async_computation.1 | async-start | bytes 1572864 | tf_op jit(solution)/shard_map/all_to_all | solution.py:674
  34.3 18.7 %all-to-all-done.1.x_ref = bf16[16,6,16,256]{3,2,1,0:T(8,128)(2,1)S(1)} async-done(((bf16[16,6,16,256]{3,2,1,0:T(8,128)(2,1)}), bf16[16,6,16,256]{3,2,1,0:T(8,128)(2,1)S(1)}, u32[]{:S(2)}, u32[]{:S(2)}) %all-to-all-start.1) | async-done | bytes 786464 | tf_op jit(solution)/shard_map/all_to_all | solution.py:674
  53.0 18.2 %columns_both.1 = (bf16[16,6,16,256]{3,2,1,0:T(8,128)(2,1)}, bf16[16,6,16,256]{3,2,1,0:T(8,128)(2,1)}, bf16[1552,256]{1,0:T(8,128)(2,1)S(1)}, bf16[1552,256]{1,0:T(8,128)(2,1)S(1)}) custom-call(s32[1]{0:T(128)} %bitcast.core_ref.at_ref, bf16[16,6,16,256]{3,2,1,0:T(8,128)(2,1)S(1)} %all-to-all-done.1.x_ref, bf16[16,6,16,256]{3,2,1,0:T(8,128)(2,1)S(1)} %all-to-all-done.up_ref, ...), custom_call_target="tpu_custom_call" | custom-call | flops 1 | bytes 1 | tf_op jit(solution)/shard_map/columns_both/pallas_call | solution.py:450
  71.2 5.5 %all-to-all-start.2 = ((bf16[16,6,16,256]{3,2,1,0:T(8,128)(2,1)}), bf16[16,6,16,256]{3,2,1,0:T(8,128)(2,1)S(1)}, u32[]{:S(2)}, u32[]{:S(2)}) async-start(bf16[16,6,16,256]{3,2,1,0:T(8,128)(2,1)} %get-tuple-element.68), calls=%async_computation.2 | async-start | bytes 1572864 | tf_op jit(solution)/shard_map/all_to_all | solution.py:677
  77.1 2.0 %collective-permute-done.refs_1_ = bf16[1552,256]{1,0:T(8,128)(2,1)S(1)} collective-permute-done((bf16[1552,256]{1,0:T(8,128)(2,1)S(1)}, bf16[1552,256]{1,0:T(8,128)(2,1)S(1)}, u32[]{:S(2)}, u32[]{:S(2)}) %collective-permute-start) | collective-permute-done | bytes 794656 | tf_op jit(solution)/shard_map/ppermute | solution.py:610
  81.1 1.9 %collective-permute-start.2 = (bf16[400,256]{1,0:T(8,128)(2,1)S(1)}, bf16[400,256]{1,0:T(8,128)(2,1)S(1)}, u32[]{:S(2)}, u32[]{:S(2)}) collective-permute-start(bf16[400,256]{1,0:T(8,128)(2,1)S(1)} %get-tuple-element.74), channel_id=1, source_target_pairs={{0,2},{1,3},{2,0},{3,1},{4,6},{5,7},{6,4},{7,5},{8,10},{9,11},{10,... | collective-permute-start | bytes 614408 | tf_op jit(solution)/shard_map/ppermute | solution.py:610
  83.1 4.4 %collective-permute-done.1.refs_1_ = bf16[400,256]{1,0:T(8,128)(2,1)S(1)} collective-permute-done((bf16[400,256]{1,0:T(8,128)(2,1)S(1)}, bf16[400,256]{1,0:T(8,128)(2,1)S(1)}, u32[]{:S(2)}, u32[]{:S(2)}) %collective-permute-start.1) | collective-permute-done | bytes 204832 | tf_op jit(solution)/shard_map/ppermute | solution.py:610
  87.5 9.7 %collective-permute-done.2.refs_2_ = bf16[400,256]{1,0:T(8,128)(2,1)S(1)} collective-permute-done((bf16[400,256]{1,0:T(8,128)(2,1)S(1)}, bf16[400,256]{1,0:T(8,128)(2,1)S(1)}, u32[]{:S(2)}, u32[]{:S(2)}) %collective-permute-start.2) | collective-permute-done | bytes 204832 | tf_op jit(solution)/shard_map/ppermute | solution.py:610
  97.3 5.5 %all-to-all-start.3 = ((bf16[16,6,16,256]{3,2,1,0:T(8,128)(2,1)}), bf16[16,6,16,256]{3,2,1,0:T(8,128)(2,1)S(1)}, u32[]{:S(2)}, u32[]{:S(2)}) async-start(bf16[16,6,16,256]{3,2,1,0:T(8,128)(2,1)} %get-tuple-element.76), calls=%async_computation.3 | async-start | bytes 1572864 | tf_op jit(solution)/shard_map/all_to_all | solution.py:677
  102.9 15.1 %rows_backward.1 = (f32[2,8,96,256]{3,2,1,0:T(8,128)}, bf16[1552,256]{1,0:T(8,128)(2,1)S(1)}, bf16[1552,256]{1,0:T(8,128)(2,1)S(1)}) custom-call(s32[1]{0:T(128)} %bitcast.core_ref.at_ref, bf16[8,12,16,256]{3,2,1,0:T(8,128)(2,1)S(1)} %bitcast.25, f32[1,256]{1,0:T(1,128)S(1)} %bitcast.28, f32[1,256]{1,0:T(1,128)S(1)} %bitcast.30, ...), custom_call_target="tpu_custom_call" | custom-call | flops 1 | bytes 1 | tf_op jit(solution)/shard_map/rows_backward/pallas_call | solution.py:416
  120.2 6.0 %collective-permute-done.5.refs_1_ = bf16[400,256]{1,0:T(8,128)(2,1)S(1)} collective-permute-done((bf16[400,256]{1,0:T(8,128)(2,1)S(1)}, bf16[400,256]{1,0:T(8,128)(2,1)S(1)}, u32[]{:S(2)}, u32[]{:S(2)}) %collective-permute-start.5) | collective-permute-done | bytes 204832 | tf_op jit(solution)/shard_map/ppermute | solution.py:610
  130.3 2.2 %collective-permute-start.10 = (bf16[400,256]{1,0:T(8,128)(2,1)S(1)}, bf16[400,256]{1,0:T(8,128)(2,1)S(1)}, u32[]{:S(2)}, u32[]{:S(2)}) collective-permute-start(bf16[400,256]{1,0:T(8,128)(2,1)S(1)} %sum_split.8.refs_2_.refs_0_), channel_id=1, source_target_pairs={{0,8},{1,9},{2,10},{3,11},{4,12},{5,13},{6,14},{7,15},{8,0},{9,1},... | collective-permute-start | bytes 614408 | tf_op jit(solution)/shard_map/ppermute | solution.py:610
  134.7 2.8 %collective-permute-done.7.refs_2_ = bf16[400,256]{1,0:T(8,128)(2,1)S(1)} collective-permute-done((bf16[400,256]{1,0:T(8,128)(2,1)S(1)}, bf16[400,256]{1,0:T(8,128)(2,1)S(1)}, u32[]{:S(2)}, u32[]{:S(2)}) %collective-permute-start.7) | collective-permute-done | bytes 204832 | tf_op jit(solution)/shard_map/ppermute | solution.py:610
  141.5 4.7 %collective-permute-done.9.refs_1_ = bf16[400,256]{1,0:T(8,128)(2,1)S(1)} collective-permute-done((bf16[400,256]{1,0:T(8,128)(2,1)S(1)}, bf16[400,256]{1,0:T(8,128)(2,1)S(1)}, u32[]{:S(2)}, u32[]{:S(2)}) %collective-permute-start.9) | collective-permute-done | bytes 204832 | tf_op jit(solution)/shard_map/ppermute | solution.py:610
  151.5 4.8 %collective-permute-done.11.refs_1_ = bf16[400,256]{1,0:T(8,128)(2,1)S(1)} collective-permute-done((bf16[400,256]{1,0:T(8,128)(2,1)S(1)}, bf16[400,256]{1,0:T(8,128)(2,1)S(1)}, u32[]{:S(2)}, u32[]{:S(2)}) %collective-permute-start.11) | collective-permute-done | bytes 204832 | tf_op jit(solution)/shard_map/ppermute | solution.py:610
  161.1 1.9 %finish.2 = (f32[1,256]{1,0:T(1,128)}, f32[256,256]{1,0:T(8,128)}, f32[256,256]{1,0:T(8,128)}, f32[256,256]{1,0:T(8,128)}, f32[256,256]{1,0:T(8,128)}, /*index=5...) custom-call(s32[1]{0:T(128)} %bitcast.core_ref.at_ref, bf16[1536,256]{1,0:T(8,128)(2,1)S(1)} %bitcast.20, ...), custom_call_target="tpu_custom_call" | custom-call | flops 1 | bytes 1 | tf_op jit(solution)/shard_map/finish/pallas_call | solution.py:581
  163.0 2.3 %collective-permute-done.12.refs_1_ = bf16[384,256]{1,0:T(8,128)(2,1)S(1)} collective-permute-done((bf16[384,256]{1,0:T(8,128)(2,1)S(1)}, bf16[384,256]{1,0:T(8,128)(2,1)S(1)}, u32[]{:S(2)}, u32[]{:S(2)}) %collective-permute-start.12) | collective-permute-done | bytes 196640 | tf_op jit(solution)/shard_map/ppermute | solution.py:610
  165.3 4.2 %collective-permute-done.13.refs_2_ = bf16[384,256]{1,0:T(8,128)(2,1)S(1)} collective-permute-done((bf16[384,256]{1,0:T(8,128)(2,1)S(1)}, bf16[384,256]{1,0:T(8,128)(2,1)S(1)}, u32[]{:S(2)}, u32[]{:S(2)}) %collective-permute-start.13) | collective-permute-done | bytes 196640 | tf_op jit(solution)/shard_map/ppermute | solution.py:610
  170.3 2.3 %collective-permute-done.19.other_ref = bf16[1536,256]{1,0:T(8,128)(2,1)S(1)} collective-permute-done((bf16[1536,256]{1,0:T(8,128)(2,1)S(1)}, bf16[1536,256]{1,0:T(8,128)(2,1)S(1)}, u32[]{:S(2)}, u32[]{:S(2)}) %collective-permute-start.19) | collective-permute-done | bytes 786464 | tf_op jit(solution)/shard_map/ppermute | solution.py:610
  172.6 1.9 %finish.3 = (f32[1,256]{1,0:T(1,128)}, f32[256,256]{1,0:T(8,128)}, f32[256,256]{1,0:T(8,128)}, f32[256,256]{1,0:T(8,128)}, f32[256,256]{1,0:T(8,128)}, /*index=5...) custom-call(s32[1]{0:T(128)} %bitcast.core_ref.at_ref, bf16[1536,256]{1,0:T(8,128)(2,1)S(1)} %bitcast.23, ...), custom_call_target="tpu_custom_call" | custom-call | flops 1 | bytes 1 | tf_op jit(solution)/shard_map/finish/pallas_call | solution.py:581
  (49 shorter events, 26.0 us)
Async XLA Ops:
  2.7 26.1 %all-to-all-start = ((bf16[16,6,16,256]{3,2,1,0:T(8,128)(2,1)}), bf16[16,6,16,256]{3,2,1,0:T(8,128)(2,1)S(1)}, u32[]{:S(2)}, u32[]{:S(2)}) async-start(bf16[16,6,16,256]{3,2,1,0:T(8,128)(2,1)} %bitcast.5), calls=%async_computation | async-start | bytes 1572864 | tf_op jit(solution)/shard_map/all_to_all | solution.py:674
  28.8 24.2 %all-to-all-start.1 = ((bf16[16,6,16,256]{3,2,1,0:T(8,128)(2,1)}), bf16[16,6,16,256]{3,2,1,0:T(8,128)(2,1)S(1)}, u32[]{:S(2)}, u32[]{:S(2)}) async-start(bf16[16,6,16,256]{3,2,1,0:T(8,128)(2,1)} %bitcast.6), calls=%async_computation.1 | async-start | bytes 1572864 | tf_op jit(solution)/shard_map/all_to_all | solution.py:674
  71.2 26.1 %all-to-all-start.2 = ((bf16[16,6,16,256]{3,2,1,0:T(8,128)(2,1)}), bf16[16,6,16,256]{3,2,1,0:T(8,128)(2,1)S(1)}, u32[]{:S(2)}, u32[]{:S(2)}) async-start(bf16[16,6,16,256]{3,2,1,0:T(8,128)(2,1)} %get-tuple-element.68), calls=%async_computation.2 | async-start | bytes 1572864 | tf_op jit(solution)/shard_map/all_to_all | solution.py:677
  76.7 2.4 %collective-permute-start = (bf16[1552,256]{1,0:T(8,128)(2,1)S(1)}, bf16[1552,256]{1,0:T(8,128)(2,1)S(1)}, u32[]{:S(2)}, u32[]{:S(2)}) collective-permute-start(bf16[1552,256]{1,0:T(8,128)(2,1)S(1)} %get-tuple-element.71), channel_id=1, source_target_pairs={{0,1},{1,0},{2,3},{3,2},{4,5},{5,4},{6,7},{7,6},{8,9},{9,8},{10,11... | collective-permute-start | bytes 2383880 | tf_op jit(solution)/shard_map/ppermute | solution.py:610
  79.6 8.0 %collective-permute-start.1 = (bf16[400,256]{1,0:T(8,128)(2,1)S(1)}, bf16[400,256]{1,0:T(8,128)(2,1)S(1)}, u32[]{:S(2)}, u32[]{:S(2)}) collective-permute-start(bf16[400,256]{1,0:T(8,128)(2,1)S(1)} %get-tuple-element.73), channel_id=1, source_target_pairs={{0,16},{1,17},{2,18},{3,19},{4,20},{5,21},{6,22},{7,23},{8,24},{9,... | collective-permute-start | bytes 614408 | tf_op jit(solution)/shard_map/ppermute | solution.py:610
  81.1 16.1 %collective-permute-start.2 = (bf16[400,256]{1,0:T(8,128)(2,1)S(1)}, bf16[400,256]{1,0:T(8,128)(2,1)S(1)}, u32[]{:S(2)}, u32[]{:S(2)}) collective-permute-start(bf16[400,256]{1,0:T(8,128)(2,1)S(1)} %get-tuple-element.74), channel_id=1, source_target_pairs={{0,2},{1,3},{2,0},{3,1},{4,6},{5,7},{6,4},{7,5},{8,10},{9,11},{10,... | collective-permute-start | bytes 614408 | tf_op jit(solution)/shard_map/ppermute | solution.py:610
  83.0 14.2 %collective-permute-start.3 = (bf16[400,256]{1,0:T(8,128)(2,1)S(1)}, bf16[400,256]{1,0:T(8,128)(2,1)S(1)}, u32[]{:S(2)}, u32[]{:S(2)}) collective-permute-start(bf16[400,256]{1,0:T(8,128)(2,1)S(1)} %get-tuple-element.75), channel_id=1, source_target_pairs={{0,18},{1,19},{2,16},{3,17},{4,22},{5,23},{6,20},{7,21},{8,26},{9,... | collective-permute-start | bytes 614408 | tf_op jit(solution)/shard_map/ppermute | solution.py:610
  97.3 35.2 %all-to-all-start.3 = ((bf16[16,6,16,256]{3,2,1,0:T(8,128)(2,1)}), bf16[16,6,16,256]{3,2,1,0:T(8,128)(2,1)S(1)}, u32[]{:S(2)}, u32[]{:S(2)}) async-start(bf16[16,6,16,256]{3,2,1,0:T(8,128)(2,1)} %get-tuple-element.76), calls=%async_computation.3 | async-start | bytes 1572864 | tf_op jit(solution)/shard_map/all_to_all | solution.py:677
  118.0 8.2 %collective-permute-start.4 = (bf16[1552,256]{1,0:T(8,128)(2,1)S(1)}, bf16[1552,256]{1,0:T(8,128)(2,1)S(1)}, u32[]{:S(2)}, u32[]{:S(2)}) collective-permute-start(bf16[1552,256]{1,0:T(8,128)(2,1)S(1)} %get-tuple-element.86), channel_id=1, source_target_pairs={{0,1},{1,0},{2,3},{3,2},{4,5},{5,4},{6,7},{7,6},{8,9},{9,8},{10,11... | collective-permute-start | bytes 2383880 | tf_op jit(solution)/shard_map/ppermute | solution.py:610
  118.5 7.7 %collective-permute-start.5 = (bf16[400,256]{1,0:T(8,128)(2,1)S(1)}, bf16[400,256]{1,0:T(8,128)(2,1)S(1)}, u32[]{:S(2)}, u32[]{:S(2)}) collective-permute-start(bf16[400,256]{1,0:T(8,128)(2,1)S(1)} %sum_split.7._.refs_0_), channel_id=1, source_target_pairs={{0,4},{1,5},{2,6},{3,7},{4,0},{5,1},{6,2},{7,3},{8,12},{9,13},{10,... | collective-permute-start | bytes 614408 | tf_op jit(solution)/shard_map/ppermute | solution.py:610
  126.7 8.0 %collective-permute-start.6 = (bf16[400,256]{1,0:T(8,128)(2,1)S(1)}, bf16[400,256]{1,0:T(8,128)(2,1)S(1)}, u32[]{:S(2)}, u32[]{:S(2)}) collective-permute-start(bf16[400,256]{1,0:T(8,128)(2,1)S(1)} %get-tuple-element.89), channel_id=1, source_target_pairs={{0,16},{1,17},{2,18},{3,19},{4,20},{5,21},{6,22},{7,23},{8,24},{9,... | collective-permute-start | bytes 614408 | tf_op jit(solution)/shard_map/ppermute | solution.py:610
  127.5 10.0 %collective-permute-start.7 = (bf16[400,256]{1,0:T(8,128)(2,1)S(1)}, bf16[400,256]{1,0:T(8,128)(2,1)S(1)}, u32[]{:S(2)}, u32[]{:S(2)}) collective-permute-start(bf16[400,256]{1,0:T(8,128)(2,1)S(1)} %get-tuple-element.90), channel_id=1, source_target_pairs={{0,2},{1,3},{2,0},{3,1},{4,6},{5,7},{6,4},{7,5},{8,10},{9,11},{10,... | collective-permute-start | bytes 614408 | tf_op jit(solution)/shard_map/ppermute | solution.py:610
  129.1 9.9 %collective-permute-start.8 = (bf16[400,256]{1,0:T(8,128)(2,1)S(1)}, bf16[400,256]{1,0:T(8,128)(2,1)S(1)}, u32[]{:S(2)}, u32[]{:S(2)}) collective-permute-start(bf16[400,256]{1,0:T(8,128)(2,1)S(1)} %get-tuple-element.91), channel_id=1, source_target_pairs={{0,18},{1,19},{2,16},{3,17},{4,22},{5,23},{6,20},{7,21},{8,26},{9,... | collective-permute-start | bytes 614408 | tf_op jit(solution)/shard_map/ppermute | solution.py:610
  130.3 11.2 %collective-permute-start.10 = (bf16[400,256]{1,0:T(8,128)(2,1)S(1)}, bf16[400,256]{1,0:T(8,128)(2,1)S(1)}, u32[]{:S(2)}, u32[]{:S(2)}) collective-permute-start(bf16[400,256]{1,0:T(8,128)(2,1)S(1)} %sum_split.8.refs_2_.refs_0_), channel_id=1, source_target_pairs={{0,8},{1,9},{2,10},{3,11},{4,12},{5,13},{6,14},{7,15},{8,0},{9,1},... | collective-permute-start | bytes 614408 | tf_op jit(solution)/shard_map/ppermute | solution.py:610
  140.2 6.0 %collective-permute-start.9 = (bf16[400,256]{1,0:T(8,128)(2,1)S(1)}, bf16[400,256]{1,0:T(8,128)(2,1)S(1)}, u32[]{:S(2)}, u32[]{:S(2)}) collective-permute-start(bf16[400,256]{1,0:T(8,128)(2,1)S(1)} %sum_split.10.refs_2_.refs_0_), channel_id=1, source_target_pairs={{0,4},{1,5},{2,6},{3,7},{4,0},{5,1},{6,2},{7,3},{8,12},{9,13},{10,... | collective-permute-start | bytes 614408 | tf_op jit(solution)/shard_map/ppermute | solution.py:610
  146.3 10.1 %collective-permute-start.11 = (bf16[400,256]{1,0:T(8,128)(2,1)S(1)}, bf16[400,256]{1,0:T(8,128)(2,1)S(1)}, u32[]{:S(2)}, u32[]{:S(2)}) collective-permute-start(bf16[400,256]{1,0:T(8,128)(2,1)S(1)} %sum_split.11.refs_0_.refs_2_), channel_id=1, source_target_pairs={{0,8},{1,9},{2,10},{3,11},{4,12},{5,13},{6,14},{7,15},{8,0},{9,1},... | collective-permute-start | bytes 614408 | tf_op jit(solution)/shard_map/ppermute | solution.py:610
  148.0 8.4 %collective-permute-start.15 = (bf16[384,256]{1,0:T(8,128)(2,1)S(1)}, bf16[384,256]{1,0:T(8,128)(2,1)S(1)}, u32[]{:S(2)}, u32[]{:S(2)}) collective-permute-start(bf16[384,256]{1,0:T(8,128)(2,1)S(1)} %get-tuple-element.92.refs_2_.refs_0_), channel_id=1, source_target_pairs={{0,16},{1,17},{2,18},{3,19},{4,20},{5,21},{6,22},{7,23},{8,24},{9,... | collective-permute-start | bytes 589832 | tf_op jit(solution)/shard_map/ppermute | solution.py:610
  148.9 8.4 %collective-permute-start.16 = (bf16[384,256]{1,0:T(8,128)(2,1)S(1)}, bf16[384,256]{1,0:T(8,128)(2,1)S(1)}, u32[]{:S(2)}, u32[]{:S(2)}) collective-permute-start(bf16[384,256]{1,0:T(8,128)(2,1)S(1)} %get-tuple-element.92.refs_2_.refs_0_), channel_id=1, source_target_pairs={{0,2},{1,3},{2,0},{3,1},{4,6},{5,7},{6,4},{7,5},{8,10},{9,11},{10,... | collective-permute-start | bytes 589832 | tf_op jit(solution)/shard_map/ppermute | solution.py:610
  150.3 7.0 %collective-permute-start.17 = (bf16[384,256]{1,0:T(8,128)(2,1)S(1)}, bf16[384,256]{1,0:T(8,128)(2,1)S(1)}, u32[]{:S(2)}, u32[]{:S(2)}) collective-permute-start(bf16[384,256]{1,0:T(8,128)(2,1)S(1)} %get-tuple-element.92.refs_2_.refs_0_), channel_id=1, source_target_pairs={{0,18},{1,19},{2,16},{3,17},{4,22},{5,23},{6,20},{7,21},{8,26},{9,... | collective-permute-start | bytes 589832 | tf_op jit(solution)/shard_map/ppermute | solution.py:610
  157.4 3.6 %collective-permute-start.18 = (bf16[1536,256]{1,0:T(8,128)(2,1)S(1)}, bf16[1536,256]{1,0:T(8,128)(2,1)S(1)}, u32[]{:S(2)}, u32[]{:S(2)}) collective-permute-start(bf16[1536,256]{1,0:T(8,128)(2,1)S(1)} %bitcast.19), channel_id=1, source_target_pairs={{0,1},{1,0},{2,3},{3,2},{4,5},{5,4},{6,7},{7,6},{8,9},{9,8},{10,11... | collective-permute-start | bytes 2359304 | tf_op jit(solution)/shard_map/ppermute | solution.py:610
  157.5 7.8 %collective-permute-start.12 = (bf16[384,256]{1,0:T(8,128)(2,1)S(1)}, bf16[384,256]{1,0:T(8,128)(2,1)S(1)}, u32[]{:S(2)}, u32[]{:S(2)}) collective-permute-start(bf16[384,256]{1,0:T(8,128)(2,1)S(1)} %get-tuple-element.93.refs_4_.refs_0_), channel_id=1, source_target_pairs={{0,16},{1,17},{2,18},{3,19},{4,20},{5,21},{6,22},{7,23},{8,24},{9,... | collective-permute-start | bytes 589832 | tf_op jit(solution)/shard_map/ppermute | solution.py:610
  158.3 11.2 %collective-permute-start.13 = (bf16[384,256]{1,0:T(8,128)(2,1)S(1)}, bf16[384,256]{1,0:T(8,128)(2,1)S(1)}, u32[]{:S(2)}, u32[]{:S(2)}) collective-permute-start(bf16[384,256]{1,0:T(8,128)(2,1)S(1)} %get-tuple-element.93.refs_4_.refs_0_), channel_id=1, source_target_pairs={{0,2},{1,3},{2,0},{3,1},{4,6},{5,7},{6,4},{7,5},{8,10},{9,11},{10,... | collective-permute-start | bytes 589832 | tf_op jit(solution)/shard_map/ppermute | solution.py:610
  159.7 9.8 %collective-permute-start.14 = (bf16[384,256]{1,0:T(8,128)(2,1)S(1)}, bf16[384,256]{1,0:T(8,128)(2,1)S(1)}, u32[]{:S(2)}, u32[]{:S(2)}) collective-permute-start(bf16[384,256]{1,0:T(8,128)(2,1)S(1)} %get-tuple-element.93.refs_4_.refs_0_), channel_id=1, source_target_pairs={{0,18},{1,19},{2,16},{3,17},{4,22},{5,23},{6,20},{7,21},{8,26},{9,... | collective-permute-start | bytes 589832 | tf_op jit(solution)/shard_map/ppermute | solution.py:610
  170.3 2.4 %collective-permute-start.19 = (bf16[1536,256]{1,0:T(8,128)(2,1)S(1)}, bf16[1536,256]{1,0:T(8,128)(2,1)S(1)}, u32[]{:S(2)}, u32[]{:S(2)}) collective-permute-start(bf16[1536,256]{1,0:T(8,128)(2,1)S(1)} %bitcast.22), channel_id=1, source_target_pairs={{0,1},{1,0},{2,3},{3,2},{4,5},{5,4},{6,7},{7,6},{8,9},{9,8},{10,11... | collective-permute-start | bytes 2359304 | tf_op jit(solution)/shard_map/ppermute | solution.py:610
  (4 other events, 48.5 us)

commit v3 on v2

--- a/solution.py
+++ b/solution.py
@@ -16,8 +16,6 @@
 VMEM_LIMIT = 24 * 1024 * 1024
 SMALL_LIMIT = 12 * 1024 * 1024
 ALL = ("img", "row")
-HEAVY = 1 << 25
-PLACE = 1
 F32 = jnp.float32
 BF16 = jnp.bfloat16
 
@@ -52,11 +50,6 @@
 
 ROOT = math.sqrt(2.0 / math.pi)
 CUBE = 0.044715
-
-
-def gelu(value):
-    bent = jnp.tanh(ROOT * (value + CUBE * (value * value * value)))
-    return 0.5 * value * (1.0 + bent)
 
 
 def gelu_both(value):
@@ -104,7 +97,7 @@
     return tuple(merge_heads(grads) for grads in (query_grads, key_grads, value_grads))
 
 
-def feed_back(normed, up_low, expand_ref, shrink_ref, acc, first, forward):
+def feed_back(normed, up_low, expand_ref, shrink_ref, put, first, forward):
     width = normed.shape[-1]
     hidden_width = expand_ref.shape[1]
     tile = min(HIDDEN_TILE, hidden_width)
@@ -120,20 +113,17 @@
             part = mm(hidden, shrink)
             result = part if result is None else result + part
         expanded_grad = (slope * mm_right_t(up_low, shrink)).astype(BF16)
-        at = first + j * width
-        acc[at : at + width, :] += mm_left_t(normed, expanded_grad)
-        at = first + hidden_width // tile * width + j * width
-        acc[at : at + width, :] += mm_left_t(up_low, hidden)
+        put(first + j, mm_left_t(normed, expanded_grad))
+        put(first + hidden_width // tile + j, mm_left_t(up_low, hidden))
         part = mm_right_t(expanded_grad, expand)
         normed_grad = part if normed_grad is None else normed_grad + part
     return result, normed_grad
 
 
-def project_back(normed_low, grads, weight_refs, acc):
-    width = normed_low.shape[-1]
+def project_back(normed_low, grads, weight_refs, put):
     total = None
     for i, (grad, weight_ref) in enumerate(zip(grads, weight_refs)):
-        acc[i * width : (i + 1) * width, :] += mm_left_t(normed_low, grad)
+        put(i, mm_left_t(normed_low, grad))
         part = mm_right_t(grad, weight_ref[...])
         total = part if total is None else total + part
     return total
@@ -145,22 +135,30 @@
     ref[at + 8 : at + 16, :] = (gains - high.astype(F32)).astype(BF16)
 
 
-def emit_grads(core, acc, gains, keep_ref, send_ref):
-    half = acc.shape[0] // 2
-    for which, (mine, other) in enumerate(((keep_ref, send_ref), (send_ref, keep_ref))):
-
-        @pl.when(core == which)
-        def _():
-            mine[0:half, :] = acc[0:half, :].astype(BF16)
-            other[0:half, :] = acc[half:, :].astype(BF16)
-
-    store_tail(keep_ref, half, gains)
-    store_tail(send_ref, half, gains)
+def putter(core, halves):
+    width = halves.shape[2]
+    blocks = halves.shape[1] // width
+
+    def put(block, value):
+        half, row = divmod(block, blocks)
+        halves[half ^ core, row * width : (row + 1) * width, :] = value.astype(BF16)
+
+    return put
+
+
+def emit_grads(halves, gains, keep_ref, send_ref):
+    for i, ref in enumerate((keep_ref, send_ref)):
+        ref[0 : halves.shape[1], :] = halves[i]
+        store_tail(ref, halves.shape[1], gains)
+
+
+def stack_gains(gain, scale):
+    return jnp.concatenate([gain, scale, jnp.zeros((6, gain.shape[1]), F32)], axis=0)
 
 
 def rows_forward_kernel(
     x_ref, ga_ref, wq_ref, wk_ref, wv_ref, wo_ref, gb_ref, w1_ref, w2_ref,
-    send_ref, q_ref, k_ref, v_ref, att_ref, mid_ref, p_ref,
+    send_ref, q_ref, k_ref, v_ref, att_ref, mid_ref, p_ref, hidden_ref, slope_ref,
 ):
     rows, images, cols, width = x_ref.shape
     tokens = rows * images * cols
@@ -191,150 +189,172 @@
     result = middle
     for j in range(hidden_width // tile):
         cut = slice(j * tile, (j + 1) * tile)
-        hidden = gelu(mm(normed_b, w1_ref[:, cut])).astype(BF16)
+        hidden, slope = gelu_both(mm(normed_b, w1_ref[:, cut]))
+        hidden = hidden.astype(BF16)
+        hidden_ref[j] = hidden
+        slope_ref[j] = slope
         result = result + mm(hidden, w2_ref[cut, :])
-    result = result.reshape(rows, images * cols // GROUP, GROUP, width)
-    result = jnp.concatenate([result[r] for r in range(rows)], axis=1)
-    send_ref[...] = result.astype(BF16).reshape(send_ref.shape)
+    result = result.astype(BF16).reshape(rows, images, cols, width)
+    part = send_ref.shape[2]
+    for i in range(send_ref.shape[0]):
+        image, first = divmod(i * part, cols)
+        send_ref[i] = result[:, image, first : first + part]
 
 
 def rows_backward_kernel(
-    core_ref, up_ref, ga_ref, gb_ref, mid_hbm, w1_hbm, w2_hbm, att_hbm, wo_hbm,
+    core_ref, up_ref, ga_ref, gb_ref, w2_hbm, slope_hbm, mid_hbm, w1_hbm, hidden_hbm, att_hbm, wo_hbm,
     q_hbm, k_hbm, v_hbm, p_hbm, x_hbm, wq_hbm, wk_hbm, wv_hbm, _,
-    grad_ref, keep_ref, send_ref,
-    acc, gains, mid_ref, w1_ref, w2_ref, att_ref, wo_ref, q_ref, k_ref, v_ref, p_ref, x_ref, wq_ref, wk_ref, wv_ref, done,
+    mid_grad_ref, dq_ref, dk_ref, dv_ref, keep_ref, send_ref,
+    halves, w2_ref, slope_ref, mid_ref, w1_ref, hidden_ref, att_ref, wo_ref,
+    q_ref, k_ref, v_ref, p_ref, x_ref, wq_ref, wk_ref, wv_ref, done,
 ):
-    rows, all_images, cols, width = x_ref.shape
-    step = pl.program_id(0)
-    images = all_images // pl.num_programs(0)
+    rows, images, cols, width = x_ref.shape
     tokens = rows * images * cols
-    here = pl.ds(step * images, images)
     features = width // HEADS
     scaling = 1.0 / math.sqrt(features)
-    sources = (mid_hbm, w1_hbm, w2_hbm, att_hbm, wo_hbm, q_hbm, k_hbm, v_hbm, p_hbm, x_hbm, wq_hbm, wk_hbm, wv_hbm)
-    targets = (mid_ref, w1_ref, w2_ref, att_ref, wo_ref, q_ref, k_ref, v_ref, p_ref, x_ref, wq_ref, wk_ref, wv_ref)
+    sources = (
+        w2_hbm, slope_hbm, mid_hbm, w1_hbm, hidden_hbm, att_hbm, wo_hbm,
+        q_hbm, k_hbm, v_hbm, p_hbm, x_hbm, wq_hbm, wk_hbm, wv_hbm,
+    )
+    targets = (
+        w2_ref, slope_ref, mid_ref, w1_ref, hidden_ref, att_ref, wo_ref,
+        q_ref, k_ref, v_ref, p_ref, x_ref, wq_ref, wk_ref, wv_ref,
+    )
     copies = [pltpu.make_async_copy(sources[i], targets[i], done.at[i]) for i in range(len(sources))]
-
-    def wait(first, last):
-        @pl.when(step == 0)
-        def _():
-            for copy in copies[first:last]:
-                copy.wait()
-
-    @pl.when(step == 0)
-    def _():
-        for copy in copies:
-            copy.start()
-        acc[...] = jnp.zeros_like(acc)
-        gains[...] = jnp.zeros_like(gains)
-
-    wait(0, 3)
-    up = up_ref[here].astype(F32).reshape(images * cols // GROUP, rows * GROUP, width)
-    up = jnp.concatenate(
-        [up[:, r * GROUP : (r + 1) * GROUP].reshape(images * cols, width) for r in range(rows)], axis=0
-    )
+    for copy in copies:
+        copy.start()
+    put = putter(core_ref[0], halves)
+    up = jnp.concatenate([up_ref[:, r].reshape(images * cols, width) for r in range(rows)], axis=0).astype(F32)
     up_low = up.astype(BF16)
-    normal_b, inverse_b = normalize(mid_ref[:, here].reshape(tokens, width))
+    tiles, _, tile = slope_ref.shape
+    copies[0].wait()
+    hidden_grads = [mm_right_t(up_low, w2_ref[j * tile : (j + 1) * tile, :]) for j in range(tiles)]
+    for copy in copies[1:5]:
+        copy.wait()
+    normal_b, inverse_b = normalize(mid_ref[...].reshape(tokens, width))
     normed_b = (normal_b * gb_ref[...]).astype(BF16)
-    _, normed_grad = feed_back(normed_b, up_low, w1_ref, w2_ref, acc, 4 * width, False)
+    normed_grad = None
+    for j in range(tiles):
+        expanded_grad = (slope_ref[j] * hidden_grads[j]).astype(BF16)
+        put(4 + j, mm_left_t(normed_b, expanded_grad))
+        put(4 + tiles + j, mm_left_t(up_low, hidden_ref[j]))
+        part = mm_right_t(expanded_grad, w1_ref[:, j * tile : (j + 1) * tile])
+        normed_grad = part if normed_grad is None else normed_grad + part
     middle_norm, scale_grad = normalize_back(normed_grad, normal_b, inverse_b, gb_ref[...])
-    gains[1:2, :] += scale_grad
     middle_grad = up + middle_norm
+    mid_grad_ref[...] = middle_grad
     middle_low = middle_grad.astype(BF16)
-    wait(3, len(sources))
-    acc[3 * width : 4 * width, :] += mm_left_t(att_ref[:, here].reshape(tokens, width), middle_low)
+    for copy in copies[5:]:
+        copy.wait()
+    put(3, mm_left_t(att_ref[...].reshape(tokens, width), middle_low))
     up_att = mm_right_t(middle_low, wo_ref[...]).astype(BF16)
-    query = q_ref[:, here].reshape(tokens, width)
-    key = k_ref[:, here].reshape(tokens, width)
-    value = v_ref[:, here].reshape(tokens, width)
+    query = q_ref[...].reshape(tokens, width)
+    key = k_ref[...].reshape(tokens, width)
+    value = v_ref[...].reshape(tokens, width)
     places = head_places(rows * images, cols, features)
-    probs = [p_ref[r, step * images + i, m] for r in range(rows) for i in range(images) for m in range(HEADS)]
+    probs = [p_ref[r, i, m] for r in range(rows) for i in range(images) for m in range(HEADS)]
     grads = attend_back(up_att, query, key, value, probs, places, scaling)
-    normal_a, inverse_a = normalize(x_ref[:, here].astype(F32).reshape(tokens, width))
-    normed_a = (normal_a * ga_ref[...]).astype(BF16)
-    normed_grad = project_back(normed_a, grads, (wq_ref, wk_ref, wv_ref), acc)
-    stream_norm, gain_grad = normalize_back(normed_grad, normal_a, inverse_a, ga_ref[...])
-    gains[0:1, :] += gain_grad
-    grad_ref[...] = (middle_grad + stream_norm).reshape(grad_ref.shape)
-
-    @pl.when(step == pl.num_programs(0) - 1)
-    def _():
-        emit_grads(core_ref[0], acc, gains[...], keep_ref, send_ref)
-
-
-def unpack_kernel(in_ref, _, out_ref):
-    rows, images, cols, width = out_ref.shape
-    array = in_ref[...].astype(F32).reshape(images * cols // GROUP, rows * GROUP, width)
-    for r in range(rows):
-        part = array[:, r * GROUP : (r + 1) * GROUP].reshape(images, cols, width)
-        out_ref[r] = part.astype(BF16)
-
-
-def load_groups(ref, first, groups):
-    sources, _, height, width = ref.shape
-    parts = [ref[:, first + i].astype(F32).reshape(sources * height, width) for i in range(groups)]
+    normed_a = (normalize(x_ref[...].astype(F32).reshape(tokens, width))[0] * ga_ref[...]).astype(BF16)
+    shared = None
+    for i, (grad, target, weight_ref) in enumerate(zip(grads, (dq_ref, dk_ref, dv_ref), (wq_ref, wk_ref, wv_ref))):
+        target[...] = grad
+        weight_grad = mm_left_t(normed_a, grad)
+        put(i, weight_grad)
+        part = weight_grad * weight_ref[...].astype(F32)
+        shared = part if shared is None else shared + part
+    gain_grad = jnp.sum(shared.T, axis=0, keepdims=True) / ga_ref[...]
+    emit_grads(halves, stack_gains(gain_grad, scale_grad), keep_ref, send_ref)
+
+
+def rows_rest_kernel(mid_grad_ref, dq_ref, dk_ref, dv_ref, x_ref, ga_ref, wq_ref, wk_ref, wv_ref, _, grad_ref, token_ref):
+    rows, images, cols, width = x_ref.shape
+    normal, inverse = normalize(x_ref[...].astype(F32).reshape(rows * images * cols, width))
+    normed_grad = None
+    for grad_ref_in, weight_ref in zip((dq_ref, dk_ref, dv_ref), (wq_ref, wk_ref, wv_ref)):
+        part = mm_right_t(grad_ref_in[...], weight_ref[...])
+        normed_grad = part if normed_grad is None else normed_grad + part
+    stream_norm, _ = normalize_back(normed_grad, normal, inverse, ga_ref[...])
+    grad_ref[...] = (mid_grad_ref[...] + stream_norm).reshape(grad_ref.shape)
+    token_ref[...] = jnp.zeros_like(token_ref)
+
+
+def unpack_kernel(in_ref, _, out_ref, token_ref, done):
+    part, cols = in_ref.shape[2], out_ref.shape[2]
+    copies = []
+    for i in range(in_ref.shape[0]):
+        image, first = divmod(i * part, cols)
+        target = out_ref.at[:, image, pl.ds(first, part)]
+        copies.append(pltpu.make_async_copy(in_ref.at[i], target, done.at[i]))
+    for copy in copies:
+        copy.start()
+    token_ref[...] = jnp.zeros_like(token_ref)
+    for copy in copies:
+        copy.wait()
+
+
+def load_groups(ref):
+    array = ref[...].astype(F32)
+    width = array.shape[-1]
+    parts = [array[:, :, i : i + GROUP].reshape(-1, width) for i in range(0, array.shape[2], GROUP)]
     return jnp.concatenate(parts, axis=0)
 
 
-def store_groups(ref, first, groups, value):
-    sources, _, height, width = ref.shape
-    tokens = sources * height
-    for i in range(groups):
-        part = value[i * tokens : (i + 1) * tokens].reshape(sources, height, width)
-        ref[:, first + i] = part.astype(ref.dtype)
+def store_groups(ref, value):
+    sources, rows, cols, width = ref.shape
+    groups = cols // GROUP
+    tokens = sources * rows * GROUP
+    parts = [value[i * tokens : (i + 1) * tokens].reshape(sources, rows, GROUP, width) for i in range(groups)]
+    ref[...] = jnp.concatenate(parts, axis=2).astype(ref.dtype)
 
 
 def columns_kernel(
-    core_ref, x_ref, up_ref, ga_ref, wq_ref, wk_ref, wv_ref, wo_ref, gb_ref, w1_ref, w2_ref,
-    out_ref, grad_ref, keep_ref, send_ref, acc, gains, bias,
+    core_ref, x_ref, up_ref, ga_ref, gb_ref, wq_hbm, wk_hbm, wv_hbm, wo_hbm, w1_hbm, w2_hbm,
+    out_ref, grad_ref, keep_ref, send_ref,
+    halves, bias, wq_ref, wk_ref, wv_ref, wo_ref, w1_ref, w2_ref, done,
 ):
-    width = x_ref.shape[-1]
-    groups = x_ref.shape[1] // pl.num_programs(0)
-    tokens = x_ref.shape[0] * x_ref.shape[2]
+    sources, rows, cols, width = x_ref.shape
+    groups = cols // GROUP
+    tokens = sources * rows * GROUP
     features = width // HEADS
     scaling = 1.0 / math.sqrt(features)
-    step = pl.program_id(0)
-
-    @pl.when(step == 0)
-    def _():
-        acc[...] = jnp.zeros_like(acc)
-        gains[...] = jnp.zeros_like(gains)
-        bias[...] = causal_bias(tokens, GROUP)
-
-    first = step * groups
-    stream = load_groups(x_ref, first, groups)
+    froms = (wq_hbm, wk_hbm, wv_hbm, wo_hbm, w1_hbm, w2_hbm)
+    targets = (wq_ref, wk_ref, wv_ref, wo_ref, w1_ref, w2_ref)
+    copies = [pltpu.make_async_copy(froms[i], targets[i], done.at[i]) for i in range(len(froms))]
+    for copy in copies:
+        copy.start()
+    put = putter(core_ref[0], halves)
+    bias[...] = causal_bias(tokens, GROUP)
+    stream = load_groups(x_ref)
     normal_a, inverse_a = normalize(stream)
     normed_a = (normal_a * ga_ref[...]).astype(BF16)
+    for copy in copies[:4]:
+        copy.wait()
     query = mm(normed_a, wq_ref[...]).astype(BF16)
     key = mm(normed_a, wk_ref[...]).astype(BF16)
     value = mm(normed_a, wv_ref[...]).astype(BF16)
     places = head_places(groups, tokens, features)
     probs = [softmax(mm_right_t(query[at], key[at]) * scaling + bias[...]) for at in places]
     heads = [mm(prob.astype(BF16), value[at]) for prob, at in zip(probs, places)]
-
     attended = merge_heads(heads).astype(BF16)
     middle = stream + mm(attended, wo_ref[...])
     normal_b, inverse_b = normalize(middle)
     normed_b = (normal_b * gb_ref[...]).astype(BF16)
-    up = load_groups(up_ref, first, groups)
+    up = load_groups(up_ref)
     up_low = up.astype(BF16)
-    result, normed_grad = feed_back(normed_b, up_low, w1_ref, w2_ref, acc, 4 * width, True)
-    store_groups(out_ref, first, groups, middle + result)
+    for copy in copies[4:]:
+        copy.wait()
+    result, normed_grad = feed_back(normed_b, up_low, w1_ref, w2_ref, put, 4, True)
+    store_groups(out_ref, middle + result)
     middle_norm, scale_grad = normalize_back(normed_grad, normal_b, inverse_b, gb_ref[...])
-    gains[1:2, :] += scale_grad
     middle_grad = up + middle_norm
     middle_low = middle_grad.astype(BF16)
-    acc[3 * width : 4 * width, :] += mm_left_t(attended, middle_low)
+    put(3, mm_left_t(attended, middle_low))
     up_att = mm_right_t(middle_low, wo_ref[...]).astype(BF16)
     grads = attend_back(up_att, query, key, value, probs, places, scaling)
-    normed_grad = project_back(normed_a, grads, (wq_ref, wk_ref, wv_ref), acc)
+    normed_grad = project_back(normed_a, grads, (wq_ref, wk_ref, wv_ref), put)
     stream_norm, gain_grad = normalize_back(normed_grad, normal_a, inverse_a, ga_ref[...])
-    gains[0:1, :] += gain_grad
-    store_groups(grad_ref, first, groups, middle_grad + stream_norm)
-
-    @pl.when(step == pl.num_programs(0) - 1)
-    def _():
-        emit_grads(core_ref[0], acc, gains[...], keep_ref, send_ref)
+    store_groups(grad_ref, middle_grad + stream_norm)
+    emit_grads(halves, stack_gains(gain_grad, scale_grad), keep_ref, send_ref)
 
 
 def whole(array):
@@ -385,16 +405,20 @@
     return pl.CostEstimate(flops=1, bytes_accessed=1, transcendentals=0)
 
 
-def rows_forward(inputs, gains, matrices):
+def rows_forward(inputs, gains, matrices, sent_shape):
     rows, images, cols, width = inputs.shape
     low = stored_shape(inputs.shape, BF16)
     wq, wk, wv, wo, w1, w2 = matrices
+    tile = min(HIDDEN_TILE, w1.shape[1])
+    feed = (w1.shape[1] // tile, rows * images * cols, tile)
     operands = [stored(array) for array in (inputs, gains[0], wq, wk, wv, wo, gains[1], w1, w2)]
     outs = [
-        held_shape((images, cols // GROUP, rows * GROUP, width), BF16),
+        held_shape(sent_shape, BF16),
         low, low, low, low,
         stored_shape(inputs.shape, F32),
         stored_shape((rows, images, HEADS, cols, cols), F32),
+        stored_shape(feed, BF16),
+        stored_shape(feed, F32),
     ]
     return pl.pallas_call(
         rows_forward_kernel,
@@ -402,66 +426,75 @@
         in_specs=[whole(array) for array in operands],
         out_specs=[HELD] + [whole_out(out.shape) for out in outs[1:]],
         out_shape=outs,
-        compiler_params=params(),
+        compiler_params=params(48 * 1024 * 1024),
         cost_estimate=cost(),
         name="rows_forward",
     )(*operands)
 
 
-def rows_backward(core, up, gains, kept, steps, after):
-    rows, images, cols, width = kept[0].shape
-    total = grad_rows(width, kept[1].shape[1])
-    part = (total // 2 + TAIL, width)
-    spec = pl.BlockSpec((rows, images // steps, cols, width), lambda i: (0, i, 0, 0))
+def rows_backward(core, up, gains, kept, after):
+    tokens, width = kept[1].shape[1], kept[2].shape[-1]
+    half = grad_rows(width, kept[0].shape[0]) // 2
+    part = held_shape((half + TAIL, width), BF16)
+    grad = held_shape((tokens, width), BF16)
     return pl.pallas_call(
         rows_backward_kernel,
-        grid=(steps,),
         in_specs=[SCALAR] + [HELD] * 3 + [UNREAD] * (len(kept) + 1),
-        out_specs=[spec, HELD, HELD],
-        out_shape=[shape_of(kept[0].shape, F32), held_shape(part, BF16), held_shape(part, BF16)],
-        scratch_shapes=[pltpu.VMEM((total, width), F32), pltpu.VMEM((8, width), F32)]
+        out_specs=[HELD] * 6,
+        out_shape=[held_shape((tokens, width), F32), grad, grad, grad, part, part],
+        scratch_shapes=[pltpu.VMEM((2, half, width), BF16)]
         + [pltpu.VMEM(array.shape, array.dtype) for array in kept]
         + [pltpu.SemaphoreType.DMA((len(kept),))],
-        compiler_params=params(40 * 1024 * 1024),
+        compiler_params=params(48 * 1024 * 1024),
         cost_estimate=cost(),
         name="rows_backward",
     )(core, held(up), *gains, *[stored(array) for array in kept], after)
+
+
+def rows_rest(grads, inputs, gain, matrices, after):
+    operands = [stored(array) for array in (inputs, gain, *matrices)]
+    return pl.pallas_call(
+        rows_rest_kernel,
+        grid=(1,),
+        in_specs=[HELD] * 4 + [whole(array) for array in operands] + [UNREAD],
+        out_specs=[whole_out(inputs.shape), HELD],
+        out_shape=[stored_shape(inputs.shape, F32), held_shape((8, 128), F32)],
+        compiler_params=params(24 * 1024 * 1024),
+        cost_estimate=cost(),
+        name="rows_rest",
+    )(*[held(grad) for grad in grads], *operands, after)
 
 
 def unpack(array, shape, after):
     return pl.pallas_call(
         unpack_kernel,
         in_specs=[HELD, UNREAD],
-        out_specs=pl.BlockSpec(memory_space=pltpu.VMEM),
-        out_shape=shape_of(shape, BF16),
+        out_specs=[UNREAD, HELD],
+        out_shape=[stored_shape(shape, BF16), held_shape((8, 128), F32)],
+        scratch_shapes=[pltpu.SemaphoreType.DMA((array.shape[0],))],
         compiler_params=params(SMALL_LIMIT),
         cost_estimate=cost(),
         name="unpack",
     )(held(array), after)
 
 
-def columns_both(core, stream, up, gains, matrices, steps):
-    sources, groups, height, width = stream.shape
-    total = grad_rows(width, matrices[4].shape[1])
-    tokens = sources * height
-    part = (total // 2 + TAIL, width)
-    wq, wk, wv, wo, w1, w2 = matrices
-    operands = [stored(array) for array in (gains[0], wq, wk, wv, wo, gains[1], w1, w2)]
+def columns_both(core, stream, up, gains, matrices):
+    sources, rows, cols, width = stream.shape
+    half = grad_rows(width, matrices[4].shape[1]) // 2
+    tokens = sources * rows * GROUP
+    part = (half + TAIL, width)
     return pl.pallas_call(
         columns_kernel,
-        grid=(steps,),
-        in_specs=[SCALAR, HELD, HELD] + [whole(array) for array in operands],
+        in_specs=[SCALAR] + [HELD] * 4 + [UNREAD] * len(matrices),
         out_specs=[HELD] * 4,
         out_shape=[held_shape(stream.shape, BF16)] * 2 + [held_shape(part, BF16)] * 2,
-        scratch_shapes=[
-            pltpu.VMEM((total, width), F32),
-            pltpu.VMEM((8, width), F32),
-            pltpu.VMEM((tokens, tokens), F32),
-        ],
-        compiler_params=params(),
+        scratch_shapes=[pltpu.VMEM((2, half, width), BF16), pltpu.VMEM((tokens, tokens), F32)]
+        + [pltpu.VMEM(array.shape, array.dtype) for array in matrices]
+        + [pltpu.SemaphoreType.DMA((len(matrices),))],
+        compiler_params=params(40 * 1024 * 1024),
         cost_estimate=cost(),
         name="columns_both",
-    )(core, held(stream), held(up), *operands)
+    )(core, held(stream), held(up), *gains, *[stored(array) for array in matrices])
 
 
 def add_parts(refs, size):
@@ -488,7 +521,7 @@
             out[step + TAIL :, :] = rider[0][...]
 
 
-def sum_split(at, arrays, size, ways, sends, after, rider=None, heavy=False):
+def sum_split(at, arrays, size, ways, sends, after, rider=None):
     width = arrays[0].shape[1]
     step = size // ways
     extra = 0 if rider is None else rider.shape[0]
@@ -501,7 +534,7 @@
         out_shape=[held_shape(shape, BF16) for shape in shapes],
         scratch_shapes=[pltpu.VMEM((ways, step, width), BF16)],
         compiler_params=params(SMALL_LIMIT),
-        cost_estimate=small_cost(arrays, heavy),
+        cost_estimate=small_cost(arrays),
         name="sum_split",
     )(at, *[held(array) for array in arrays], after, *riders)
 
@@ -513,7 +546,7 @@
     store_tail(tail, 0, gains)
 
 
-def sum_last(arrays, size, after, heavy=False):
+def sum_last(arrays, size, after):
     width = arrays[0].shape[1]
     return pl.pallas_call(
         functools.partial(sum_last_kernel, len(arrays), size),
@@ -521,7 +554,7 @@
         out_specs=[HELD] * 2,
         out_shape=[held_shape((size, width), BF16), held_shape((TAIL, width), BF16)],
         compiler_params=params(SMALL_LIMIT),
-        cost_estimate=small_cost(arrays, heavy),
+        cost_estimate=small_cost(arrays),
         name="sum_last",
     )(*[held(array) for array in arrays], after)
 
@@ -549,7 +582,8 @@
 
 
 def finish_kernel(buffers, at_ref, own_ref, other_ref, tail_ref, _, *refs):
-    outs, halves = list(refs[:-1]), refs[-1]
+    *outs, token_ref, halves = refs
+    token_ref[...] = jnp.zeros_like(token_ref)
     width = own_ref.shape[1]
     halves[at_ref[0]] = own_ref[...]
     halves[at_ref[0] ^ 1] = other_ref[...]
@@ -578,23 +612,22 @@
     shapes = {"square": (width, width), "columns": (width, hidden_width), "rows": (hidden_width, width)}
     kinds = [kind for _, each in buffers for kind in each]
     outs = [shapes.get(kind, (1, width)) for kind in kinds]
-    outs = pl.pallas_call(
+    *outs, token = pl.pallas_call(
         functools.partial(finish_kernel, buffers),
         grid=(1,),
         in_specs=[SCALAR, HELD, HELD, HELD, UNREAD],
-        out_specs=[whole_out(shape) for shape in outs],
-        out_shape=[shape_of(shape, F32) for shape in outs],
+        out_specs=[whole_out(shape) for shape in outs] + [HELD],
+        out_shape=[shape_of(shape, F32) for shape in outs] + [held_shape((8, 128), F32)],
         scratch_shapes=[pltpu.VMEM((2, half, width), BF16)],
         compiler_params=params(24 * 1024 * 1024),
         cost_estimate=cost(),
         name="finish",
     )(at, held(own), held(other), held(tail), after)
-    return [out.reshape(width) if isinstance(kind, int) else out for kind, out in zip(kinds, outs)]
-
-
-def small_cost(arrays, heavy=False):
-    moved = HEAVY if heavy else 1
-    return pl.CostEstimate(flops=moved, bytes_accessed=moved, transcendentals=0)
+    return [out.reshape(width) if isinstance(kind, int) else out for kind, out in zip(kinds, outs)], token
+
+
+def small_cost(arrays):
+    return pl.CostEstimate(flops=1, bytes_accessed=1, transcendentals=0)
 
 
 class Exchange:
@@ -625,14 +658,14 @@
         self.rows //= ways
         return parts[0]
 
-    def add(self, after, heavy=False):
+    def add(self, after):
         exchange = self.others.pop(0)
-        (part,) = sum_split(self.pair.place, self.arrays, self.rows, 1, 1, after, heavy=heavy)
+        (part,) = sum_split(self.pair.place, self.arrays, self.rows, 1, 1, after)
         self.arrays = [part, exchange.swap(part, 1)]
         return part
 
-    def last(self, after, heavy=False):
-        self.part, self.tail = sum_last(self.arrays, self.rows, after, heavy)
+    def last(self, after):
+        self.part, self.tail = sum_last(self.arrays, self.rows, after)
         return self.part
 
     def spread(self):
@@ -649,13 +682,14 @@
         return self.own
 
     def finish(self, after):
-        self.results = finish(self.pair.place, self.own, self.other, self.tail, self.buffers, self.hidden_width, after)
-        return self.results[0]
+        self.results, token = finish(
+            self.pair.place, self.own, self.other, self.tail, self.buffers, self.hidden_width, after
+        )
+        return token
 
 
 def on_device(inputs, cotangent, *weights):
     rows, images, cols, width = inputs.shape
-    groups = cols // GROUP
     height = lax.axis_size("row")
     devices = height * lax.axis_size("img")
     flat = lax.axis_index("img") * height + lax.axis_index("row")
@@ -667,47 +701,37 @@
     column_gains = [weights[i].reshape(1, width) for i in (8, 13)]
     matrices = [w for w in weights if w.ndim == 2]
     hidden_width = matrices[4].shape[1]
-    owned = images * groups // height
-
-    def to_columns(array):
-        array = array.reshape(height, owned, rows * GROUP, width)
+    owned = images * cols // height
+
+    def trade(array):
         return lax.all_to_all(array, "row", 0, 0, tiled=True)
-
-    def to_rows(array):
-        array = lax.all_to_all(array, "row", 0, 0, tiled=True)
-        return array.reshape(images, groups, rows * GROUP, width)
-
-    def gather_rows(array):
-        array = array.reshape(rows, images, groups, GROUP, width)
-        return array.transpose(1, 2, 0, 3, 4)
 
     squares = ("square",) * 4
     total = grad_rows(width, hidden_width)
-    steps = 2 if images % 2 == 0 and owned % 2 == 0 else 1
-    up = to_columns(gather_rows(cotangent))
-    sent, query, key, value, attended, middle, probs = rows_forward(inputs, rows_gains, matrices[:6])
+    sent_shape = (height, rows, owned, width)
+    up = cotangent.reshape(rows, height, owned, width).transpose(1, 0, 2, 3)
+    up = trade(up)
+    sent, query, key, value, attended, middle, probs, hidden, slope = rows_forward(
+        inputs, rows_gains, matrices[:6], sent_shape
+    )
     sent, up = lax.optimization_barrier((sent, up))
-    stream = to_columns(sent)
-    final, between_grad, keep, send = columns_both(core, stream, up, column_gains, matrices[6:], steps)
+    stream = trade(sent)
+    final, between_grad, keep, send = columns_both(core, stream, up, column_gains, matrices[6:])
     kinds = (0, *squares, 1, "columns", "rows")
     columns = Chain(exchanges, ((total, kinds),), keep, send, hidden_width)
-    token = columns.cut(columns.token)
-    token = columns.add(token)
-    between_grad = to_rows(between_grad)
+    token = columns.add(columns.cut(columns.token))
+    between_grad = trade(between_grad)
     between_grad, final, token = lax.optimization_barrier((between_grad, final, token))
-    final = to_rows(final)
+    final = trade(final)
     wq, wk, wv, wo, w1, w2 = matrices[:6]
-    kept = (middle, w1, w2, attended, wo, query, key, value, probs, inputs, wq, wk, wv)
-    stream_grad, keep, send = rows_backward(core, between_grad, rows_gains, kept, steps, token)
+    kept = (w2, slope, middle, w1, hidden, attended, wo, query, key, value, probs, inputs, wq, wk, wv)
+    *grads, keep, send = rows_backward(core, between_grad, rows_gains, kept, token)
     rows_chain = Chain(exchanges, ((total, kinds),), keep, send, hidden_width)
-    token = rows_chain.token
-    if PLACE == 0:
-        token = final = unpack(final, inputs.shape, token)
-    while len(columns.others):
+    token = rows_chain.cut(rows_chain.token)
+    stream_grad, token = rows_rest(grads, inputs, rows_gains[0], (wq, wk, wv), token)
+    while columns.others:
         token = columns.add(token)
-    token = rows_chain.cut(token)
-    if PLACE == 1:
-        token = final = unpack(final, inputs.shape, token)
+    final, token = unpack(final, inputs.shape, token)
     token = rows_chain.add(token)
     token = columns.last(token)
     columns.spread()

time: 175 us -> 181 us (1.034)
  starting transfers between devices: 45.7 us -> 56.6 us
  waiting for transfers between devices: 76.4 us -> 66.6 us
  Pallas kernels: 47.7 us -> 51.9 us
    all_to_all x4, starting transfers between devices: 23.9 us -> 33.2 us  [trade(): return lax.all_to_all(array, 'row', 0, 0, tiled=True)]
    all_to_all x4, waiting for transfers between devices: 29.4 us -> 24.4 us  [trade(): return lax.all_to_all(array, 'row', 0, 0, tiled=True)]
    ppermute x20, waiting for transfers between devices: 47.1 us -> 42.2 us  [swap(): lax.ppermute(array, ALL, [(i, i ^ mask) for i in range(self.devices)])]
    pallas_call x1, Pallas kernels: 8.04 us -> 12.7 us  [rows_forward(): pl.pallas_call(rows_forward_kernel, grid=(1,), in_specs=[whole(array) for...]
    pallas_call x3 -> x4, Pallas kernels: 34.3 us -> 33.8 us  [the longest x1 16.1 us: columns_both(): pl.pallas_call(columns_kernel, in_specs=[SCALAR] + [HELD] * 4 + [UNREAD]...]
  transfers between devices with their start and end apart: 24 -> 24, of which waited for: 16 -> 15; matrix products, arithmetic and copies ran while one was open for 0% -> 0% of each run, Pallas kernels for 16% -> 19%
where the time goes in v3:
time: 181 us; the launch traced here: 179 us
  waiting for transfers between devices  66.6 us (37%)
  starting transfers between devices  56.6 us (31%)
  Pallas kernels  51.9 us (29%)
  local copies, waits for them, and re-layouts  2.78 us (2%)
    ppermute x20, waiting for transfers between devices, swap(): lax.ppermute(array, ALL, [(i, i ^ mask) for i in range(self.devices)])  42.2 us
    all_to_all x4, starting transfers between devices, trade(): return lax.all_to_all(array, 'row', 0, 0, tiled=True)  33.2 us
    all_to_all x4, waiting for transfers between devices, trade(): return lax.all_to_all(array, 'row', 0, 0, tiled=True)  24.4 us
    ppermute x20, starting transfers between devices, swap(): lax.ppermute(array, ALL, [(i, i ^ mask) for i in range(self.devices)])  23.3 us
    pallas_call x1, Pallas kernels, columns_both(): pl.pallas_call(columns_kernel, in_specs=[SCALAR] + [HELD] * 4 + [UNREAD]...  16.1 us
    pallas_call x1, Pallas kernels, rows_backward(): pl.pallas_call(rows_backward_kernel, in_specs=[SCALAR] + [HELD] * 3 + [UN...  12.8 us
    pallas_call x1, Pallas kernels, rows_forward(): pl.pallas_call(rows_forward_kernel, grid=(1,), in_specs=[whole(array) for...  12.7 us
    pallas_call x1, Pallas kernels, rows_rest(): pl.pallas_call(rows_rest_kernel, grid=(1,), in_specs=[HELD] * 4 + [whole(...  3.92 us
  transfers between devices with their start and end apart: 24, of which 15 were waited for; matrix products, arithmetic and copies ran while one was open for 0% of the time, Pallas kernels for 19%

profile of v3, /device:TPU:0, one launch (start us, length us, event | category | flops | bytes accessed | tf_op | source)
XLA Modules:
  0.0 178.9 jit_solution(12017999115649057616)
XLA Ops:
  0.7 2.1 %copy.38 = bf16[2,16,48,256]{3,2,0,1:T(8,128)(2,1)} copy(bf16[2,16,48,256]{3,2,1,0:T(8,128)(2,1)} %bitcast.24) | data formatting | bytes 1572864 | tf_op jit(solution)/shard_map/reshape | solution.py:712
  2.7 7.4 %all-to-all-start = ((bf16[16,2,48,256]{3,2,1,0:T(8,128)(2,1)}), bf16[16,2,48,256]{3,2,1,0:T(8,128)(2,1)S(1)}, u32[]{:S(2)}, u32[]{:S(2)}) async-start(bf16[16,2,48,256]{3,2,1,0:T(8,128)(2,1)} %bitcast.15), calls=%async_computation | async-start | bytes 1572864 | tf_op jit(solution)/shard_map/all_to_all | solution.py:707
  10.2 12.7 %rows_forward.1 = (bf16[16,2,48,256]{3,2,1,0:T(8,128)(2,1)}, bf16[2,8,96,256]{3,2,1,0:T(8,128)(2,1)}, bf16[2,8,96,256]{3,2,1,0:T(8,128)(2,1)}, bf16[2,8,96,256]{...) custom-call(bf16[2,8,96,256]{3,2,1,0:T(8,128)(2,1)} %x_ref.3, ...), custom_call_target="tpu_custom_call" | custom-call | flops 1 | bytes 1 | tf_op jit(solution)/shard_map/rows_forward/pallas_call | solution.py:423
  22.9 5.9 %all-to-all-done.up_ref = bf16[16,2,48,256]{3,2,1,0:T(8,128)(2,1)S(1)} async-done(((bf16[16,2,48,256]{3,2,1,0:T(8,128)(2,1)}), bf16[16,2,48,256]{3,2,1,0:T(8,128)(2,1)S(1)}, u32[]{:S(2)}, u32[]{:S(2)}) %all-to-all-start) | async-done | bytes 786464 | tf_op jit(solution)/shard_map/all_to_all | solution.py:707
  28.8 5.7 %all-to-all-start.1 = ((bf16[16,2,48,256]{3,2,1,0:T(8,128)(2,1)}), bf16[16,2,48,256]{3,2,1,0:T(8,128)(2,1)S(1)}, u32[]{:S(2)}, u32[]{:S(2)}) async-start(bf16[16,2,48,256]{3,2,1,0:T(8,128)(2,1)} %get-tuple-element.76), calls=%async_computation.1 | async-start | bytes 1572864 | tf_op jit(solution)/shard_map/all_to_all | solution.py:707
  34.6 18.4 %all-to-all-done.1.x_ref = bf16[16,2,48,256]{3,2,1,0:T(8,128)(2,1)S(1)} async-done(((bf16[16,2,48,256]{3,2,1,0:T(8,128)(2,1)}), bf16[16,2,48,256]{3,2,1,0:T(8,128)(2,1)S(1)}, u32[]{:S(2)}, u32[]{:S(2)}) %all-to-all-start.1) | async-done | bytes 786464 | tf_op jit(solution)/shard_map/all_to_all | solution.py:707
  53.0 16.1 %columns_both.1 = (bf16[16,2,48,256]{3,2,1,0:T(8,128)(2,1)}, bf16[16,2,48,256]{3,2,1,0:T(8,128)(2,1)}, bf16[1552,256]{1,0:T(8,128)(2,1)S(1)}, bf16[1552,256]{1,0:T(8,128)(2,1)S(1)}) custom-call(s32[1]{0:T(128)} %bitcast.core_ref.at_ref, bf16[16,2,48,256]{3,2,1,0:T(8,128)(2,1)S(1)} %all-to-all-done.1.x_ref, bf16[16,2,48,256]{3,2,1,0:T(8,128)(2,1)S(1)} %all-to-all-done.up_ref, ...), custom_call_target="tpu_custom_call" | custom-call | flops 1 | bytes 1 | tf_op jit(solution)/shard_map/columns_both/pallas_call | solution.py:486
  69.2 5.5 %all-to-all-start.2 = ((bf16[16,2,48,256]{3,2,1,0:T(8,128)(2,1)}), bf16[16,2,48,256]{3,2,1,0:T(8,128)(2,1)S(1)}, u32[]{:S(2)}, u32[]{:S(2)}) async-start(bf16[16,2,48,256]{3,2,1,0:T(8,128)(2,1)} %get-tuple-element.78), calls=%async_computation.2 | async-start | bytes 1572864 | tf_op jit(solution)/shard_map/all_to_all | solution.py:707
  75.1 2.0 %collective-permute-done.refs_1_ = bf16[1552,256]{1,0:T(8,128)(2,1)S(1)} collective-permute-done((bf16[1552,256]{1,0:T(8,128)(2,1)S(1)}, bf16[1552,256]{1,0:T(8,128)(2,1)S(1)}, u32[]{:S(2)}, u32[]{:S(2)}) %collective-permute-start) | collective-permute-done | bytes 794656 | tf_op jit(solution)/shard_map/ppermute | solution.py:643
  81.1 4.4 %collective-permute-done.1.refs_1_ = bf16[400,256]{1,0:T(8,128)(2,1)S(1)} collective-permute-done((bf16[400,256]{1,0:T(8,128)(2,1)S(1)}, bf16[400,256]{1,0:T(8,128)(2,1)S(1)}, u32[]{:S(2)}, u32[]{:S(2)}) %collective-permute-start.1) | collective-permute-done | bytes 204832 | tf_op jit(solution)/shard_map/ppermute | solution.py:643
  85.5 9.7 %collective-permute-done.2.refs_2_ = bf16[400,256]{1,0:T(8,128)(2,1)S(1)} collective-permute-done((bf16[400,256]{1,0:T(8,128)(2,1)S(1)}, bf16[400,256]{1,0:T(8,128)(2,1)S(1)}, u32[]{:S(2)}, u32[]{:S(2)}) %collective-permute-start.2) | collective-permute-done | bytes 204832 | tf_op jit(solution)/shard_map/ppermute | solution.py:643
  95.9 14.6 %all-to-all-start.3 = ((bf16[16,2,48,256]{3,2,1,0:T(8,128)(2,1)}), bf16[16,2,48,256]{3,2,1,0:T(8,128)(2,1)S(1)}, u32[]{:S(2)}, u32[]{:S(2)}) async-start(bf16[16,2,48,256]{3,2,1,0:T(8,128)(2,1)} %get-tuple-element.86), calls=%async_computation.3 | async-start | bytes 1572864 | tf_op jit(solution)/shard_map/all_to_all | solution.py:707
  110.6 12.8 %rows_backward.1 = (f32[1536,256]{1,0:T(8,128)S(1)}, bf16[1536,256]{1,0:T(8,128)(2,1)S(1)}, bf16[1536,256]{1,0:T(8,128)(2,1)S(1)}, bf16[1536,256]{1,0:T(8,128)(2...) custom-call(s32[1]{0:T(128)} %bitcast.core_ref.at_ref, ...), custom_call_target="tpu_custom_call" | custom-call | flops 1 | bytes 1 | tf_op jit(solution)/shard_map/rows_backward/pallas_call | solution.py:440
  129.8 3.9 %rows_rest.1 = (f32[2,8,96,256]{3,2,1,0:T(8,128)}, f32[8,128]{1,0:T(8,128)S(1)}) custom-call(f32[1536,256]{1,0:T(8,128)S(1)} %get-tuple-element.97.mid_grad_ref, bf16[1536,256]{1,0:T(8,128)(2,1)S(1)} %get-tuple-element.98.dq_ref, bf16[1536,256]{1,0:T(8,128)(2,1)S(1)} %get-tuple-element.99.dk_ref, bf16[1536,256]{1,0:T(8,128)(2,1)S(1)} %get-tuple-element.100.dv_ref, ...), custom_call_target="tpu_custom_call" | custom-call | flops 1 | bytes 1 | tf_op jit(solution)/shard_map/rows_rest/pallas_call | solution.py:456
  133.8 2.6 %collective-permute-start.10 = (bf16[400,256]{1,0:T(8,128)(2,1)S(1)}, bf16[400,256]{1,0:T(8,128)(2,1)S(1)}, u32[]{:S(2)}, u32[]{:S(2)}) collective-permute-start(bf16[400,256]{1,0:T(8,128)(2,1)S(1)} %sum_split.9._.refs_0_), channel_id=1, source_target_pairs={{0,8},{1,9},{2,10},{3,11},{4,12},{5,13},{6,14},{7,15},{8,0},{9,1},... | collective-permute-start | bytes 614408 | tf_op jit(solution)/shard_map/ppermute | solution.py:643
  140.6 5.0 %collective-permute-done.10.refs_1_ = bf16[400,256]{1,0:T(8,128)(2,1)S(1)} collective-permute-done((bf16[400,256]{1,0:T(8,128)(2,1)S(1)}, bf16[400,256]{1,0:T(8,128)(2,1)S(1)}, u32[]{:S(2)}, u32[]{:S(2)}) %collective-permute-start.10) | collective-permute-done | bytes 204832 | tf_op jit(solution)/shard_map/ppermute | solution.py:643
  145.6 3.0 %collective-permute-done.9.refs_1_ = bf16[400,256]{1,0:T(8,128)(2,1)S(1)} collective-permute-done((bf16[400,256]{1,0:T(8,128)(2,1)S(1)}, bf16[400,256]{1,0:T(8,128)(2,1)S(1)}, u32[]{:S(2)}, u32[]{:S(2)}) %collective-permute-start.9) | collective-permute-done | bytes 204832 | tf_op jit(solution)/shard_map/ppermute | solution.py:643
  148.6 2.5 %collective-permute-start.11 = (bf16[400,256]{1,0:T(8,128)(2,1)S(1)}, bf16[400,256]{1,0:T(8,128)(2,1)S(1)}, u32[]{:S(2)}, u32[]{:S(2)}) collective-permute-start(bf16[400,256]{1,0:T(8,128)(2,1)S(1)} %sum_split.11.refs_0_.refs_2_), channel_id=1, source_target_pairs={{0,8},{1,9},{2,10},{3,11},{4,12},{5,13},{6,14},{7,15},{8,0},{9,1},... | collective-permute-start | bytes 614408 | tf_op jit(solution)/shard_map/ppermute | solution.py:643
  154.6 5.8 %collective-permute-done.11.refs_1_ = bf16[400,256]{1,0:T(8,128)(2,1)S(1)} collective-permute-done((bf16[400,256]{1,0:T(8,128)(2,1)S(1)}, bf16[400,256]{1,0:T(8,128)(2,1)S(1)}, u32[]{:S(2)}, u32[]{:S(2)}) %collective-permute-start.11) | collective-permute-done | bytes 204832 | tf_op jit(solution)/shard_map/ppermute | solution.py:643
  165.5 1.9 %finish.2 = (f32[1,256]{1,0:T(1,128)}, f32[256,256]{1,0:T(8,128)}, f32[256,256]{1,0:T(8,128)}, f32[256,256]{1,0:T(8,128)}, f32[256,256]{1,0:T(8,128)}, /*index=5...) custom-call(s32[1]{0:T(128)} %bitcast.core_ref.at_ref, ...), custom_call_target="tpu_custom_call" | custom-call | flops 1 | bytes 1 | tf_op jit(solution)/shard_map/finish/pallas_call | solution.py:615
  167.4 3.2 %collective-permute-done.14.refs_3_ = bf16[384,256]{1,0:T(8,128)(2,1)S(1)} collective-permute-done((bf16[384,256]{1,0:T(8,128)(2,1)S(1)}, bf16[384,256]{1,0:T(8,128)(2,1)S(1)}, u32[]{:S(2)}, u32[]{:S(2)}) %collective-permute-start.14) | collective-permute-done | bytes 196640 | tf_op jit(solution)/shard_map/ppermute | solution.py:643
  170.6 3.7 %collective-permute-done.13.refs_2_ = bf16[384,256]{1,0:T(8,128)(2,1)S(1)} collective-permute-done((bf16[384,256]{1,0:T(8,128)(2,1)S(1)}, bf16[384,256]{1,0:T(8,128)(2,1)S(1)}, u32[]{:S(2)}, u32[]{:S(2)}) %collective-permute-start.13) | collective-permute-done | bytes 196640 | tf_op jit(solution)/shard_map/ppermute | solution.py:643
  174.5 2.2 %collective-permute-done.19.other_ref = bf16[1536,256]{1,0:T(8,128)(2,1)S(1)} collective-permute-done((bf16[1536,256]{1,0:T(8,128)(2,1)S(1)}, bf16[1536,256]{1,0:T(8,128)(2,1)S(1)}, u32[]{:S(2)}, u32[]{:S(2)}) %collective-permute-start.19) | collective-permute-done | bytes 786464 | tf_op jit(solution)/shard_map/ppermute | solution.py:643
  176.8 1.9 %finish.3 = (f32[1,256]{1,0:T(1,128)}, f32[256,256]{1,0:T(8,128)}, f32[256,256]{1,0:T(8,128)}, f32[256,256]{1,0:T(8,128)}, f32[256,256]{1,0:T(8,128)}, /*index=5...) custom-call(s32[1]{0:T(128)} %bitcast.core_ref.at_ref, ...), custom_call_target="tpu_custom_call" | custom-call | flops 1 | bytes 1 | tf_op jit(solution)/shard_map/finish/pallas_call | solution.py:615
  (50 shorter events, 24.6 us)
Async XLA Ops:
  2.7 26.1 %all-to-all-start = ((bf16[16,2,48,256]{3,2,1,0:T(8,128)(2,1)}), bf16[16,2,48,256]{3,2,1,0:T(8,128)(2,1)S(1)}, u32[]{:S(2)}, u32[]{:S(2)}) async-start(bf16[16,2,48,256]{3,2,1,0:T(8,128)(2,1)} %bitcast.15), calls=%async_computation | async-start | bytes 1572864 | tf_op jit(solution)/shard_map/all_to_all | solution.py:707
  28.8 24.2 %all-to-all-start.1 = ((bf16[16,2,48,256]{3,2,1,0:T(8,128)(2,1)}), bf16[16,2,48,256]{3,2,1,0:T(8,128)(2,1)S(1)}, u32[]{:S(2)}, u32[]{:S(2)}) async-start(bf16[16,2,48,256]{3,2,1,0:T(8,128)(2,1)} %get-tuple-element.76), calls=%async_computation.1 | async-start | bytes 1572864 | tf_op jit(solution)/shard_map/all_to_all | solution.py:707
  69.2 26.8 %all-to-all-start.2 = ((bf16[16,2,48,256]{3,2,1,0:T(8,128)(2,1)}), bf16[16,2,48,256]{3,2,1,0:T(8,128)(2,1)S(1)}, u32[]{:S(2)}, u32[]{:S(2)}) async-start(bf16[16,2,48,256]{3,2,1,0:T(8,128)(2,1)} %get-tuple-element.78), calls=%async_computation.2 | async-start | bytes 1572864 | tf_op jit(solution)/shard_map/all_to_all | solution.py:707
  74.7 2.4 %collective-permute-start = (bf16[1552,256]{1,0:T(8,128)(2,1)S(1)}, bf16[1552,256]{1,0:T(8,128)(2,1)S(1)}, u32[]{:S(2)}, u32[]{:S(2)}) collective-permute-start(bf16[1552,256]{1,0:T(8,128)(2,1)S(1)} %get-tuple-element.81), channel_id=1, source_target_pairs={{0,1},{1,0},{2,3},{3,2},{4,5},{5,4},{6,7},{7,6},{8,9},{9,8},{10,11... | collective-permute-start | bytes 2383880 | tf_op jit(solution)/shard_map/ppermute | solution.py:643
  77.5 8.0 %collective-permute-start.1 = (bf16[400,256]{1,0:T(8,128)(2,1)S(1)}, bf16[400,256]{1,0:T(8,128)(2,1)S(1)}, u32[]{:S(2)}, u32[]{:S(2)}) collective-permute-start(bf16[400,256]{1,0:T(8,128)(2,1)S(1)} %get-tuple-element.83), channel_id=1, source_target_pairs={{0,16},{1,17},{2,18},{3,19},{4,20},{5,21},{6,22},{7,23},{8,24},{9,... | collective-permute-start | bytes 614408 | tf_op jit(solution)/shard_map/ppermute | solution.py:643
  79.1 16.1 %collective-permute-start.2 = (bf16[400,256]{1,0:T(8,128)(2,1)S(1)}, bf16[400,256]{1,0:T(8,128)(2,1)S(1)}, u32[]{:S(2)}, u32[]{:S(2)}) collective-permute-start(bf16[400,256]{1,0:T(8,128)(2,1)S(1)} %get-tuple-element.84), channel_id=1, source_target_pairs={{0,2},{1,3},{2,0},{3,1},{4,6},{5,7},{6,4},{7,5},{8,10},{9,11},{10,... | collective-permute-start | bytes 614408 | tf_op jit(solution)/shard_map/ppermute | solution.py:643
  80.9 14.2 %collective-permute-start.3 = (bf16[400,256]{1,0:T(8,128)(2,1)S(1)}, bf16[400,256]{1,0:T(8,128)(2,1)S(1)}, u32[]{:S(2)}, u32[]{:S(2)}) collective-permute-start(bf16[400,256]{1,0:T(8,128)(2,1)S(1)} %get-tuple-element.85), channel_id=1, source_target_pairs={{0,18},{1,19},{2,16},{3,17},{4,22},{5,23},{6,20},{7,21},{8,26},{9,... | collective-permute-start | bytes 614408 | tf_op jit(solution)/shard_map/ppermute | solution.py:643
  95.9 40.5 %all-to-all-start.3 = ((bf16[16,2,48,256]{3,2,1,0:T(8,128)(2,1)}), bf16[16,2,48,256]{3,2,1,0:T(8,128)(2,1)S(1)}, u32[]{:S(2)}, u32[]{:S(2)}) async-start(bf16[16,2,48,256]{3,2,1,0:T(8,128)(2,1)} %get-tuple-element.86), calls=%async_computation.3 | async-start | bytes 1572864 | tf_op jit(solution)/shard_map/all_to_all | solution.py:707
  123.4 2.4 %collective-permute-start.5 = (bf16[1552,256]{1,0:T(8,128)(2,1)S(1)}, bf16[1552,256]{1,0:T(8,128)(2,1)S(1)}, u32[]{:S(2)}, u32[]{:S(2)}) collective-permute-start(bf16[1552,256]{1,0:T(8,128)(2,1)S(1)} %get-tuple-element.102), channel_id=1, source_target_pairs={{0,1},{1,0},{2,3},{3,2},{4,5},{5,4},{6,7},{7,6},{8,9},{9,8},{10,11... | collective-permute-start | bytes 2383880 | tf_op jit(solution)/shard_map/ppermute | solution.py:643
  123.6 10.1 %collective-permute-start.4 = (bf16[400,256]{1,0:T(8,128)(2,1)S(1)}, bf16[400,256]{1,0:T(8,128)(2,1)S(1)}, u32[]{:S(2)}, u32[]{:S(2)}) collective-permute-start(bf16[400,256]{1,0:T(8,128)(2,1)S(1)} %copy-done.1), channel_id=1, source_target_pairs={{0,4},{1,5},{2,6},{3,7},{4,0},{5,1},{6,2},{7,3},{8,12},{9,13},{10,... | collective-permute-start | bytes 614408 | tf_op jit(solution)/shard_map/ppermute | solution.py:643
  126.2 11.2 %collective-permute-start.6 = (bf16[400,256]{1,0:T(8,128)(2,1)S(1)}, bf16[400,256]{1,0:T(8,128)(2,1)S(1)}, u32[]{:S(2)}, u32[]{:S(2)}) collective-permute-start(bf16[400,256]{1,0:T(8,128)(2,1)S(1)} %get-tuple-element.107), channel_id=1, source_target_pairs={{0,16},{1,17},{2,18},{3,19},{4,20},{5,21},{6,22},{7,23},{8,24},{9,... | collective-permute-start | bytes 614408 | tf_op jit(solution)/shard_map/ppermute | solution.py:643
  127.0 10.5 %collective-permute-start.7 = (bf16[400,256]{1,0:T(8,128)(2,1)S(1)}, bf16[400,256]{1,0:T(8,128)(2,1)S(1)}, u32[]{:S(2)}, u32[]{:S(2)}) collective-permute-start(bf16[400,256]{1,0:T(8,128)(2,1)S(1)} %get-tuple-element.108), channel_id=1, source_target_pairs={{0,2},{1,3},{2,0},{3,1},{4,6},{5,7},{6,4},{7,5},{8,10},{9,11},{10,... | collective-permute-start | bytes 614408 | tf_op jit(solution)/shard_map/ppermute | solution.py:643
  128.7 10.2 %collective-permute-start.8 = (bf16[400,256]{1,0:T(8,128)(2,1)S(1)}, bf16[400,256]{1,0:T(8,128)(2,1)S(1)}, u32[]{:S(2)}, u32[]{:S(2)}) collective-permute-start(bf16[400,256]{1,0:T(8,128)(2,1)S(1)} %get-tuple-element.109), channel_id=1, source_target_pairs={{0,18},{1,19},{2,16},{3,17},{4,22},{5,23},{6,20},{7,21},{8,26},{9,... | collective-permute-start | bytes 614408 | tf_op jit(solution)/shard_map/ppermute | solution.py:643
  133.8 11.8 %collective-permute-start.10 = (bf16[400,256]{1,0:T(8,128)(2,1)S(1)}, bf16[400,256]{1,0:T(8,128)(2,1)S(1)}, u32[]{:S(2)}, u32[]{:S(2)}) collective-permute-start(bf16[400,256]{1,0:T(8,128)(2,1)S(1)} %sum_split.9._.refs_0_), channel_id=1, source_target_pairs={{0,8},{1,9},{2,10},{3,11},{4,12},{5,13},{6,14},{7,15},{8,0},{9,1},... | collective-permute-start | bytes 614408 | tf_op jit(solution)/shard_map/ppermute | solution.py:643
  139.0 9.5 %collective-permute-start.9 = (bf16[400,256]{1,0:T(8,128)(2,1)S(1)}, bf16[400,256]{1,0:T(8,128)(2,1)S(1)}, u32[]{:S(2)}, u32[]{:S(2)}) collective-permute-start(bf16[400,256]{1,0:T(8,128)(2,1)S(1)} %sum_split.10.refs_2_.refs_0_), channel_id=1, source_target_pairs={{0,4},{1,5},{2,6},{3,7},{4,0},{5,1},{6,2},{7,3},{8,12},{9,13},{10,... | collective-permute-start | bytes 614408 | tf_op jit(solution)/shard_map/ppermute | solution.py:643
  148.6 11.8 %collective-permute-start.11 = (bf16[400,256]{1,0:T(8,128)(2,1)S(1)}, bf16[400,256]{1,0:T(8,128)(2,1)S(1)}, u32[]{:S(2)}, u32[]{:S(2)}) collective-permute-start(bf16[400,256]{1,0:T(8,128)(2,1)S(1)} %sum_split.11.refs_0_.refs_2_), channel_id=1, source_target_pairs={{0,8},{1,9},{2,10},{3,11},{4,12},{5,13},{6,14},{7,15},{8,0},{9,1},... | collective-permute-start | bytes 614408 | tf_op jit(solution)/shard_map/ppermute | solution.py:643
  151.1 9.3 %collective-permute-start.17 = (bf16[384,256]{1,0:T(8,128)(2,1)S(1)}, bf16[384,256]{1,0:T(8,128)(2,1)S(1)}, u32[]{:S(2)}, u32[]{:S(2)}) collective-permute-start(bf16[384,256]{1,0:T(8,128)(2,1)S(1)} %get-tuple-element.111.refs_2_.refs_0_), channel_id=1, source_target_pairs={{0,18},{1,19},{2,16},{3,17},{4,22},{5,23},{6,20},{7,21},{8,26},{9,... | collective-permute-start | bytes 589832 | tf_op jit(solution)/shard_map/ppermute | solution.py:643
  152.0 9.8 %collective-permute-start.16 = (bf16[384,256]{1,0:T(8,128)(2,1)S(1)}, bf16[384,256]{1,0:T(8,128)(2,1)S(1)}, u32[]{:S(2)}, u32[]{:S(2)}) collective-permute-start(bf16[384,256]{1,0:T(8,128)(2,1)S(1)} %get-tuple-element.111.refs_2_.refs_0_), channel_id=1, source_target_pairs={{0,2},{1,3},{2,0},{3,1},{4,6},{5,7},{6,4},{7,5},{8,10},{9,11},{10,... | collective-permute-start | bytes 589832 | tf_op jit(solution)/shard_map/ppermute | solution.py:643
  153.4 8.4 %collective-permute-start.15 = (bf16[384,256]{1,0:T(8,128)(2,1)S(1)}, bf16[384,256]{1,0:T(8,128)(2,1)S(1)}, u32[]{:S(2)}, u32[]{:S(2)}) collective-permute-start(bf16[384,256]{1,0:T(8,128)(2,1)S(1)} %get-tuple-element.111.refs_2_.refs_0_), channel_id=1, source_target_pairs={{0,16},{1,17},{2,18},{3,19},{4,20},{5,21},{6,22},{7,23},{8,24},{9,... | collective-permute-start | bytes 589832 | tf_op jit(solution)/shard_map/ppermute | solution.py:643
  161.9 3.6 %collective-permute-start.18 = (bf16[1536,256]{1,0:T(8,128)(2,1)S(1)}, bf16[1536,256]{1,0:T(8,128)(2,1)S(1)}, u32[]{:S(2)}, u32[]{:S(2)}) collective-permute-start(bf16[1536,256]{1,0:T(8,128)(2,1)S(1)} %bitcast.16), channel_id=1, source_target_pairs={{0,1},{1,0},{2,3},{3,2},{4,5},{5,4},{6,7},{7,6},{8,9},{9,8},{10,11... | collective-permute-start | bytes 2359304 | tf_op jit(solution)/shard_map/ppermute | solution.py:643
  161.9 8.7 %collective-permute-start.14 = (bf16[384,256]{1,0:T(8,128)(2,1)S(1)}, bf16[384,256]{1,0:T(8,128)(2,1)S(1)}, u32[]{:S(2)}, u32[]{:S(2)}) collective-permute-start(bf16[384,256]{1,0:T(8,128)(2,1)S(1)} %get-tuple-element.112.refs_4_.refs_0_), channel_id=1, source_target_pairs={{0,18},{1,19},{2,16},{3,17},{4,22},{5,23},{6,20},{7,21},{8,26},{9,... | collective-permute-start | bytes 589832 | tf_op jit(solution)/shard_map/ppermute | solution.py:643
  163.5 10.9 %collective-permute-start.13 = (bf16[384,256]{1,0:T(8,128)(2,1)S(1)}, bf16[384,256]{1,0:T(8,128)(2,1)S(1)}, u32[]{:S(2)}, u32[]{:S(2)}) collective-permute-start(bf16[384,256]{1,0:T(8,128)(2,1)S(1)} %get-tuple-element.112.refs_4_.refs_0_), channel_id=1, source_target_pairs={{0,2},{1,3},{2,0},{3,1},{4,6},{5,7},{6,4},{7,5},{8,10},{9,11},{10,... | collective-permute-start | bytes 589832 | tf_op jit(solution)/shard_map/ppermute | solution.py:643
  164.6 9.7 %collective-permute-start.12 = (bf16[384,256]{1,0:T(8,128)(2,1)S(1)}, bf16[384,256]{1,0:T(8,128)(2,1)S(1)}, u32[]{:S(2)}, u32[]{:S(2)}) collective-permute-start(bf16[384,256]{1,0:T(8,128)(2,1)S(1)} %get-tuple-element.112.refs_4_.refs_0_), channel_id=1, source_target_pairs={{0,16},{1,17},{2,18},{3,19},{4,20},{5,21},{6,22},{7,23},{8,24},{9,... | collective-permute-start | bytes 589832 | tf_op jit(solution)/shard_map/ppermute | solution.py:643
  174.4 2.4 %collective-permute-start.19 = (bf16[1536,256]{1,0:T(8,128)(2,1)S(1)}, bf16[1536,256]{1,0:T(8,128)(2,1)S(1)}, u32[]{:S(2)}, u32[]{:S(2)}) collective-permute-start(bf16[1536,256]{1,0:T(8,128)(2,1)S(1)} %bitcast.19), channel_id=1, source_target_pairs={{0,1},{1,0},{2,3},{3,2},{4,5},{5,4},{6,7},{7,6},{8,9},{9,8},{10,11... | collective-permute-start | bytes 2359304 | tf_op jit(solution)/shard_map/ppermute | solution.py:643
  (4 other events, 99.5 us)

commit v4 on v3

--- a/solution.py
+++ b/solution.py
@@ -97,27 +97,23 @@
     return tuple(merge_heads(grads) for grads in (query_grads, key_grads, value_grads))
 
 
-def feed_back(normed, up_low, expand_ref, shrink_ref, put, first, forward):
-    width = normed.shape[-1]
+def feed_back(normed, up_low, expand_ref, shrink_ref, put, first, result_ref, grad_ref):
     hidden_width = expand_ref.shape[1]
     tile = min(HIDDEN_TILE, hidden_width)
-    result = None
-    normed_grad = None
-    for j in range(hidden_width // tile):
-        cut = slice(j * tile, (j + 1) * tile)
+    tiles = hidden_width // tile
+
+    @pl.loop(0, tiles)
+    def _(j):
+        cut = pl.ds(pl.multiple_of(j * tile, tile), tile)
         expand = expand_ref[:, cut]
         shrink = shrink_ref[cut, :]
         hidden, slope = gelu_both(mm(normed, expand))
         hidden = hidden.astype(BF16)
-        if forward:
-            part = mm(hidden, shrink)
-            result = part if result is None else result + part
+        result_ref[...] += mm(hidden, shrink)
         expanded_grad = (slope * mm_right_t(up_low, shrink)).astype(BF16)
         put(first + j, mm_left_t(normed, expanded_grad))
-        put(first + hidden_width // tile + j, mm_left_t(up_low, hidden))
-        part = mm_right_t(expanded_grad, expand)
-        normed_grad = part if normed_grad is None else normed_grad + part
-    return result, normed_grad
+        put(first + tiles + j, mm_left_t(up_low, hidden))
+        grad_ref[...] += mm_right_t(expanded_grad, expand)
 
 
 def project_back(normed_low, grads, weight_refs, put):
@@ -140,8 +136,8 @@
     blocks = halves.shape[1] // width
 
     def put(block, value):
-        half, row = divmod(block, blocks)
-        halves[half ^ core, row * width : (row + 1) * width, :] = value.astype(BF16)
+        start = pl.multiple_of(lax.rem(block, blocks) * width, width)
+        halves[lax.div(block, blocks) ^ core, pl.ds(start, width), :] = value.astype(BF16)
 
     return put
 
@@ -158,7 +154,7 @@
 
 def rows_forward_kernel(
     x_ref, ga_ref, wq_ref, wk_ref, wv_ref, wo_ref, gb_ref, w1_ref, w2_ref,
-    send_ref, q_ref, k_ref, v_ref, att_ref, mid_ref, p_ref, hidden_ref, slope_ref,
+    send_ref, q_ref, k_ref, v_ref, att_ref, mid_ref, p_ref, hidden_ref, slope_ref, result_ref,
 ):
     rows, images, cols, width = x_ref.shape
     tokens = rows * images * cols
@@ -184,16 +180,19 @@
     middle = stream + mm(attended, wo_ref[...])
     mid_ref[...] = middle.reshape(mid_ref.shape)
     normed_b = (normalize(middle)[0] * gb_ref[...]).astype(BF16)
-    hidden_width = w1_ref.shape[1]
-    tile = min(HIDDEN_TILE, hidden_width)
-    result = middle
-    for j in range(hidden_width // tile):
-        cut = slice(j * tile, (j + 1) * tile)
+    tiles, _, tile = hidden_ref.shape
+    result_ref[...] = middle
+
+    @pl.loop(0, tiles)
+    def _(j):
+        cut = pl.ds(pl.multiple_of(j * tile, tile), tile)
         hidden, slope = gelu_both(mm(normed_b, w1_ref[:, cut]))
         hidden = hidden.astype(BF16)
         hidden_ref[j] = hidden
         slope_ref[j] = slope
-        result = result + mm(hidden, w2_ref[cut, :])
+        result_ref[...] += mm(hidden, w2_ref[cut, :])
+
+    result = result_ref[...]
     result = result.astype(BF16).reshape(rows, images, cols, width)
     part = send_ref.shape[2]
     for i in range(send_ref.shape[0]):
@@ -202,49 +201,66 @@
 
 
 def rows_backward_kernel(
-    core_ref, up_ref, ga_ref, gb_ref, w2_hbm, slope_hbm, mid_hbm, w1_hbm, hidden_hbm, att_hbm, wo_hbm,
+    core_ref, up_ref, ga_ref, gb_ref, slope_hbm, hidden_hbm, w2_hbm, mid_hbm, w1_hbm, att_hbm, wo_hbm,
     q_hbm, k_hbm, v_hbm, p_hbm, x_hbm, wq_hbm, wk_hbm, wv_hbm, _,
     mid_grad_ref, dq_ref, dk_ref, dv_ref, keep_ref, send_ref,
-    halves, w2_ref, slope_ref, mid_ref, w1_ref, hidden_ref, att_ref, wo_ref,
-    q_ref, k_ref, v_ref, p_ref, x_ref, wq_ref, wk_ref, wv_ref, done,
+    halves, feed_grad_ref, slope_ref, hidden_ref, w2_ref, mid_ref, w1_ref, att_ref, wo_ref,
+    q_ref, k_ref, v_ref, p_ref, x_ref, wq_ref, wk_ref, wv_ref, done, tile_done,
 ):
     rows, images, cols, width = x_ref.shape
     tokens = rows * images * cols
     features = width // HEADS
     scaling = 1.0 / math.sqrt(features)
     sources = (
-        w2_hbm, slope_hbm, mid_hbm, w1_hbm, hidden_hbm, att_hbm, wo_hbm,
+        w2_hbm, mid_hbm, w1_hbm, att_hbm, wo_hbm,
         q_hbm, k_hbm, v_hbm, p_hbm, x_hbm, wq_hbm, wk_hbm, wv_hbm,
     )
     targets = (
-        w2_ref, slope_ref, mid_ref, w1_ref, hidden_ref, att_ref, wo_ref,
+        w2_ref, mid_ref, w1_ref, att_ref, wo_ref,
         q_ref, k_ref, v_ref, p_ref, x_ref, wq_ref, wk_ref, wv_ref,
     )
     copies = [pltpu.make_async_copy(sources[i], targets[i], done.at[i]) for i in range(len(sources))]
-    for copy in copies:
+    tiles, _, tile = slope_ref.shape
+
+    def tile_copies(j):
+        return (
+            pltpu.make_async_copy(slope_hbm.at[j], slope_ref.at[j], tile_done.at[0, j]),
+            pltpu.make_async_copy(hidden_hbm.at[j], hidden_ref.at[j], tile_done.at[1, j]),
+        )
+
+    for copy in copies[:3]:
+        copy.start()
+    for j in range(tiles):
+        for copy in tile_copies(j):
+            copy.start()
+    for copy in copies[3:]:
         copy.start()
     put = putter(core_ref[0], halves)
     up = jnp.concatenate([up_ref[:, r].reshape(images * cols, width) for r in range(rows)], axis=0).astype(F32)
     up_low = up.astype(BF16)
-    tiles, _, tile = slope_ref.shape
-    copies[0].wait()
-    hidden_grads = [mm_right_t(up_low, w2_ref[j * tile : (j + 1) * tile, :]) for j in range(tiles)]
-    for copy in copies[1:5]:
+    for copy in copies[:3]:
         copy.wait()
     normal_b, inverse_b = normalize(mid_ref[...].reshape(tokens, width))
     normed_b = (normal_b * gb_ref[...]).astype(BF16)
-    normed_grad = None
-    for j in range(tiles):
-        expanded_grad = (slope_ref[j] * hidden_grads[j]).astype(BF16)
+    feed_grad_ref[...] = jnp.zeros_like(feed_grad_ref)
+
+    @pl.loop(0, tiles)
+    def _(j):
+        cut = pl.ds(pl.multiple_of(j * tile, tile), tile)
+        hidden_grad = mm_right_t(up_low, w2_ref[cut, :])
+        for copy in tile_copies(j):
+            copy.wait()
+        expanded_grad = (slope_ref[j] * hidden_grad).astype(BF16)
         put(4 + j, mm_left_t(normed_b, expanded_grad))
         put(4 + tiles + j, mm_left_t(up_low, hidden_ref[j]))
-        part = mm_right_t(expanded_grad, w1_ref[:, j * tile : (j + 1) * tile])
-        normed_grad = part if normed_grad is None else normed_grad + part
+        feed_grad_ref[...] += mm_right_t(expanded_grad, w1_ref[:, cut])
+
+    normed_grad = feed_grad_ref[...]
     middle_norm, scale_grad = normalize_back(normed_grad, normal_b, inverse_b, gb_ref[...])
     middle_grad = up + middle_norm
     mid_grad_ref[...] = middle_grad
     middle_low = middle_grad.astype(BF16)
-    for copy in copies[5:]:
+    for copy in copies[3:]:
         copy.wait()
     put(3, mm_left_t(att_ref[...].reshape(tokens, width), middle_low))
     up_att = mm_right_t(middle_low, wo_ref[...]).astype(BF16)
@@ -310,7 +326,7 @@
 def columns_kernel(
     core_ref, x_ref, up_ref, ga_ref, gb_ref, wq_hbm, wk_hbm, wv_hbm, wo_hbm, w1_hbm, w2_hbm,
     out_ref, grad_ref, keep_ref, send_ref,
-    halves, bias, wq_ref, wk_ref, wv_ref, wo_ref, w1_ref, w2_ref, done,
+    halves, bias, result_ref, feed_grad_ref, wq_ref, wk_ref, wv_ref, wo_ref, w1_ref, w2_ref, done,
 ):
     sources, rows, cols, width = x_ref.shape
     groups = cols // GROUP
@@ -343,8 +359,11 @@
     up_low = up.astype(BF16)
     for copy in copies[4:]:
         copy.wait()
-    result, normed_grad = feed_back(normed_b, up_low, w1_ref, w2_ref, put, 4, True)
-    store_groups(out_ref, middle + result)
+    result_ref[...] = middle
+    feed_grad_ref[...] = jnp.zeros_like(feed_grad_ref)
+    feed_back(normed_b, up_low, w1_ref, w2_ref, put, 4, result_ref, feed_grad_ref)
+    store_groups(out_ref, result_ref[...])
+    normed_grad = feed_grad_ref[...]
     middle_norm, scale_grad = normalize_back(normed_grad, normal_b, inverse_b, gb_ref[...])
     middle_grad = up + middle_norm
     middle_low = middle_grad.astype(BF16)
@@ -426,6 +445,7 @@
         in_specs=[whole(array) for array in operands],
         out_specs=[HELD] + [whole_out(out.shape) for out in outs[1:]],
         out_shape=outs,
+        scratch_shapes=[pltpu.VMEM((rows * images * cols, width), F32)],
         compiler_params=params(48 * 1024 * 1024),
         cost_estimate=cost(),
         name="rows_forward",
@@ -433,8 +453,9 @@
 
 
 def rows_backward(core, up, gains, kept, after):
-    tokens, width = kept[1].shape[1], kept[2].shape[-1]
-    half = grad_rows(width, kept[0].shape[0]) // 2
+    tiles, tokens, _ = kept[0].shape
+    hidden_width, width = kept[2].shape
+    half = grad_rows(width, hidden_width) // 2
     part = held_shape((half + TAIL, width), BF16)
     grad = held_shape((tokens, width), BF16)
     return pl.pallas_call(
@@ -442,9 +463,9 @@
         in_specs=[SCALAR] + [HELD] * 3 + [UNREAD] * (len(kept) + 1),
         out_specs=[HELD] * 6,
         out_shape=[held_shape((tokens, width), F32), grad, grad, grad, part, part],
-        scratch_shapes=[pltpu.VMEM((2, half, width), BF16)]
+        scratch_shapes=[pltpu.VMEM((2, half, width), BF16), pltpu.VMEM((tokens, width), F32)]
         + [pltpu.VMEM(array.shape, array.dtype) for array in kept]
-        + [pltpu.SemaphoreType.DMA((len(kept),))],
+        + [pltpu.SemaphoreType.DMA((len(kept) - 2,)), pltpu.SemaphoreType.DMA((2, tiles))],
         compiler_params=params(48 * 1024 * 1024),
         cost_estimate=cost(),
         name="rows_backward",
@@ -489,6 +510,7 @@
         out_specs=[HELD] * 4,
         out_shape=[held_shape(stream.shape, BF16)] * 2 + [held_shape(part, BF16)] * 2,
         scratch_shapes=[pltpu.VMEM((2, half, width), BF16), pltpu.VMEM((tokens, tokens), F32)]
+        + [pltpu.VMEM((tokens * (cols // GROUP), width), F32)] * 2
         + [pltpu.VMEM(array.shape, array.dtype) for array in matrices]
         + [pltpu.SemaphoreType.DMA((len(matrices),))],
         compiler_params=params(40 * 1024 * 1024),
@@ -724,7 +746,7 @@
     between_grad, final, token = lax.optimization_barrier((between_grad, final, token))
     final = trade(final)
     wq, wk, wv, wo, w1, w2 = matrices[:6]
-    kept = (w2, slope, middle, w1, hidden, attended, wo, query, key, value, probs, inputs, wq, wk, wv)
+    kept = (slope, hidden, w2, middle, w1, attended, wo, query, key, value, probs, inputs, wq, wk, wv)
     *grads, keep, send = rows_backward(core, between_grad, rows_gains, kept, token)
     rows_chain = Chain(exchanges, ((total, kinds),), keep, send, hidden_width)
     token = rows_chain.cut(rows_chain.token)

time: 181 us -> 173 us (0.956)
  starting transfers between devices: 56.6 us -> 47.7 us
  Pallas kernels: 51.9 us -> 55.6 us
    all_to_all x4, starting transfers between devices: 33.2 us -> 23.9 us  [trade(): return lax.all_to_all(array, 'row', 0, 0, tiled=True)]
  transfers between devices with their start and end apart: 24 -> 24, of which waited for: 15 -> 15; matrix products, arithmetic and copies ran while one was open for 0% -> 0% of each run, Pallas kernels for 19% -> 21%
where the time goes in v4:
time: 173 us; the launch traced here: 172 us
  waiting for transfers between devices  65 us (38%)
  Pallas kernels  55.6 us (32%)
  starting transfers between devices  47.7 us (28%)
  local copies, waits for them, and re-layouts  2.78 us (2%)
    ppermute x20, waiting for transfers between devices, swap(): lax.ppermute(array, ALL, [(i, i ^ mask) for i in range(self.devices)])  42 us
    all_to_all x4, starting transfers between devices, trade(): return lax.all_to_all(array, 'row', 0, 0, tiled=True)  23.9 us
    ppermute x20, starting transfers between devices, swap(): lax.ppermute(array, ALL, [(i, i ^ mask) for i in range(self.devices)])  23.8 us
    all_to_all x4, waiting for transfers between devices, trade(): return lax.all_to_all(array, 'row', 0, 0, tiled=True)  23 us
    pallas_call x1, Pallas kernels, columns_both(): pl.pallas_call(columns_kernel, in_specs=[SCALAR] + [HELD] * 4 + [UNREAD]...  17.1 us
    pallas_call x1, Pallas kernels, rows_forward(): pl.pallas_call(rows_forward_kernel, grid=(1,), in_specs=[whole(array) for...  14.4 us
    pallas_call x1, Pallas kernels, rows_backward(): pl.pallas_call(rows_backward_kernel, in_specs=[SCALAR] + [HELD] * 3 + [UN...  13.9 us
    pallas_call x1, Pallas kernels, rows_rest(): pl.pallas_call(rows_rest_kernel, grid=(1,), in_specs=[HELD] * 4 + [whole(...  3.92 us
  transfers between devices with their start and end apart: 24, of which 15 were waited for; matrix products, arithmetic and copies ran while one was open for 0% of the time, Pallas kernels for 21%

profile of v4, /device:TPU:0, one launch (start us, length us, event | category | flops | bytes accessed | tf_op | source)
XLA Modules:
  0.0 171.9 jit_solution(1042231893832739951)
XLA Ops:
  0.7 2.1 %copy.38 = bf16[2,16,48,256]{3,2,0,1:T(8,128)(2,1)} copy(bf16[2,16,48,256]{3,2,1,0:T(8,128)(2,1)} %bitcast.24) | data formatting | bytes 1572864 | tf_op jit(solution)/shard_map/reshape | solution.py:734
  2.7 7.4 %all-to-all-start = ((bf16[16,2,48,256]{3,2,1,0:T(8,128)(2,1)}), bf16[16,2,48,256]{3,2,1,0:T(8,128)(2,1)S(1)}, u32[]{:S(2)}, u32[]{:S(2)}) async-start(bf16[16,2,48,256]{3,2,1,0:T(8,128)(2,1)} %bitcast.15), calls=%async_computation | async-start | bytes 1572864 | tf_op jit(solution)/shard_map/all_to_all | solution.py:729
  10.2 14.4 %rows_forward.1 = (bf16[16,2,48,256]{3,2,1,0:T(8,128)(2,1)}, bf16[2,8,96,256]{3,2,1,0:T(8,128)(2,1)}, bf16[2,8,96,256]{3,2,1,0:T(8,128)(2,1)}, bf16[2,8,96,256]{...) custom-call(bf16[2,8,96,256]{3,2,1,0:T(8,128)(2,1)} %x_ref.3, ...), custom_call_target="tpu_custom_call" | custom-call | flops 1 | bytes 1 | tf_op jit(solution)/shard_map/rows_forward/pallas_call | solution.py:442
  24.5 4.3 %all-to-all-done.up_ref = bf16[16,2,48,256]{3,2,1,0:T(8,128)(2,1)S(1)} async-done(((bf16[16,2,48,256]{3,2,1,0:T(8,128)(2,1)}), bf16[16,2,48,256]{3,2,1,0:T(8,128)(2,1)S(1)}, u32[]{:S(2)}, u32[]{:S(2)}) %all-to-all-start) | async-done | bytes 786464 | tf_op jit(solution)/shard_map/all_to_all | solution.py:729
  28.8 5.5 %all-to-all-start.1 = ((bf16[16,2,48,256]{3,2,1,0:T(8,128)(2,1)}), bf16[16,2,48,256]{3,2,1,0:T(8,128)(2,1)S(1)}, u32[]{:S(2)}, u32[]{:S(2)}) async-start(bf16[16,2,48,256]{3,2,1,0:T(8,128)(2,1)} %get-tuple-element.76), calls=%async_computation.1 | async-start | bytes 1572864 | tf_op jit(solution)/shard_map/all_to_all | solution.py:729
  34.3 18.7 %all-to-all-done.1.x_ref = bf16[16,2,48,256]{3,2,1,0:T(8,128)(2,1)S(1)} async-done(((bf16[16,2,48,256]{3,2,1,0:T(8,128)(2,1)}), bf16[16,2,48,256]{3,2,1,0:T(8,128)(2,1)S(1)}, u32[]{:S(2)}, u32[]{:S(2)}) %all-to-all-start.1) | async-done | bytes 786464 | tf_op jit(solution)/shard_map/all_to_all | solution.py:729
  53.0 17.1 %columns_both.1 = (bf16[16,2,48,256]{3,2,1,0:T(8,128)(2,1)}, bf16[16,2,48,256]{3,2,1,0:T(8,128)(2,1)}, bf16[1552,256]{1,0:T(8,128)(2,1)S(1)}, bf16[1552,256]{1,0:T(8,128)(2,1)S(1)}) custom-call(s32[1]{0:T(128)} %bitcast.core_ref.at_ref, bf16[16,2,48,256]{3,2,1,0:T(8,128)(2,1)S(1)} %all-to-all-done.1.x_ref, bf16[16,2,48,256]{3,2,1,0:T(8,128)(2,1)S(1)} %all-to-all-done.up_ref, ...), custom_call_target="tpu_custom_call" | custom-call | flops 1 | bytes 1 | tf_op jit(solution)/shard_map/columns_both/pallas_call | solution.py:507
  70.2 5.5 %all-to-all-start.2 = ((bf16[16,2,48,256]{3,2,1,0:T(8,128)(2,1)}), bf16[16,2,48,256]{3,2,1,0:T(8,128)(2,1)S(1)}, u32[]{:S(2)}, u32[]{:S(2)}) async-start(bf16[16,2,48,256]{3,2,1,0:T(8,128)(2,1)} %get-tuple-element.78), calls=%async_computation.2 | async-start | bytes 1572864 | tf_op jit(solution)/shard_map/all_to_all | solution.py:729
  76.1 2.0 %collective-permute-done.refs_1_ = bf16[1552,256]{1,0:T(8,128)(2,1)S(1)} collective-permute-done((bf16[1552,256]{1,0:T(8,128)(2,1)S(1)}, bf16[1552,256]{1,0:T(8,128)(2,1)S(1)}, u32[]{:S(2)}, u32[]{:S(2)}) %collective-permute-start) | collective-permute-done | bytes 794656 | tf_op jit(solution)/shard_map/ppermute | solution.py:665
  82.0 4.4 %collective-permute-done.1.refs_1_ = bf16[400,256]{1,0:T(8,128)(2,1)S(1)} collective-permute-done((bf16[400,256]{1,0:T(8,128)(2,1)S(1)}, bf16[400,256]{1,0:T(8,128)(2,1)S(1)}, u32[]{:S(2)}, u32[]{:S(2)}) %collective-permute-start.1) | collective-permute-done | bytes 204832 | tf_op jit(solution)/shard_map/ppermute | solution.py:665
  86.4 9.7 %collective-permute-done.2.refs_2_ = bf16[400,256]{1,0:T(8,128)(2,1)S(1)} collective-permute-done((bf16[400,256]{1,0:T(8,128)(2,1)S(1)}, bf16[400,256]{1,0:T(8,128)(2,1)S(1)}, u32[]{:S(2)}, u32[]{:S(2)}) %collective-permute-start.2) | collective-permute-done | bytes 204832 | tf_op jit(solution)/shard_map/ppermute | solution.py:665
  96.9 5.5 %all-to-all-start.3 = ((bf16[16,2,48,256]{3,2,1,0:T(8,128)(2,1)}), bf16[16,2,48,256]{3,2,1,0:T(8,128)(2,1)S(1)}, u32[]{:S(2)}, u32[]{:S(2)}) async-start(bf16[16,2,48,256]{3,2,1,0:T(8,128)(2,1)} %get-tuple-element.86), calls=%async_computation.3 | async-start | bytes 1572864 | tf_op jit(solution)/shard_map/all_to_all | solution.py:729
  102.5 13.9 %rows_backward.1 = (f32[1536,256]{1,0:T(8,128)S(1)}, bf16[1536,256]{1,0:T(8,128)(2,1)S(1)}, bf16[1536,256]{1,0:T(8,128)(2,1)S(1)}, bf16[1536,256]{1,0:T(8,128)(2...) custom-call(s32[1]{0:T(128)} %bitcast.core_ref.at_ref, ...), custom_call_target="tpu_custom_call" | custom-call | flops 1 | bytes 1 | tf_op jit(solution)/shard_map/rows_backward/pallas_call | solution.py:461
  122.8 3.9 %rows_rest.1 = (f32[2,8,96,256]{3,2,1,0:T(8,128)}, f32[8,128]{1,0:T(8,128)S(1)}) custom-call(f32[1536,256]{1,0:T(8,128)S(1)} %get-tuple-element.97.mid_grad_ref, bf16[1536,256]{1,0:T(8,128)(2,1)S(1)} %get-tuple-element.98.dq_ref, bf16[1536,256]{1,0:T(8,128)(2,1)S(1)} %get-tuple-element.99.dk_ref, bf16[1536,256]{1,0:T(8,128)(2,1)S(1)} %get-tuple-element.100.dv_ref, ...), custom_call_target="tpu_custom_call" | custom-call | flops 1 | bytes 1 | tf_op jit(solution)/shard_map/rows_rest/pallas_call | solution.py:477
  126.8 2.8 %collective-permute-start.10 = (bf16[400,256]{1,0:T(8,128)(2,1)S(1)}, bf16[400,256]{1,0:T(8,128)(2,1)S(1)}, u32[]{:S(2)}, u32[]{:S(2)}) collective-permute-start(bf16[400,256]{1,0:T(8,128)(2,1)S(1)} %sum_split.9._.refs_0_), channel_id=1, source_target_pairs={{0,8},{1,9},{2,10},{3,11},{4,12},{5,13},{6,14},{7,15},{8,0},{9,1},... | collective-permute-start | bytes 614408 | tf_op jit(solution)/shard_map/ppermute | solution.py:665
  133.8 4.9 %collective-permute-done.10.refs_1_ = bf16[400,256]{1,0:T(8,128)(2,1)S(1)} collective-permute-done((bf16[400,256]{1,0:T(8,128)(2,1)S(1)}, bf16[400,256]{1,0:T(8,128)(2,1)S(1)}, u32[]{:S(2)}, u32[]{:S(2)}) %collective-permute-start.10) | collective-permute-done | bytes 204832 | tf_op jit(solution)/shard_map/ppermute | solution.py:665
  138.8 3.0 %collective-permute-done.9.refs_1_ = bf16[400,256]{1,0:T(8,128)(2,1)S(1)} collective-permute-done((bf16[400,256]{1,0:T(8,128)(2,1)S(1)}, bf16[400,256]{1,0:T(8,128)(2,1)S(1)}, u32[]{:S(2)}, u32[]{:S(2)}) %collective-permute-start.9) | collective-permute-done | bytes 204832 | tf_op jit(solution)/shard_map/ppermute | solution.py:665
  141.8 2.5 %collective-permute-start.11 = (bf16[400,256]{1,0:T(8,128)(2,1)S(1)}, bf16[400,256]{1,0:T(8,128)(2,1)S(1)}, u32[]{:S(2)}, u32[]{:S(2)}) collective-permute-start(bf16[400,256]{1,0:T(8,128)(2,1)S(1)} %sum_split.11.refs_0_.refs_2_), channel_id=1, source_target_pairs={{0,8},{1,9},{2,10},{3,11},{4,12},{5,13},{6,14},{7,15},{8,0},{9,1},... | collective-permute-start | bytes 614408 | tf_op jit(solution)/shard_map/ppermute | solution.py:665
  147.8 5.8 %collective-permute-done.11.refs_1_ = bf16[400,256]{1,0:T(8,128)(2,1)S(1)} collective-permute-done((bf16[400,256]{1,0:T(8,128)(2,1)S(1)}, bf16[400,256]{1,0:T(8,128)(2,1)S(1)}, u32[]{:S(2)}, u32[]{:S(2)}) %collective-permute-start.11) | collective-permute-done | bytes 204832 | tf_op jit(solution)/shard_map/ppermute | solution.py:665
  158.7 1.9 %finish.2 = (f32[1,256]{1,0:T(1,128)}, f32[256,256]{1,0:T(8,128)}, f32[256,256]{1,0:T(8,128)}, f32[256,256]{1,0:T(8,128)}, f32[256,256]{1,0:T(8,128)}, /*index=5...) custom-call(s32[1]{0:T(128)} %bitcast.core_ref.at_ref, ...), custom_call_target="tpu_custom_call" | custom-call | flops 1 | bytes 1 | tf_op jit(solution)/shard_map/finish/pallas_call | solution.py:637
  160.6 3.2 %collective-permute-done.14.refs_3_ = bf16[384,256]{1,0:T(8,128)(2,1)S(1)} collective-permute-done((bf16[384,256]{1,0:T(8,128)(2,1)S(1)}, bf16[384,256]{1,0:T(8,128)(2,1)S(1)}, u32[]{:S(2)}, u32[]{:S(2)}) %collective-permute-start.14) | collective-permute-done | bytes 196640 | tf_op jit(solution)/shard_map/ppermute | solution.py:665
  163.8 3.7 %collective-permute-done.13.refs_2_ = bf16[384,256]{1,0:T(8,128)(2,1)S(1)} collective-permute-done((bf16[384,256]{1,0:T(8,128)(2,1)S(1)}, bf16[384,256]{1,0:T(8,128)(2,1)S(1)}, u32[]{:S(2)}, u32[]{:S(2)}) %collective-permute-start.13) | collective-permute-done | bytes 196640 | tf_op jit(solution)/shard_map/ppermute | solution.py:665
  167.7 2.2 %collective-permute-done.19.other_ref = bf16[1536,256]{1,0:T(8,128)(2,1)S(1)} collective-permute-done((bf16[1536,256]{1,0:T(8,128)(2,1)S(1)}, bf16[1536,256]{1,0:T(8,128)(2,1)S(1)}, u32[]{:S(2)}, u32[]{:S(2)}) %collective-permute-start.19) | collective-permute-done | bytes 786464 | tf_op jit(solution)/shard_map/ppermute | solution.py:665
  170.0 1.9 %finish.3 = (f32[1,256]{1,0:T(1,128)}, f32[256,256]{1,0:T(8,128)}, f32[256,256]{1,0:T(8,128)}, f32[256,256]{1,0:T(8,128)}, f32[256,256]{1,0:T(8,128)}, /*index=5...) custom-call(s32[1]{0:T(128)} %bitcast.core_ref.at_ref, ...), custom_call_target="tpu_custom_call" | custom-call | flops 1 | bytes 1 | tf_op jit(solution)/shard_map/finish/pallas_call | solution.py:637
  (50 shorter events, 24.7 us)
Async XLA Ops:
  2.7 26.1 %all-to-all-start = ((bf16[16,2,48,256]{3,2,1,0:T(8,128)(2,1)}), bf16[16,2,48,256]{3,2,1,0:T(8,128)(2,1)S(1)}, u32[]{:S(2)}, u32[]{:S(2)}) async-start(bf16[16,2,48,256]{3,2,1,0:T(8,128)(2,1)} %bitcast.15), calls=%async_computation | async-start | bytes 1572864 | tf_op jit(solution)/shard_map/all_to_all | solution.py:729
  28.8 24.2 %all-to-all-start.1 = ((bf16[16,2,48,256]{3,2,1,0:T(8,128)(2,1)}), bf16[16,2,48,256]{3,2,1,0:T(8,128)(2,1)S(1)}, u32[]{:S(2)}, u32[]{:S(2)}) async-start(bf16[16,2,48,256]{3,2,1,0:T(8,128)(2,1)} %get-tuple-element.76), calls=%async_computation.1 | async-start | bytes 1572864 | tf_op jit(solution)/shard_map/all_to_all | solution.py:729
  70.2 26.8 %all-to-all-start.2 = ((bf16[16,2,48,256]{3,2,1,0:T(8,128)(2,1)}), bf16[16,2,48,256]{3,2,1,0:T(8,128)(2,1)S(1)}, u32[]{:S(2)}, u32[]{:S(2)}) async-start(bf16[16,2,48,256]{3,2,1,0:T(8,128)(2,1)} %get-tuple-element.78), calls=%async_computation.2 | async-start | bytes 1572864 | tf_op jit(solution)/shard_map/all_to_all | solution.py:729
  75.7 2.4 %collective-permute-start = (bf16[1552,256]{1,0:T(8,128)(2,1)S(1)}, bf16[1552,256]{1,0:T(8,128)(2,1)S(1)}, u32[]{:S(2)}, u32[]{:S(2)}) collective-permute-start(bf16[1552,256]{1,0:T(8,128)(2,1)S(1)} %get-tuple-element.81), channel_id=1, source_target_pairs={{0,1},{1,0},{2,3},{3,2},{4,5},{5,4},{6,7},{7,6},{8,9},{9,8},{10,11... | collective-permute-start | bytes 2383880 | tf_op jit(solution)/shard_map/ppermute | solution.py:665
  78.5 8.0 %collective-permute-start.1 = (bf16[400,256]{1,0:T(8,128)(2,1)S(1)}, bf16[400,256]{1,0:T(8,128)(2,1)S(1)}, u32[]{:S(2)}, u32[]{:S(2)}) collective-permute-start(bf16[400,256]{1,0:T(8,128)(2,1)S(1)} %get-tuple-element.83), channel_id=1, source_target_pairs={{0,16},{1,17},{2,18},{3,19},{4,20},{5,21},{6,22},{7,23},{8,24},{9,... | collective-permute-start | bytes 614408 | tf_op jit(solution)/shard_map/ppermute | solution.py:665
  80.0 16.1 %collective-permute-start.2 = (bf16[400,256]{1,0:T(8,128)(2,1)S(1)}, bf16[400,256]{1,0:T(8,128)(2,1)S(1)}, u32[]{:S(2)}, u32[]{:S(2)}) collective-permute-start(bf16[400,256]{1,0:T(8,128)(2,1)S(1)} %get-tuple-element.84), channel_id=1, source_target_pairs={{0,2},{1,3},{2,0},{3,1},{4,6},{5,7},{6,4},{7,5},{8,10},{9,11},{10,... | collective-permute-start | bytes 614408 | tf_op jit(solution)/shard_map/ppermute | solution.py:665
  81.9 14.2 %collective-permute-start.3 = (bf16[400,256]{1,0:T(8,128)(2,1)S(1)}, bf16[400,256]{1,0:T(8,128)(2,1)S(1)}, u32[]{:S(2)}, u32[]{:S(2)}) collective-permute-start(bf16[400,256]{1,0:T(8,128)(2,1)S(1)} %get-tuple-element.85), channel_id=1, source_target_pairs={{0,18},{1,19},{2,16},{3,17},{4,22},{5,23},{6,20},{7,21},{8,26},{9,... | collective-permute-start | bytes 614408 | tf_op jit(solution)/shard_map/ppermute | solution.py:665
  96.9 32.7 %all-to-all-start.3 = ((bf16[16,2,48,256]{3,2,1,0:T(8,128)(2,1)}), bf16[16,2,48,256]{3,2,1,0:T(8,128)(2,1)S(1)}, u32[]{:S(2)}, u32[]{:S(2)}) async-start(bf16[16,2,48,256]{3,2,1,0:T(8,128)(2,1)} %get-tuple-element.86), calls=%async_computation.3 | async-start | bytes 1572864 | tf_op jit(solution)/shard_map/all_to_all | solution.py:729
  116.4 2.4 %collective-permute-start.5 = (bf16[1552,256]{1,0:T(8,128)(2,1)S(1)}, bf16[1552,256]{1,0:T(8,128)(2,1)S(1)}, u32[]{:S(2)}, u32[]{:S(2)}) collective-permute-start(bf16[1552,256]{1,0:T(8,128)(2,1)S(1)} %get-tuple-element.102), channel_id=1, source_target_pairs={{0,1},{1,0},{2,3},{3,2},{4,5},{5,4},{6,7},{7,6},{8,9},{9,8},{10,11... | collective-permute-start | bytes 2383880 | tf_op jit(solution)/shard_map/ppermute | solution.py:665
  116.8 9.9 %collective-permute-start.4 = (bf16[400,256]{1,0:T(8,128)(2,1)S(1)}, bf16[400,256]{1,0:T(8,128)(2,1)S(1)}, u32[]{:S(2)}, u32[]{:S(2)}) collective-permute-start(bf16[400,256]{1,0:T(8,128)(2,1)S(1)} %copy-done.1), channel_id=1, source_target_pairs={{0,4},{1,5},{2,6},{3,7},{4,0},{5,1},{6,2},{7,3},{8,12},{9,13},{10,... | collective-permute-start | bytes 614408 | tf_op jit(solution)/shard_map/ppermute | solution.py:665
  119.2 11.4 %collective-permute-start.6 = (bf16[400,256]{1,0:T(8,128)(2,1)S(1)}, bf16[400,256]{1,0:T(8,128)(2,1)S(1)}, u32[]{:S(2)}, u32[]{:S(2)}) collective-permute-start(bf16[400,256]{1,0:T(8,128)(2,1)S(1)} %get-tuple-element.107), channel_id=1, source_target_pairs={{0,16},{1,17},{2,18},{3,19},{4,20},{5,21},{6,22},{7,23},{8,24},{9,... | collective-permute-start | bytes 614408 | tf_op jit(solution)/shard_map/ppermute | solution.py:665
  120.0 10.7 %collective-permute-start.7 = (bf16[400,256]{1,0:T(8,128)(2,1)S(1)}, bf16[400,256]{1,0:T(8,128)(2,1)S(1)}, u32[]{:S(2)}, u32[]{:S(2)}) collective-permute-start(bf16[400,256]{1,0:T(8,128)(2,1)S(1)} %get-tuple-element.108), channel_id=1, source_target_pairs={{0,2},{1,3},{2,0},{3,1},{4,6},{5,7},{6,4},{7,5},{8,10},{9,11},{10,... | collective-permute-start | bytes 614408 | tf_op jit(solution)/shard_map/ppermute | solution.py:665
  121.9 10.2 %collective-permute-start.8 = (bf16[400,256]{1,0:T(8,128)(2,1)S(1)}, bf16[400,256]{1,0:T(8,128)(2,1)S(1)}, u32[]{:S(2)}, u32[]{:S(2)}) collective-permute-start(bf16[400,256]{1,0:T(8,128)(2,1)S(1)} %get-tuple-element.109), channel_id=1, source_target_pairs={{0,18},{1,19},{2,16},{3,17},{4,22},{5,23},{6,20},{7,21},{8,26},{9,... | collective-permute-start | bytes 614408 | tf_op jit(solution)/shard_map/ppermute | solution.py:665
  126.8 12.0 %collective-permute-start.10 = (bf16[400,256]{1,0:T(8,128)(2,1)S(1)}, bf16[400,256]{1,0:T(8,128)(2,1)S(1)}, u32[]{:S(2)}, u32[]{:S(2)}) collective-permute-start(bf16[400,256]{1,0:T(8,128)(2,1)S(1)} %sum_split.9._.refs_0_), channel_id=1, source_target_pairs={{0,8},{1,9},{2,10},{3,11},{4,12},{5,13},{6,14},{7,15},{8,0},{9,1},... | collective-permute-start | bytes 614408 | tf_op jit(solution)/shard_map/ppermute | solution.py:665
  132.2 9.5 %collective-permute-start.9 = (bf16[400,256]{1,0:T(8,128)(2,1)S(1)}, bf16[400,256]{1,0:T(8,128)(2,1)S(1)}, u32[]{:S(2)}, u32[]{:S(2)}) collective-permute-start(bf16[400,256]{1,0:T(8,128)(2,1)S(1)} %sum_split.10.refs_2_.refs_0_), channel_id=1, source_target_pairs={{0,4},{1,5},{2,6},{3,7},{4,0},{5,1},{6,2},{7,3},{8,12},{9,13},{10,... | collective-permute-start | bytes 614408 | tf_op jit(solution)/shard_map/ppermute | solution.py:665
  141.8 11.8 %collective-permute-start.11 = (bf16[400,256]{1,0:T(8,128)(2,1)S(1)}, bf16[400,256]{1,0:T(8,128)(2,1)S(1)}, u32[]{:S(2)}, u32[]{:S(2)}) collective-permute-start(bf16[400,256]{1,0:T(8,128)(2,1)S(1)} %sum_split.11.refs_0_.refs_2_), channel_id=1, source_target_pairs={{0,8},{1,9},{2,10},{3,11},{4,12},{5,13},{6,14},{7,15},{8,0},{9,1},... | collective-permute-start | bytes 614408 | tf_op jit(solution)/shard_map/ppermute | solution.py:665
  144.4 9.3 %collective-permute-start.17 = (bf16[384,256]{1,0:T(8,128)(2,1)S(1)}, bf16[384,256]{1,0:T(8,128)(2,1)S(1)}, u32[]{:S(2)}, u32[]{:S(2)}) collective-permute-start(bf16[384,256]{1,0:T(8,128)(2,1)S(1)} %get-tuple-element.111.refs_2_.refs_0_), channel_id=1, source_target_pairs={{0,18},{1,19},{2,16},{3,17},{4,22},{5,23},{6,20},{7,21},{8,26},{9,... | collective-permute-start | bytes 589832 | tf_op jit(solution)/shard_map/ppermute | solution.py:665
  145.1 9.8 %collective-permute-start.16 = (bf16[384,256]{1,0:T(8,128)(2,1)S(1)}, bf16[384,256]{1,0:T(8,128)(2,1)S(1)}, u32[]{:S(2)}, u32[]{:S(2)}) collective-permute-start(bf16[384,256]{1,0:T(8,128)(2,1)S(1)} %get-tuple-element.111.refs_2_.refs_0_), channel_id=1, source_target_pairs={{0,2},{1,3},{2,0},{3,1},{4,6},{5,7},{6,4},{7,5},{8,10},{9,11},{10,... | collective-permute-start | bytes 589832 | tf_op jit(solution)/shard_map/ppermute | solution.py:665
  146.6 8.4 %collective-permute-start.15 = (bf16[384,256]{1,0:T(8,128)(2,1)S(1)}, bf16[384,256]{1,0:T(8,128)(2,1)S(1)}, u32[]{:S(2)}, u32[]{:S(2)}) collective-permute-start(bf16[384,256]{1,0:T(8,128)(2,1)S(1)} %get-tuple-element.111.refs_2_.refs_0_), channel_id=1, source_target_pairs={{0,16},{1,17},{2,18},{3,19},{4,20},{5,21},{6,22},{7,23},{8,24},{9,... | collective-permute-start | bytes 589832 | tf_op jit(solution)/shard_map/ppermute | solution.py:665
  155.1 3.6 %collective-permute-start.18 = (bf16[1536,256]{1,0:T(8,128)(2,1)S(1)}, bf16[1536,256]{1,0:T(8,128)(2,1)S(1)}, u32[]{:S(2)}, u32[]{:S(2)}) collective-permute-start(bf16[1536,256]{1,0:T(8,128)(2,1)S(1)} %bitcast.16), channel_id=1, source_target_pairs={{0,1},{1,0},{2,3},{3,2},{4,5},{5,4},{6,7},{7,6},{8,9},{9,8},{10,11... | collective-permute-start | bytes 2359304 | tf_op jit(solution)/shard_map/ppermute | solution.py:665
  155.1 8.7 %collective-permute-start.14 = (bf16[384,256]{1,0:T(8,128)(2,1)S(1)}, bf16[384,256]{1,0:T(8,128)(2,1)S(1)}, u32[]{:S(2)}, u32[]{:S(2)}) collective-permute-start(bf16[384,256]{1,0:T(8,128)(2,1)S(1)} %get-tuple-element.112.refs_4_.refs_0_), channel_id=1, source_target_pairs={{0,18},{1,19},{2,16},{3,17},{4,22},{5,23},{6,20},{7,21},{8,26},{9,... | collective-permute-start | bytes 589832 | tf_op jit(solution)/shard_map/ppermute | solution.py:665
  156.7 10.9 %collective-permute-start.13 = (bf16[384,256]{1,0:T(8,128)(2,1)S(1)}, bf16[384,256]{1,0:T(8,128)(2,1)S(1)}, u32[]{:S(2)}, u32[]{:S(2)}) collective-permute-start(bf16[384,256]{1,0:T(8,128)(2,1)S(1)} %get-tuple-element.112.refs_4_.refs_0_), channel_id=1, source_target_pairs={{0,2},{1,3},{2,0},{3,1},{4,6},{5,7},{6,4},{7,5},{8,10},{9,11},{10,... | collective-permute-start | bytes 589832 | tf_op jit(solution)/shard_map/ppermute | solution.py:665
  157.9 9.7 %collective-permute-start.12 = (bf16[384,256]{1,0:T(8,128)(2,1)S(1)}, bf16[384,256]{1,0:T(8,128)(2,1)S(1)}, u32[]{:S(2)}, u32[]{:S(2)}) collective-permute-start(bf16[384,256]{1,0:T(8,128)(2,1)S(1)} %get-tuple-element.112.refs_4_.refs_0_), channel_id=1, source_target_pairs={{0,16},{1,17},{2,18},{3,19},{4,20},{5,21},{6,22},{7,23},{8,24},{9,... | collective-permute-start | bytes 589832 | tf_op jit(solution)/shard_map/ppermute | solution.py:665
  167.6 2.4 %collective-permute-start.19 = (bf16[1536,256]{1,0:T(8,128)(2,1)S(1)}, bf16[1536,256]{1,0:T(8,128)(2,1)S(1)}, u32[]{:S(2)}, u32[]{:S(2)}) collective-permute-start(bf16[1536,256]{1,0:T(8,128)(2,1)S(1)} %bitcast.19), channel_id=1, source_target_pairs={{0,1},{1,0},{2,3},{3,2},{4,5},{5,4},{6,7},{7,6},{8,9},{9,8},{10,11... | collective-permute-start | bytes 2359304 | tf_op jit(solution)/shard_map/ppermute | solution.py:665
  (4 other events, 100.8 us)

commit v5 on v4

--- a/solution.py
+++ b/solution.py
@@ -201,10 +201,10 @@
 
 
 def rows_backward_kernel(
-    core_ref, up_ref, ga_ref, gb_ref, slope_hbm, hidden_hbm, w2_hbm, mid_hbm, w1_hbm, att_hbm, wo_hbm,
+    core_ref, up_ref, slope_hbm, hidden_hbm, w2_hbm, mid_hbm, w1_hbm, ga_hbm, gb_hbm, att_hbm, wo_hbm,
     q_hbm, k_hbm, v_hbm, p_hbm, x_hbm, wq_hbm, wk_hbm, wv_hbm, _,
     mid_grad_ref, dq_ref, dk_ref, dv_ref, keep_ref, send_ref,
-    halves, feed_grad_ref, slope_ref, hidden_ref, w2_ref, mid_ref, w1_ref, att_ref, wo_ref,
+    halves, feed_grad_ref, slope_ref, hidden_ref, w2_ref, mid_ref, w1_ref, ga_ref, gb_ref, att_ref, wo_ref,
     q_ref, k_ref, v_ref, p_ref, x_ref, wq_ref, wk_ref, wv_ref, done, tile_done,
 ):
     rows, images, cols, width = x_ref.shape
@@ -212,11 +212,11 @@
     features = width // HEADS
     scaling = 1.0 / math.sqrt(features)
     sources = (
-        w2_hbm, mid_hbm, w1_hbm, att_hbm, wo_hbm,
+        w2_hbm, mid_hbm, w1_hbm, ga_hbm, gb_hbm, att_hbm, wo_hbm,
         q_hbm, k_hbm, v_hbm, p_hbm, x_hbm, wq_hbm, wk_hbm, wv_hbm,
     )
     targets = (
-        w2_ref, mid_ref, w1_ref, att_ref, wo_ref,
+        w2_ref, mid_ref, w1_ref, ga_ref, gb_ref, att_ref, wo_ref,
         q_ref, k_ref, v_ref, p_ref, x_ref, wq_ref, wk_ref, wv_ref,
     )
     copies = [pltpu.make_async_copy(sources[i], targets[i], done.at[i]) for i in range(len(sources))]
@@ -228,17 +228,17 @@
             pltpu.make_async_copy(hidden_hbm.at[j], hidden_ref.at[j], tile_done.at[1, j]),
         )
 
-    for copy in copies[:3]:
+    for copy in copies[:5]:
         copy.start()
     for j in range(tiles):
         for copy in tile_copies(j):
             copy.start()
-    for copy in copies[3:]:
+    for copy in copies[5:]:
         copy.start()
     put = putter(core_ref[0], halves)
     up = jnp.concatenate([up_ref[:, r].reshape(images * cols, width) for r in range(rows)], axis=0).astype(F32)
     up_low = up.astype(BF16)
-    for copy in copies[:3]:
+    for copy in copies[:5]:
         copy.wait()
     normal_b, inverse_b = normalize(mid_ref[...].reshape(tokens, width))
     normed_b = (normal_b * gb_ref[...]).astype(BF16)
@@ -260,7 +260,7 @@
     middle_grad = up + middle_norm
     mid_grad_ref[...] = middle_grad
     middle_low = middle_grad.astype(BF16)
-    for copy in copies[3:]:
+    for copy in copies[5:]:
         copy.wait()
     put(3, mm_left_t(att_ref[...].reshape(tokens, width), middle_low))
     up_att = mm_right_t(middle_low, wo_ref[...]).astype(BF16)
@@ -452,7 +452,7 @@
     )(*operands)
 
 
-def rows_backward(core, up, gains, kept, after):
+def rows_backward(core, up, kept, after):
     tiles, tokens, _ = kept[0].shape
     hidden_width, width = kept[2].shape
     half = grad_rows(width, hidden_width) // 2
@@ -460,7 +460,7 @@
     grad = held_shape((tokens, width), BF16)
     return pl.pallas_call(
         rows_backward_kernel,
-        in_specs=[SCALAR] + [HELD] * 3 + [UNREAD] * (len(kept) + 1),
+        in_specs=[SCALAR, HELD] + [UNREAD] * (len(kept) + 1),
         out_specs=[HELD] * 6,
         out_shape=[held_shape((tokens, width), F32), grad, grad, grad, part, part],
         scratch_shapes=[pltpu.VMEM((2, half, width), BF16), pltpu.VMEM((tokens, width), F32)]
@@ -469,7 +469,7 @@
         compiler_params=params(48 * 1024 * 1024),
         cost_estimate=cost(),
         name="rows_backward",
-    )(core, held(up), *gains, *[stored(array) for array in kept], after)
+    )(core, held(up), *[stored(array) for array in kept], after)
 
 
 def rows_rest(grads, inputs, gain, matrices, after):
@@ -746,8 +746,8 @@
     between_grad, final, token = lax.optimization_barrier((between_grad, final, token))
     final = trade(final)
     wq, wk, wv, wo, w1, w2 = matrices[:6]
-    kept = (slope, hidden, w2, middle, w1, attended, wo, query, key, value, probs, inputs, wq, wk, wv)
-    *grads, keep, send = rows_backward(core, between_grad, rows_gains, kept, token)
+    kept = (slope, hidden, w2, middle, w1, *rows_gains, attended, wo, query, key, value, probs, inputs, wq, wk, wv)
+    *grads, keep, send = rows_backward(core, between_grad, kept, token)
     rows_chain = Chain(exchanges, ((total, kinds),), keep, send, hidden_width)
     token = rows_chain.cut(rows_chain.token)
     stream_grad, token = rows_rest(grads, inputs, rows_gains[0], (wq, wk, wv), token)

time: 173 us -> 172 us (level)
  no operation moved by 1% of the time
where the time goes in v5:
time: 172 us; the launch traced here: 171 us
  waiting for transfers between devices  65.1 us (38%)
  Pallas kernels  54.9 us (32%)
  starting transfers between devices  47.6 us (28%)
  local copies, waits for them, and re-layouts  2.78 us (2%)
    ppermute x20, waiting for transfers between devices, swap(): lax.ppermute(array, ALL, [(i, i ^ mask) for i in range(self.devices)])  42.1 us
    all_to_all x4, starting transfers between devices, trade(): return lax.all_to_all(array, 'row', 0, 0, tiled=True)  23.9 us
    ppermute x20, starting transfers between devices, swap(): lax.ppermute(array, ALL, [(i, i ^ mask) for i in range(self.devices)])  23.8 us
    all_to_all x4, waiting for transfers between devices, trade(): return lax.all_to_all(array, 'row', 0, 0, tiled=True)  23 us
    pallas_call x1, Pallas kernels, columns_both(): pl.pallas_call(columns_kernel, in_specs=[SCALAR] + [HELD] * 4 + [UNREAD]...  17.1 us
    pallas_call x1, Pallas kernels, rows_forward(): pl.pallas_call(rows_forward_kernel, grid=(1,), in_specs=[whole(array) for...  14.4 us
    pallas_call x1, Pallas kernels, rows_backward(): pl.pallas_call(rows_backward_kernel, in_specs=[SCALAR, HELD] + [UNREAD] *...  13.2 us
    pallas_call x1, Pallas kernels, rows_rest(): pl.pallas_call(rows_rest_kernel, grid=(1,), in_specs=[HELD] * 4 + [whole(...  3.92 us
  transfers between devices with their start and end apart: 24, of which 15 were waited for; matrix products, arithmetic and copies ran while one was open for 0% of the time, Pallas kernels for 21%

profile of v5, /device:TPU:0, one launch (start us, length us, event | category | flops | bytes accessed | tf_op | source)
XLA Modules:
  0.0 171.3 jit_solution(7779262501975969111)
XLA Ops:
  0.7 2.1 %copy.38 = bf16[2,16,48,256]{3,2,0,1:T(8,128)(2,1)} copy(bf16[2,16,48,256]{3,2,1,0:T(8,128)(2,1)} %bitcast.24) | data formatting | bytes 1572864 | tf_op jit(solution)/shard_map/reshape | solution.py:734
  2.7 7.4 %all-to-all-start = ((bf16[16,2,48,256]{3,2,1,0:T(8,128)(2,1)}), bf16[16,2,48,256]{3,2,1,0:T(8,128)(2,1)S(1)}, u32[]{:S(2)}, u32[]{:S(2)}) async-start(bf16[16,2,48,256]{3,2,1,0:T(8,128)(2,1)} %bitcast.15), calls=%async_computation | async-start | bytes 1572864 | tf_op jit(solution)/shard_map/all_to_all | solution.py:729
  10.2 14.4 %rows_forward.1 = (bf16[16,2,48,256]{3,2,1,0:T(8,128)(2,1)}, bf16[2,8,96,256]{3,2,1,0:T(8,128)(2,1)}, bf16[2,8,96,256]{3,2,1,0:T(8,128)(2,1)}, bf16[2,8,96,256]{...) custom-call(bf16[2,8,96,256]{3,2,1,0:T(8,128)(2,1)} %x_ref.3, ...), custom_call_target="tpu_custom_call" | custom-call | flops 1 | bytes 1 | tf_op jit(solution)/shard_map/rows_forward/pallas_call | solution.py:442
  24.5 4.3 %all-to-all-done.up_ref = bf16[16,2,48,256]{3,2,1,0:T(8,128)(2,1)S(1)} async-done(((bf16[16,2,48,256]{3,2,1,0:T(8,128)(2,1)}), bf16[16,2,48,256]{3,2,1,0:T(8,128)(2,1)S(1)}, u32[]{:S(2)}, u32[]{:S(2)}) %all-to-all-start) | async-done | bytes 786464 | tf_op jit(solution)/shard_map/all_to_all | solution.py:729
  28.8 5.5 %all-to-all-start.1 = ((bf16[16,2,48,256]{3,2,1,0:T(8,128)(2,1)}), bf16[16,2,48,256]{3,2,1,0:T(8,128)(2,1)S(1)}, u32[]{:S(2)}, u32[]{:S(2)}) async-start(bf16[16,2,48,256]{3,2,1,0:T(8,128)(2,1)} %get-tuple-element.76), calls=%async_computation.1 | async-start | bytes 1572864 | tf_op jit(solution)/shard_map/all_to_all | solution.py:729
  34.3 18.7 %all-to-all-done.1.x_ref = bf16[16,2,48,256]{3,2,1,0:T(8,128)(2,1)S(1)} async-done(((bf16[16,2,48,256]{3,2,1,0:T(8,128)(2,1)}), bf16[16,2,48,256]{3,2,1,0:T(8,128)(2,1)S(1)}, u32[]{:S(2)}, u32[]{:S(2)}) %all-to-all-start.1) | async-done | bytes 786464 | tf_op jit(solution)/shard_map/all_to_all | solution.py:729
  53.0 17.1 %columns_both.1 = (bf16[16,2,48,256]{3,2,1,0:T(8,128)(2,1)}, bf16[16,2,48,256]{3,2,1,0:T(8,128)(2,1)}, bf16[1552,256]{1,0:T(8,128)(2,1)S(1)}, bf16[1552,256]{1,0:T(8,128)(2,1)S(1)}) custom-call(s32[1]{0:T(128)} %bitcast.core_ref.at_ref, bf16[16,2,48,256]{3,2,1,0:T(8,128)(2,1)S(1)} %all-to-all-done.1.x_ref, bf16[16,2,48,256]{3,2,1,0:T(8,128)(2,1)S(1)} %all-to-all-done.up_ref, ...), custom_call_target="tpu_custom_call" | custom-call | flops 1 | bytes 1 | tf_op jit(solution)/shard_map/columns_both/pallas_call | solution.py:507
  70.2 5.5 %all-to-all-start.2 = ((bf16[16,2,48,256]{3,2,1,0:T(8,128)(2,1)}), bf16[16,2,48,256]{3,2,1,0:T(8,128)(2,1)S(1)}, u32[]{:S(2)}, u32[]{:S(2)}) async-start(bf16[16,2,48,256]{3,2,1,0:T(8,128)(2,1)} %get-tuple-element.78), calls=%async_computation.2 | async-start | bytes 1572864 | tf_op jit(solution)/shard_map/all_to_all | solution.py:729
  76.1 2.0 %collective-permute-done.refs_1_ = bf16[1552,256]{1,0:T(8,128)(2,1)S(1)} collective-permute-done((bf16[1552,256]{1,0:T(8,128)(2,1)S(1)}, bf16[1552,256]{1,0:T(8,128)(2,1)S(1)}, u32[]{:S(2)}, u32[]{:S(2)}) %collective-permute-start) | collective-permute-done | bytes 794656 | tf_op jit(solution)/shard_map/ppermute | solution.py:665
  82.0 4.4 %collective-permute-done.1.refs_1_ = bf16[400,256]{1,0:T(8,128)(2,1)S(1)} collective-permute-done((bf16[400,256]{1,0:T(8,128)(2,1)S(1)}, bf16[400,256]{1,0:T(8,128)(2,1)S(1)}, u32[]{:S(2)}, u32[]{:S(2)}) %collective-permute-start.1) | collective-permute-done | bytes 204832 | tf_op jit(solution)/shard_map/ppermute | solution.py:665
  86.4 9.7 %collective-permute-done.2.refs_2_ = bf16[400,256]{1,0:T(8,128)(2,1)S(1)} collective-permute-done((bf16[400,256]{1,0:T(8,128)(2,1)S(1)}, bf16[400,256]{1,0:T(8,128)(2,1)S(1)}, u32[]{:S(2)}, u32[]{:S(2)}) %collective-permute-start.2) | collective-permute-done | bytes 204832 | tf_op jit(solution)/shard_map/ppermute | solution.py:665
  96.9 5.5 %all-to-all-start.3 = ((bf16[16,2,48,256]{3,2,1,0:T(8,128)(2,1)}), bf16[16,2,48,256]{3,2,1,0:T(8,128)(2,1)S(1)}, u32[]{:S(2)}, u32[]{:S(2)}) async-start(bf16[16,2,48,256]{3,2,1,0:T(8,128)(2,1)} %get-tuple-element.86), calls=%async_computation.3 | async-start | bytes 1572864 | tf_op jit(solution)/shard_map/all_to_all | solution.py:729
  102.5 13.2 %rows_backward.1 = (f32[1536,256]{1,0:T(8,128)S(1)}, bf16[1536,256]{1,0:T(8,128)(2,1)S(1)}, bf16[1536,256]{1,0:T(8,128)(2,1)S(1)}, bf16[1536,256]{1,0:T(8,128)(2...) custom-call(s32[1]{0:T(128)} %bitcast.core_ref.at_ref, ...), custom_call_target="tpu_custom_call" | custom-call | flops 1 | bytes 1 | tf_op jit(solution)/shard_map/rows_backward/pallas_call | solution.py:461
  122.1 3.9 %rows_rest.1 = (f32[2,8,96,256]{3,2,1,0:T(8,128)}, f32[8,128]{1,0:T(8,128)S(1)}) custom-call(f32[1536,256]{1,0:T(8,128)S(1)} %get-tuple-element.97.mid_grad_ref, bf16[1536,256]{1,0:T(8,128)(2,1)S(1)} %get-tuple-element.98.dq_ref, bf16[1536,256]{1,0:T(8,128)(2,1)S(1)} %get-tuple-element.99.dk_ref, bf16[1536,256]{1,0:T(8,128)(2,1)S(1)} %get-tuple-element.100.dv_ref, ...), custom_call_target="tpu_custom_call" | custom-call | flops 1 | bytes 1 | tf_op jit(solution)/shard_map/rows_rest/pallas_call | solution.py:477
  126.1 2.8 %collective-permute-start.10 = (bf16[400,256]{1,0:T(8,128)(2,1)S(1)}, bf16[400,256]{1,0:T(8,128)(2,1)S(1)}, u32[]{:S(2)}, u32[]{:S(2)}) collective-permute-start(bf16[400,256]{1,0:T(8,128)(2,1)S(1)} %sum_split.9._.refs_0_), channel_id=1, source_target_pairs={{0,8},{1,9},{2,10},{3,11},{4,12},{5,13},{6,14},{7,15},{8,0},{9,1},... | collective-permute-start | bytes 614408 | tf_op jit(solution)/shard_map/ppermute | solution.py:665
  133.1 5.0 %collective-permute-done.10.refs_1_ = bf16[400,256]{1,0:T(8,128)(2,1)S(1)} collective-permute-done((bf16[400,256]{1,0:T(8,128)(2,1)S(1)}, bf16[400,256]{1,0:T(8,128)(2,1)S(1)}, u32[]{:S(2)}, u32[]{:S(2)}) %collective-permute-start.10) | collective-permute-done | bytes 204832 | tf_op jit(solution)/shard_map/ppermute | solution.py:665
  138.1 3.0 %collective-permute-done.9.refs_1_ = bf16[400,256]{1,0:T(8,128)(2,1)S(1)} collective-permute-done((bf16[400,256]{1,0:T(8,128)(2,1)S(1)}, bf16[400,256]{1,0:T(8,128)(2,1)S(1)}, u32[]{:S(2)}, u32[]{:S(2)}) %collective-permute-start.9) | collective-permute-done | bytes 204832 | tf_op jit(solution)/shard_map/ppermute | solution.py:665
  141.2 2.5 %collective-permute-start.11 = (bf16[400,256]{1,0:T(8,128)(2,1)S(1)}, bf16[400,256]{1,0:T(8,128)(2,1)S(1)}, u32[]{:S(2)}, u32[]{:S(2)}) collective-permute-start(bf16[400,256]{1,0:T(8,128)(2,1)S(1)} %sum_split.11.refs_0_.refs_2_), channel_id=1, source_target_pairs={{0,8},{1,9},{2,10},{3,11},{4,12},{5,13},{6,14},{7,15},{8,0},{9,1},... | collective-permute-start | bytes 614408 | tf_op jit(solution)/shard_map/ppermute | solution.py:665
  147.2 5.8 %collective-permute-done.11.refs_1_ = bf16[400,256]{1,0:T(8,128)(2,1)S(1)} collective-permute-done((bf16[400,256]{1,0:T(8,128)(2,1)S(1)}, bf16[400,256]{1,0:T(8,128)(2,1)S(1)}, u32[]{:S(2)}, u32[]{:S(2)}) %collective-permute-start.11) | collective-permute-done | bytes 204832 | tf_op jit(solution)/shard_map/ppermute | solution.py:665
  158.0 1.9 %finish.2 = (f32[1,256]{1,0:T(1,128)}, f32[256,256]{1,0:T(8,128)}, f32[256,256]{1,0:T(8,128)}, f32[256,256]{1,0:T(8,128)}, f32[256,256]{1,0:T(8,128)}, /*index=5...) custom-call(s32[1]{0:T(128)} %bitcast.core_ref.at_ref, ...), custom_call_target="tpu_custom_call" | custom-call | flops 1 | bytes 1 | tf_op jit(solution)/shard_map/finish/pallas_call | solution.py:637
  160.0 3.2 %collective-permute-done.14.refs_3_ = bf16[384,256]{1,0:T(8,128)(2,1)S(1)} collective-permute-done((bf16[384,256]{1,0:T(8,128)(2,1)S(1)}, bf16[384,256]{1,0:T(8,128)(2,1)S(1)}, u32[]{:S(2)}, u32[]{:S(2)}) %collective-permute-start.14) | collective-permute-done | bytes 196640 | tf_op jit(solution)/shard_map/ppermute | solution.py:665
  163.2 3.7 %collective-permute-done.13.refs_2_ = bf16[384,256]{1,0:T(8,128)(2,1)S(1)} collective-permute-done((bf16[384,256]{1,0:T(8,128)(2,1)S(1)}, bf16[384,256]{1,0:T(8,128)(2,1)S(1)}, u32[]{:S(2)}, u32[]{:S(2)}) %collective-permute-start.13) | collective-permute-done | bytes 196640 | tf_op jit(solution)/shard_map/ppermute | solution.py:665
  167.1 2.2 %collective-permute-done.19.other_ref = bf16[1536,256]{1,0:T(8,128)(2,1)S(1)} collective-permute-done((bf16[1536,256]{1,0:T(8,128)(2,1)S(1)}, bf16[1536,256]{1,0:T(8,128)(2,1)S(1)}, u32[]{:S(2)}, u32[]{:S(2)}) %collective-permute-start.19) | collective-permute-done | bytes 786464 | tf_op jit(solution)/shard_map/ppermute | solution.py:665
  169.3 1.9 %finish.3 = (f32[1,256]{1,0:T(1,128)}, f32[256,256]{1,0:T(8,128)}, f32[256,256]{1,0:T(8,128)}, f32[256,256]{1,0:T(8,128)}, f32[256,256]{1,0:T(8,128)}, /*index=5...) custom-call(s32[1]{0:T(128)} %bitcast.core_ref.at_ref, ...), custom_call_target="tpu_custom_call" | custom-call | flops 1 | bytes 1 | tf_op jit(solution)/shard_map/finish/pallas_call | solution.py:637
  (50 shorter events, 24.7 us)
Async XLA Ops:
  2.7 26.1 %all-to-all-start = ((bf16[16,2,48,256]{3,2,1,0:T(8,128)(2,1)}), bf16[16,2,48,256]{3,2,1,0:T(8,128)(2,1)S(1)}, u32[]{:S(2)}, u32[]{:S(2)}) async-start(bf16[16,2,48,256]{3,2,1,0:T(8,128)(2,1)} %bitcast.15), calls=%async_computation | async-start | bytes 1572864 | tf_op jit(solution)/shard_map/all_to_all | solution.py:729
  28.8 24.2 %all-to-all-start.1 = ((bf16[16,2,48,256]{3,2,1,0:T(8,128)(2,1)}), bf16[16,2,48,256]{3,2,1,0:T(8,128)(2,1)S(1)}, u32[]{:S(2)}, u32[]{:S(2)}) async-start(bf16[16,2,48,256]{3,2,1,0:T(8,128)(2,1)} %get-tuple-element.76), calls=%async_computation.1 | async-start | bytes 1572864 | tf_op jit(solution)/shard_map/all_to_all | solution.py:729
  70.2 26.8 %all-to-all-start.2 = ((bf16[16,2,48,256]{3,2,1,0:T(8,128)(2,1)}), bf16[16,2,48,256]{3,2,1,0:T(8,128)(2,1)S(1)}, u32[]{:S(2)}, u32[]{:S(2)}) async-start(bf16[16,2,48,256]{3,2,1,0:T(8,128)(2,1)} %get-tuple-element.78), calls=%async_computation.2 | async-start | bytes 1572864 | tf_op jit(solution)/shard_map/all_to_all | solution.py:729
  75.7 2.4 %collective-permute-start = (bf16[1552,256]{1,0:T(8,128)(2,1)S(1)}, bf16[1552,256]{1,0:T(8,128)(2,1)S(1)}, u32[]{:S(2)}, u32[]{:S(2)}) collective-permute-start(bf16[1552,256]{1,0:T(8,128)(2,1)S(1)} %get-tuple-element.81), channel_id=1, source_target_pairs={{0,1},{1,0},{2,3},{3,2},{4,5},{5,4},{6,7},{7,6},{8,9},{9,8},{10,11... | collective-permute-start | bytes 2383880 | tf_op jit(solution)/shard_map/ppermute | solution.py:665
  78.5 8.0 %collective-permute-start.1 = (bf16[400,256]{1,0:T(8,128)(2,1)S(1)}, bf16[400,256]{1,0:T(8,128)(2,1)S(1)}, u32[]{:S(2)}, u32[]{:S(2)}) collective-permute-start(bf16[400,256]{1,0:T(8,128)(2,1)S(1)} %get-tuple-element.83), channel_id=1, source_target_pairs={{0,16},{1,17},{2,18},{3,19},{4,20},{5,21},{6,22},{7,23},{8,24},{9,... | collective-permute-start | bytes 614408 | tf_op jit(solution)/shard_map/ppermute | solution.py:665
  80.0 16.1 %collective-permute-start.2 = (bf16[400,256]{1,0:T(8,128)(2,1)S(1)}, bf16[400,256]{1,0:T(8,128)(2,1)S(1)}, u32[]{:S(2)}, u32[]{:S(2)}) collective-permute-start(bf16[400,256]{1,0:T(8,128)(2,1)S(1)} %get-tuple-element.84), channel_id=1, source_target_pairs={{0,2},{1,3},{2,0},{3,1},{4,6},{5,7},{6,4},{7,5},{8,10},{9,11},{10,... | collective-permute-start | bytes 614408 | tf_op jit(solution)/shard_map/ppermute | solution.py:665
  81.9 14.2 %collective-permute-start.3 = (bf16[400,256]{1,0:T(8,128)(2,1)S(1)}, bf16[400,256]{1,0:T(8,128)(2,1)S(1)}, u32[]{:S(2)}, u32[]{:S(2)}) collective-permute-start(bf16[400,256]{1,0:T(8,128)(2,1)S(1)} %get-tuple-element.85), channel_id=1, source_target_pairs={{0,18},{1,19},{2,16},{3,17},{4,22},{5,23},{6,20},{7,21},{8,26},{9,... | collective-permute-start | bytes 614408 | tf_op jit(solution)/shard_map/ppermute | solution.py:665
  96.9 32.0 %all-to-all-start.3 = ((bf16[16,2,48,256]{3,2,1,0:T(8,128)(2,1)}), bf16[16,2,48,256]{3,2,1,0:T(8,128)(2,1)S(1)}, u32[]{:S(2)}, u32[]{:S(2)}) async-start(bf16[16,2,48,256]{3,2,1,0:T(8,128)(2,1)} %get-tuple-element.86), calls=%async_computation.3 | async-start | bytes 1572864 | tf_op jit(solution)/shard_map/all_to_all | solution.py:729
  115.7 2.4 %collective-permute-start.5 = (bf16[1552,256]{1,0:T(8,128)(2,1)S(1)}, bf16[1552,256]{1,0:T(8,128)(2,1)S(1)}, u32[]{:S(2)}, u32[]{:S(2)}) collective-permute-start(bf16[1552,256]{1,0:T(8,128)(2,1)S(1)} %get-tuple-element.102), channel_id=1, source_target_pairs={{0,1},{1,0},{2,3},{3,2},{4,5},{5,4},{6,7},{7,6},{8,9},{9,8},{10,11... | collective-permute-start | bytes 2383880 | tf_op jit(solution)/shard_map/ppermute | solution.py:665
  116.2 9.9 %collective-permute-start.4 = (bf16[400,256]{1,0:T(8,128)(2,1)S(1)}, bf16[400,256]{1,0:T(8,128)(2,1)S(1)}, u32[]{:S(2)}, u32[]{:S(2)}) collective-permute-start(bf16[400,256]{1,0:T(8,128)(2,1)S(1)} %copy-done.1), channel_id=1, source_target_pairs={{0,4},{1,5},{2,6},{3,7},{4,0},{5,1},{6,2},{7,3},{8,12},{9,13},{10,... | collective-permute-start | bytes 614408 | tf_op jit(solution)/shard_map/ppermute | solution.py:665
  118.5 11.4 %collective-permute-start.6 = (bf16[400,256]{1,0:T(8,128)(2,1)S(1)}, bf16[400,256]{1,0:T(8,128)(2,1)S(1)}, u32[]{:S(2)}, u32[]{:S(2)}) collective-permute-start(bf16[400,256]{1,0:T(8,128)(2,1)S(1)} %get-tuple-element.107), channel_id=1, source_target_pairs={{0,16},{1,17},{2,18},{3,19},{4,20},{5,21},{6,22},{7,23},{8,24},{9,... | collective-permute-start | bytes 614408 | tf_op jit(solution)/shard_map/ppermute | solution.py:665
  119.4 10.7 %collective-permute-start.7 = (bf16[400,256]{1,0:T(8,128)(2,1)S(1)}, bf16[400,256]{1,0:T(8,128)(2,1)S(1)}, u32[]{:S(2)}, u32[]{:S(2)}) collective-permute-start(bf16[400,256]{1,0:T(8,128)(2,1)S(1)} %get-tuple-element.108), channel_id=1, source_target_pairs={{0,2},{1,3},{2,0},{3,1},{4,6},{5,7},{6,4},{7,5},{8,10},{9,11},{10,... | collective-permute-start | bytes 614408 | tf_op jit(solution)/shard_map/ppermute | solution.py:665
  121.2 10.2 %collective-permute-start.8 = (bf16[400,256]{1,0:T(8,128)(2,1)S(1)}, bf16[400,256]{1,0:T(8,128)(2,1)S(1)}, u32[]{:S(2)}, u32[]{:S(2)}) collective-permute-start(bf16[400,256]{1,0:T(8,128)(2,1)S(1)} %get-tuple-element.109), channel_id=1, source_target_pairs={{0,18},{1,19},{2,16},{3,17},{4,22},{5,23},{6,20},{7,21},{8,26},{9,... | collective-permute-start | bytes 614408 | tf_op jit(solution)/shard_map/ppermute | solution.py:665
  126.1 12.0 %collective-permute-start.10 = (bf16[400,256]{1,0:T(8,128)(2,1)S(1)}, bf16[400,256]{1,0:T(8,128)(2,1)S(1)}, u32[]{:S(2)}, u32[]{:S(2)}) collective-permute-start(bf16[400,256]{1,0:T(8,128)(2,1)S(1)} %sum_split.9._.refs_0_), channel_id=1, source_target_pairs={{0,8},{1,9},{2,10},{3,11},{4,12},{5,13},{6,14},{7,15},{8,0},{9,1},... | collective-permute-start | bytes 614408 | tf_op jit(solution)/shard_map/ppermute | solution.py:665
  131.6 9.6 %collective-permute-start.9 = (bf16[400,256]{1,0:T(8,128)(2,1)S(1)}, bf16[400,256]{1,0:T(8,128)(2,1)S(1)}, u32[]{:S(2)}, u32[]{:S(2)}) collective-permute-start(bf16[400,256]{1,0:T(8,128)(2,1)S(1)} %sum_split.10.refs_2_.refs_0_), channel_id=1, source_target_pairs={{0,4},{1,5},{2,6},{3,7},{4,0},{5,1},{6,2},{7,3},{8,12},{9,13},{10,... | collective-permute-start | bytes 614408 | tf_op jit(solution)/shard_map/ppermute | solution.py:665
  141.2 11.8 %collective-permute-start.11 = (bf16[400,256]{1,0:T(8,128)(2,1)S(1)}, bf16[400,256]{1,0:T(8,128)(2,1)S(1)}, u32[]{:S(2)}, u32[]{:S(2)}) collective-permute-start(bf16[400,256]{1,0:T(8,128)(2,1)S(1)} %sum_split.11.refs_0_.refs_2_), channel_id=1, source_target_pairs={{0,8},{1,9},{2,10},{3,11},{4,12},{5,13},{6,14},{7,15},{8,0},{9,1},... | collective-permute-start | bytes 614408 | tf_op jit(solution)/shard_map/ppermute | solution.py:665
  143.7 9.3 %collective-permute-start.17 = (bf16[384,256]{1,0:T(8,128)(2,1)S(1)}, bf16[384,256]{1,0:T(8,128)(2,1)S(1)}, u32[]{:S(2)}, u32[]{:S(2)}) collective-permute-start(bf16[384,256]{1,0:T(8,128)(2,1)S(1)} %get-tuple-element.111.refs_2_.refs_0_), channel_id=1, source_target_pairs={{0,18},{1,19},{2,16},{3,17},{4,22},{5,23},{6,20},{7,21},{8,26},{9,... | collective-permute-start | bytes 589832 | tf_op jit(solution)/shard_map/ppermute | solution.py:665
  144.5 9.8 %collective-permute-start.16 = (bf16[384,256]{1,0:T(8,128)(2,1)S(1)}, bf16[384,256]{1,0:T(8,128)(2,1)S(1)}, u32[]{:S(2)}, u32[]{:S(2)}) collective-permute-start(bf16[384,256]{1,0:T(8,128)(2,1)S(1)} %get-tuple-element.111.refs_2_.refs_0_), channel_id=1, source_target_pairs={{0,2},{1,3},{2,0},{3,1},{4,6},{5,7},{6,4},{7,5},{8,10},{9,11},{10,... | collective-permute-start | bytes 589832 | tf_op jit(solution)/shard_map/ppermute | solution.py:665
  145.9 8.4 %collective-permute-start.15 = (bf16[384,256]{1,0:T(8,128)(2,1)S(1)}, bf16[384,256]{1,0:T(8,128)(2,1)S(1)}, u32[]{:S(2)}, u32[]{:S(2)}) collective-permute-start(bf16[384,256]{1,0:T(8,128)(2,1)S(1)} %get-tuple-element.111.refs_2_.refs_0_), channel_id=1, source_target_pairs={{0,16},{1,17},{2,18},{3,19},{4,20},{5,21},{6,22},{7,23},{8,24},{9,... | collective-permute-start | bytes 589832 | tf_op jit(solution)/shard_map/ppermute | solution.py:665
  154.4 3.6 %collective-permute-start.18 = (bf16[1536,256]{1,0:T(8,128)(2,1)S(1)}, bf16[1536,256]{1,0:T(8,128)(2,1)S(1)}, u32[]{:S(2)}, u32[]{:S(2)}) collective-permute-start(bf16[1536,256]{1,0:T(8,128)(2,1)S(1)} %bitcast.16), channel_id=1, source_target_pairs={{0,1},{1,0},{2,3},{3,2},{4,5},{5,4},{6,7},{7,6},{8,9},{9,8},{10,11... | collective-permute-start | bytes 2359304 | tf_op jit(solution)/shard_map/ppermute | solution.py:665
  154.5 8.7 %collective-permute-start.14 = (bf16[384,256]{1,0:T(8,128)(2,1)S(1)}, bf16[384,256]{1,0:T(8,128)(2,1)S(1)}, u32[]{:S(2)}, u32[]{:S(2)}) collective-permute-start(bf16[384,256]{1,0:T(8,128)(2,1)S(1)} %get-tuple-element.112.refs_4_.refs_0_), channel_id=1, source_target_pairs={{0,18},{1,19},{2,16},{3,17},{4,22},{5,23},{6,20},{7,21},{8,26},{9,... | collective-permute-start | bytes 589832 | tf_op jit(solution)/shard_map/ppermute | solution.py:665
  156.0 10.9 %collective-permute-start.13 = (bf16[384,256]{1,0:T(8,128)(2,1)S(1)}, bf16[384,256]{1,0:T(8,128)(2,1)S(1)}, u32[]{:S(2)}, u32[]{:S(2)}) collective-permute-start(bf16[384,256]{1,0:T(8,128)(2,1)S(1)} %get-tuple-element.112.refs_4_.refs_0_), channel_id=1, source_target_pairs={{0,2},{1,3},{2,0},{3,1},{4,6},{5,7},{6,4},{7,5},{8,10},{9,11},{10,... | collective-permute-start | bytes 589832 | tf_op jit(solution)/shard_map/ppermute | solution.py:665
  157.2 9.7 %collective-permute-start.12 = (bf16[384,256]{1,0:T(8,128)(2,1)S(1)}, bf16[384,256]{1,0:T(8,128)(2,1)S(1)}, u32[]{:S(2)}, u32[]{:S(2)}) collective-permute-start(bf16[384,256]{1,0:T(8,128)(2,1)S(1)} %get-tuple-element.112.refs_4_.refs_0_), channel_id=1, source_target_pairs={{0,16},{1,17},{2,18},{3,19},{4,20},{5,21},{6,22},{7,23},{8,24},{9,... | collective-permute-start | bytes 589832 | tf_op jit(solution)/shard_map/ppermute | solution.py:665
  167.0 2.4 %collective-permute-start.19 = (bf16[1536,256]{1,0:T(8,128)(2,1)S(1)}, bf16[1536,256]{1,0:T(8,128)(2,1)S(1)}, u32[]{:S(2)}, u32[]{:S(2)}) collective-permute-start(bf16[1536,256]{1,0:T(8,128)(2,1)S(1)} %bitcast.19), channel_id=1, source_target_pairs={{0,1},{1,0},{2,3},{3,2},{4,5},{5,4},{6,7},{7,6},{8,9},{9,8},{10,11... | collective-permute-start | bytes 2359304 | tf_op jit(solution)/shard_map/ppermute | solution.py:665
  (4 other events, 100.2 us)

commit v6 on v5

--- a/solution.py
+++ b/solution.py
@@ -102,7 +102,7 @@
     tile = min(HIDDEN_TILE, hidden_width)
     tiles = hidden_width // tile
 
-    @pl.loop(0, tiles)
+    @pl.loop(0, tiles, unroll=2)
     def _(j):
         cut = pl.ds(pl.multiple_of(j * tile, tile), tile)
         expand = expand_ref[:, cut]
@@ -244,7 +244,7 @@
     normed_b = (normal_b * gb_ref[...]).astype(BF16)
     feed_grad_ref[...] = jnp.zeros_like(feed_grad_ref)
 
-    @pl.loop(0, tiles)
+    @pl.loop(0, tiles, unroll=2)
     def _(j):
         cut = pl.ds(pl.multiple_of(j * tile, tile), tile)
         hidden_grad = mm_right_t(up_low, w2_ref[cut, :])

time: 172 us -> 171 us (level)
  no operation moved by 1% of the time
where the time goes in v6:
time: 171 us; the launch traced here: 170 us
  waiting for transfers between devices  64.8 us (38%)
  Pallas kernels  53.7 us (31%)
  starting transfers between devices  47.9 us (28%)
  local copies, waits for them, and re-layouts  2.78 us (2%)
    ppermute x20, waiting for transfers between devices, swap(): lax.ppermute(array, ALL, [(i, i ^ mask) for i in range(self.devices)])  41.8 us
    ppermute x20, starting transfers between devices, swap(): lax.ppermute(array, ALL, [(i, i ^ mask) for i in range(self.devices)])  24 us
    all_to_all x4, starting transfers between devices, trade(): return lax.all_to_all(array, 'row', 0, 0, tiled=True)  23.9 us
    all_to_all x4, waiting for transfers between devices, trade(): return lax.all_to_all(array, 'row', 0, 0, tiled=True)  23 us
    pallas_call x1, Pallas kernels, columns_both(): pl.pallas_call(columns_kernel, in_specs=[SCALAR] + [HELD] * 4 + [UNREAD]...  16.4 us
    pallas_call x1, Pallas kernels, rows_forward(): pl.pallas_call(rows_forward_kernel, grid=(1,), in_specs=[whole(array) for...  14.4 us
    pallas_call x1, Pallas kernels, rows_backward(): pl.pallas_call(rows_backward_kernel, in_specs=[SCALAR, HELD] + [UNREAD] *...  12.7 us
    pallas_call x1, Pallas kernels, rows_rest(): pl.pallas_call(rows_rest_kernel, grid=(1,), in_specs=[HELD] * 4 + [whole(...  3.92 us
  transfers between devices with their start and end apart: 24, of which 15 were waited for; matrix products, arithmetic and copies ran while one was open for 0% of the time, Pallas kernels for 21%

profile of v6, /device:TPU:0, one launch (start us, length us, event | category | flops | bytes accessed | tf_op | source)
XLA Modules:
  0.0 170.1 jit_solution(2449411687081130972)
XLA Ops:
  0.7 2.1 %copy.38 = bf16[2,16,48,256]{3,2,0,1:T(8,128)(2,1)} copy(bf16[2,16,48,256]{3,2,1,0:T(8,128)(2,1)} %bitcast.24) | data formatting | bytes 1572864 | tf_op jit(solution)/shard_map/reshape | solution.py:734
  2.7 7.4 %all-to-all-start = ((bf16[16,2,48,256]{3,2,1,0:T(8,128)(2,1)}), bf16[16,2,48,256]{3,2,1,0:T(8,128)(2,1)S(1)}, u32[]{:S(2)}, u32[]{:S(2)}) async-start(bf16[16,2,48,256]{3,2,1,0:T(8,128)(2,1)} %bitcast.15), calls=%async_computation | async-start | bytes 1572864 | tf_op jit(solution)/shard_map/all_to_all | solution.py:729
  10.2 14.4 %rows_forward.1 = (bf16[16,2,48,256]{3,2,1,0:T(8,128)(2,1)}, bf16[2,8,96,256]{3,2,1,0:T(8,128)(2,1)}, bf16[2,8,96,256]{3,2,1,0:T(8,128)(2,1)}, bf16[2,8,96,256]{...) custom-call(bf16[2,8,96,256]{3,2,1,0:T(8,128)(2,1)} %x_ref.3, ...), custom_call_target="tpu_custom_call" | custom-call | flops 1 | bytes 1 | tf_op jit(solution)/shard_map/rows_forward/pallas_call | solution.py:442
  24.5 4.3 %all-to-all-done.up_ref = bf16[16,2,48,256]{3,2,1,0:T(8,128)(2,1)S(1)} async-done(((bf16[16,2,48,256]{3,2,1,0:T(8,128)(2,1)}), bf16[16,2,48,256]{3,2,1,0:T(8,128)(2,1)S(1)}, u32[]{:S(2)}, u32[]{:S(2)}) %all-to-all-start) | async-done | bytes 786464 | tf_op jit(solution)/shard_map/all_to_all | solution.py:729
  28.8 5.5 %all-to-all-start.1 = ((bf16[16,2,48,256]{3,2,1,0:T(8,128)(2,1)}), bf16[16,2,48,256]{3,2,1,0:T(8,128)(2,1)S(1)}, u32[]{:S(2)}, u32[]{:S(2)}) async-start(bf16[16,2,48,256]{3,2,1,0:T(8,128)(2,1)} %get-tuple-element.76), calls=%async_computation.1 | async-start | bytes 1572864 | tf_op jit(solution)/shard_map/all_to_all | solution.py:729
  34.3 18.7 %all-to-all-done.1.x_ref = bf16[16,2,48,256]{3,2,1,0:T(8,128)(2,1)S(1)} async-done(((bf16[16,2,48,256]{3,2,1,0:T(8,128)(2,1)}), bf16[16,2,48,256]{3,2,1,0:T(8,128)(2,1)S(1)}, u32[]{:S(2)}, u32[]{:S(2)}) %all-to-all-start.1) | async-done | bytes 786464 | tf_op jit(solution)/shard_map/all_to_all | solution.py:729
  53.0 16.4 %columns_both.1 = (bf16[16,2,48,256]{3,2,1,0:T(8,128)(2,1)}, bf16[16,2,48,256]{3,2,1,0:T(8,128)(2,1)}, bf16[1552,256]{1,0:T(8,128)(2,1)S(1)}, bf16[1552,256]{1,0:T(8,128)(2,1)S(1)}) custom-call(s32[1]{0:T(128)} %bitcast.core_ref.at_ref, bf16[16,2,48,256]{3,2,1,0:T(8,128)(2,1)S(1)} %all-to-all-done.1.x_ref, bf16[16,2,48,256]{3,2,1,0:T(8,128)(2,1)S(1)} %all-to-all-done.up_ref, ...), custom_call_target="tpu_custom_call" | custom-call | flops 1 | bytes 1 | tf_op jit(solution)/shard_map/columns_both/pallas_call | solution.py:507
  69.5 5.5 %all-to-all-start.2 = ((bf16[16,2,48,256]{3,2,1,0:T(8,128)(2,1)}), bf16[16,2,48,256]{3,2,1,0:T(8,128)(2,1)S(1)}, u32[]{:S(2)}, u32[]{:S(2)}) async-start(bf16[16,2,48,256]{3,2,1,0:T(8,128)(2,1)} %get-tuple-element.78), calls=%async_computation.2 | async-start | bytes 1572864 | tf_op jit(solution)/shard_map/all_to_all | solution.py:729
  75.4 1.9 %collective-permute-done.refs_1_ = bf16[1552,256]{1,0:T(8,128)(2,1)S(1)} collective-permute-done((bf16[1552,256]{1,0:T(8,128)(2,1)S(1)}, bf16[1552,256]{1,0:T(8,128)(2,1)S(1)}, u32[]{:S(2)}, u32[]{:S(2)}) %collective-permute-start) | collective-permute-done | bytes 794656 | tf_op jit(solution)/shard_map/ppermute | solution.py:665
  81.4 4.4 %collective-permute-done.1.refs_1_ = bf16[400,256]{1,0:T(8,128)(2,1)S(1)} collective-permute-done((bf16[400,256]{1,0:T(8,128)(2,1)S(1)}, bf16[400,256]{1,0:T(8,128)(2,1)S(1)}, u32[]{:S(2)}, u32[]{:S(2)}) %collective-permute-start.1) | collective-permute-done | bytes 204832 | tf_op jit(solution)/shard_map/ppermute | solution.py:665
  85.8 9.7 %collective-permute-done.2.refs_2_ = bf16[400,256]{1,0:T(8,128)(2,1)S(1)} collective-permute-done((bf16[400,256]{1,0:T(8,128)(2,1)S(1)}, bf16[400,256]{1,0:T(8,128)(2,1)S(1)}, u32[]{:S(2)}, u32[]{:S(2)}) %collective-permute-start.2) | collective-permute-done | bytes 204832 | tf_op jit(solution)/shard_map/ppermute | solution.py:665
  96.3 5.5 %all-to-all-start.3 = ((bf16[16,2,48,256]{3,2,1,0:T(8,128)(2,1)}), bf16[16,2,48,256]{3,2,1,0:T(8,128)(2,1)S(1)}, u32[]{:S(2)}, u32[]{:S(2)}) async-start(bf16[16,2,48,256]{3,2,1,0:T(8,128)(2,1)} %get-tuple-element.86), calls=%async_computation.3 | async-start | bytes 1572864 | tf_op jit(solution)/shard_map/all_to_all | solution.py:729
  101.8 12.7 %rows_backward.1 = (f32[1536,256]{1,0:T(8,128)S(1)}, bf16[1536,256]{1,0:T(8,128)(2,1)S(1)}, bf16[1536,256]{1,0:T(8,128)(2,1)S(1)}, bf16[1536,256]{1,0:T(8,128)(2...) custom-call(s32[1]{0:T(128)} %bitcast.core_ref.at_ref, ...), custom_call_target="tpu_custom_call" | custom-call | flops 1 | bytes 1 | tf_op jit(solution)/shard_map/rows_backward/pallas_call | solution.py:461
  121.0 3.9 %rows_rest.1 = (f32[2,8,96,256]{3,2,1,0:T(8,128)}, f32[8,128]{1,0:T(8,128)S(1)}) custom-call(f32[1536,256]{1,0:T(8,128)S(1)} %get-tuple-element.97.mid_grad_ref, bf16[1536,256]{1,0:T(8,128)(2,1)S(1)} %get-tuple-element.98.dq_ref, bf16[1536,256]{1,0:T(8,128)(2,1)S(1)} %get-tuple-element.99.dk_ref, bf16[1536,256]{1,0:T(8,128)(2,1)S(1)} %get-tuple-element.100.dv_ref, ...), custom_call_target="tpu_custom_call" | custom-call | flops 1 | bytes 1 | tf_op jit(solution)/shard_map/rows_rest/pallas_call | solution.py:477
  124.9 2.8 %collective-permute-start.10 = (bf16[400,256]{1,0:T(8,128)(2,1)S(1)}, bf16[400,256]{1,0:T(8,128)(2,1)S(1)}, u32[]{:S(2)}, u32[]{:S(2)}) collective-permute-start(bf16[400,256]{1,0:T(8,128)(2,1)S(1)} %sum_split.9._.refs_0_), channel_id=1, source_target_pairs={{0,8},{1,9},{2,10},{3,11},{4,12},{5,13},{6,14},{7,15},{8,0},{9,1},... | collective-permute-start | bytes 614408 | tf_op jit(solution)/shard_map/ppermute | solution.py:665
  132.1 4.8 %collective-permute-done.10.refs_1_ = bf16[400,256]{1,0:T(8,128)(2,1)S(1)} collective-permute-done((bf16[400,256]{1,0:T(8,128)(2,1)S(1)}, bf16[400,256]{1,0:T(8,128)(2,1)S(1)}, u32[]{:S(2)}, u32[]{:S(2)}) %collective-permute-start.10) | collective-permute-done | bytes 204832 | tf_op jit(solution)/shard_map/ppermute | solution.py:665
  137.0 3.0 %collective-permute-done.9.refs_1_ = bf16[400,256]{1,0:T(8,128)(2,1)S(1)} collective-permute-done((bf16[400,256]{1,0:T(8,128)(2,1)S(1)}, bf16[400,256]{1,0:T(8,128)(2,1)S(1)}, u32[]{:S(2)}, u32[]{:S(2)}) %collective-permute-start.9) | collective-permute-done | bytes 204832 | tf_op jit(solution)/shard_map/ppermute | solution.py:665
  140.0 2.5 %collective-permute-start.11 = (bf16[400,256]{1,0:T(8,128)(2,1)S(1)}, bf16[400,256]{1,0:T(8,128)(2,1)S(1)}, u32[]{:S(2)}, u32[]{:S(2)}) collective-permute-start(bf16[400,256]{1,0:T(8,128)(2,1)S(1)} %sum_split.11.refs_0_.refs_2_), channel_id=1, source_target_pairs={{0,8},{1,9},{2,10},{3,11},{4,12},{5,13},{6,14},{7,15},{8,0},{9,1},... | collective-permute-start | bytes 614408 | tf_op jit(solution)/shard_map/ppermute | solution.py:665
  146.0 5.8 %collective-permute-done.11.refs_1_ = bf16[400,256]{1,0:T(8,128)(2,1)S(1)} collective-permute-done((bf16[400,256]{1,0:T(8,128)(2,1)S(1)}, bf16[400,256]{1,0:T(8,128)(2,1)S(1)}, u32[]{:S(2)}, u32[]{:S(2)}) %collective-permute-start.11) | collective-permute-done | bytes 204832 | tf_op jit(solution)/shard_map/ppermute | solution.py:665
  156.9 1.9 %finish.2 = (f32[1,256]{1,0:T(1,128)}, f32[256,256]{1,0:T(8,128)}, f32[256,256]{1,0:T(8,128)}, f32[256,256]{1,0:T(8,128)}, f32[256,256]{1,0:T(8,128)}, /*index=5...) custom-call(s32[1]{0:T(128)} %bitcast.core_ref.at_ref, ...), custom_call_target="tpu_custom_call" | custom-call | flops 1 | bytes 1 | tf_op jit(solution)/shard_map/finish/pallas_call | solution.py:637
  158.8 3.2 %collective-permute-done.14.refs_3_ = bf16[384,256]{1,0:T(8,128)(2,1)S(1)} collective-permute-done((bf16[384,256]{1,0:T(8,128)(2,1)S(1)}, bf16[384,256]{1,0:T(8,128)(2,1)S(1)}, u32[]{:S(2)}, u32[]{:S(2)}) %collective-permute-start.14) | collective-permute-done | bytes 196640 | tf_op jit(solution)/shard_map/ppermute | solution.py:665
  162.0 3.7 %collective-permute-done.13.refs_2_ = bf16[384,256]{1,0:T(8,128)(2,1)S(1)} collective-permute-done((bf16[384,256]{1,0:T(8,128)(2,1)S(1)}, bf16[384,256]{1,0:T(8,128)(2,1)S(1)}, u32[]{:S(2)}, u32[]{:S(2)}) %collective-permute-start.13) | collective-permute-done | bytes 196640 | tf_op jit(solution)/shard_map/ppermute | solution.py:665
  165.9 2.2 %collective-permute-done.19.other_ref = bf16[1536,256]{1,0:T(8,128)(2,1)S(1)} collective-permute-done((bf16[1536,256]{1,0:T(8,128)(2,1)S(1)}, bf16[1536,256]{1,0:T(8,128)(2,1)S(1)}, u32[]{:S(2)}, u32[]{:S(2)}) %collective-permute-start.19) | collective-permute-done | bytes 786464 | tf_op jit(solution)/shard_map/ppermute | solution.py:665
  168.1 1.9 %finish.3 = (f32[1,256]{1,0:T(1,128)}, f32[256,256]{1,0:T(8,128)}, f32[256,256]{1,0:T(8,128)}, f32[256,256]{1,0:T(8,128)}, f32[256,256]{1,0:T(8,128)}, /*index=5...) custom-call(s32[1]{0:T(128)} %bitcast.core_ref.at_ref, ...), custom_call_target="tpu_custom_call" | custom-call | flops 1 | bytes 1 | tf_op jit(solution)/shard_map/finish/pallas_call | solution.py:637
  (50 shorter events, 24.9 us)
Async XLA Ops:
  2.7 26.1 %all-to-all-start = ((bf16[16,2,48,256]{3,2,1,0:T(8,128)(2,1)}), bf16[16,2,48,256]{3,2,1,0:T(8,128)(2,1)S(1)}, u32[]{:S(2)}, u32[]{:S(2)}) async-start(bf16[16,2,48,256]{3,2,1,0:T(8,128)(2,1)} %bitcast.15), calls=%async_computation | async-start | bytes 1572864 | tf_op jit(solution)/shard_map/all_to_all | solution.py:729
  28.8 24.2 %all-to-all-start.1 = ((bf16[16,2,48,256]{3,2,1,0:T(8,128)(2,1)}), bf16[16,2,48,256]{3,2,1,0:T(8,128)(2,1)S(1)}, u32[]{:S(2)}, u32[]{:S(2)}) async-start(bf16[16,2,48,256]{3,2,1,0:T(8,128)(2,1)} %get-tuple-element.76), calls=%async_computation.1 | async-start | bytes 1572864 | tf_op jit(solution)/shard_map/all_to_all | solution.py:729
  69.5 26.8 %all-to-all-start.2 = ((bf16[16,2,48,256]{3,2,1,0:T(8,128)(2,1)}), bf16[16,2,48,256]{3,2,1,0:T(8,128)(2,1)S(1)}, u32[]{:S(2)}, u32[]{:S(2)}) async-start(bf16[16,2,48,256]{3,2,1,0:T(8,128)(2,1)} %get-tuple-element.78), calls=%async_computation.2 | async-start | bytes 1572864 | tf_op jit(solution)/shard_map/all_to_all | solution.py:729
  75.0 2.4 %collective-permute-start = (bf16[1552,256]{1,0:T(8,128)(2,1)S(1)}, bf16[1552,256]{1,0:T(8,128)(2,1)S(1)}, u32[]{:S(2)}, u32[]{:S(2)}) collective-permute-start(bf16[1552,256]{1,0:T(8,128)(2,1)S(1)} %get-tuple-element.81), channel_id=1, source_target_pairs={{0,1},{1,0},{2,3},{3,2},{4,5},{5,4},{6,7},{7,6},{8,9},{9,8},{10,11... | collective-permute-start | bytes 2383880 | tf_op jit(solution)/shard_map/ppermute | solution.py:665
  77.8 8.0 %collective-permute-start.1 = (bf16[400,256]{1,0:T(8,128)(2,1)S(1)}, bf16[400,256]{1,0:T(8,128)(2,1)S(1)}, u32[]{:S(2)}, u32[]{:S(2)}) collective-permute-start(bf16[400,256]{1,0:T(8,128)(2,1)S(1)} %get-tuple-element.83), channel_id=1, source_target_pairs={{0,16},{1,17},{2,18},{3,19},{4,20},{5,21},{6,22},{7,23},{8,24},{9,... | collective-permute-start | bytes 614408 | tf_op jit(solution)/shard_map/ppermute | solution.py:665
  79.4 16.1 %collective-permute-start.2 = (bf16[400,256]{1,0:T(8,128)(2,1)S(1)}, bf16[400,256]{1,0:T(8,128)(2,1)S(1)}, u32[]{:S(2)}, u32[]{:S(2)}) collective-permute-start(bf16[400,256]{1,0:T(8,128)(2,1)S(1)} %get-tuple-element.84), channel_id=1, source_target_pairs={{0,2},{1,3},{2,0},{3,1},{4,6},{5,7},{6,4},{7,5},{8,10},{9,11},{10,... | collective-permute-start | bytes 614408 | tf_op jit(solution)/shard_map/ppermute | solution.py:665
  81.3 14.2 %collective-permute-start.3 = (bf16[400,256]{1,0:T(8,128)(2,1)S(1)}, bf16[400,256]{1,0:T(8,128)(2,1)S(1)}, u32[]{:S(2)}, u32[]{:S(2)}) collective-permute-start(bf16[400,256]{1,0:T(8,128)(2,1)S(1)} %get-tuple-element.85), channel_id=1, source_target_pairs={{0,18},{1,19},{2,16},{3,17},{4,22},{5,23},{6,20},{7,21},{8,26},{9,... | collective-permute-start | bytes 614408 | tf_op jit(solution)/shard_map/ppermute | solution.py:665
  96.3 31.5 %all-to-all-start.3 = ((bf16[16,2,48,256]{3,2,1,0:T(8,128)(2,1)}), bf16[16,2,48,256]{3,2,1,0:T(8,128)(2,1)S(1)}, u32[]{:S(2)}, u32[]{:S(2)}) async-start(bf16[16,2,48,256]{3,2,1,0:T(8,128)(2,1)} %get-tuple-element.86), calls=%async_computation.3 | async-start | bytes 1572864 | tf_op jit(solution)/shard_map/all_to_all | solution.py:729
  114.5 2.4 %collective-permute-start.5 = (bf16[1552,256]{1,0:T(8,128)(2,1)S(1)}, bf16[1552,256]{1,0:T(8,128)(2,1)S(1)}, u32[]{:S(2)}, u32[]{:S(2)}) collective-permute-start(bf16[1552,256]{1,0:T(8,128)(2,1)S(1)} %get-tuple-element.102), channel_id=1, source_target_pairs={{0,1},{1,0},{2,3},{3,2},{4,5},{5,4},{6,7},{7,6},{8,9},{9,8},{10,11... | collective-permute-start | bytes 2383880 | tf_op jit(solution)/shard_map/ppermute | solution.py:665
  115.0 9.9 %collective-permute-start.4 = (bf16[400,256]{1,0:T(8,128)(2,1)S(1)}, bf16[400,256]{1,0:T(8,128)(2,1)S(1)}, u32[]{:S(2)}, u32[]{:S(2)}) collective-permute-start(bf16[400,256]{1,0:T(8,128)(2,1)S(1)} %copy-done.1), channel_id=1, source_target_pairs={{0,4},{1,5},{2,6},{3,7},{4,0},{5,1},{6,2},{7,3},{8,12},{9,13},{10,... | collective-permute-start | bytes 614408 | tf_op jit(solution)/shard_map/ppermute | solution.py:665
  117.4 11.4 %collective-permute-start.6 = (bf16[400,256]{1,0:T(8,128)(2,1)S(1)}, bf16[400,256]{1,0:T(8,128)(2,1)S(1)}, u32[]{:S(2)}, u32[]{:S(2)}) collective-permute-start(bf16[400,256]{1,0:T(8,128)(2,1)S(1)} %get-tuple-element.107), channel_id=1, source_target_pairs={{0,16},{1,17},{2,18},{3,19},{4,20},{5,21},{6,22},{7,23},{8,24},{9,... | collective-permute-start | bytes 614408 | tf_op jit(solution)/shard_map/ppermute | solution.py:665
  118.2 10.7 %collective-permute-start.7 = (bf16[400,256]{1,0:T(8,128)(2,1)S(1)}, bf16[400,256]{1,0:T(8,128)(2,1)S(1)}, u32[]{:S(2)}, u32[]{:S(2)}) collective-permute-start(bf16[400,256]{1,0:T(8,128)(2,1)S(1)} %get-tuple-element.108), channel_id=1, source_target_pairs={{0,2},{1,3},{2,0},{3,1},{4,6},{5,7},{6,4},{7,5},{8,10},{9,11},{10,... | collective-permute-start | bytes 614408 | tf_op jit(solution)/shard_map/ppermute | solution.py:665
  120.1 10.2 %collective-permute-start.8 = (bf16[400,256]{1,0:T(8,128)(2,1)S(1)}, bf16[400,256]{1,0:T(8,128)(2,1)S(1)}, u32[]{:S(2)}, u32[]{:S(2)}) collective-permute-start(bf16[400,256]{1,0:T(8,128)(2,1)S(1)} %get-tuple-element.109), channel_id=1, source_target_pairs={{0,18},{1,19},{2,16},{3,17},{4,22},{5,23},{6,20},{7,21},{8,26},{9,... | collective-permute-start | bytes 614408 | tf_op jit(solution)/shard_map/ppermute | solution.py:665
  124.9 12.0 %collective-permute-start.10 = (bf16[400,256]{1,0:T(8,128)(2,1)S(1)}, bf16[400,256]{1,0:T(8,128)(2,1)S(1)}, u32[]{:S(2)}, u32[]{:S(2)}) collective-permute-start(bf16[400,256]{1,0:T(8,128)(2,1)S(1)} %sum_split.9._.refs_0_), channel_id=1, source_target_pairs={{0,8},{1,9},{2,10},{3,11},{4,12},{5,13},{6,14},{7,15},{8,0},{9,1},... | collective-permute-start | bytes 614408 | tf_op jit(solution)/shard_map/ppermute | solution.py:665
  130.4 9.6 %collective-permute-start.9 = (bf16[400,256]{1,0:T(8,128)(2,1)S(1)}, bf16[400,256]{1,0:T(8,128)(2,1)S(1)}, u32[]{:S(2)}, u32[]{:S(2)}) collective-permute-start(bf16[400,256]{1,0:T(8,128)(2,1)S(1)} %sum_split.10.refs_2_.refs_0_), channel_id=1, source_target_pairs={{0,4},{1,5},{2,6},{3,7},{4,0},{5,1},{6,2},{7,3},{8,12},{9,13},{10,... | collective-permute-start | bytes 614408 | tf_op jit(solution)/shard_map/ppermute | solution.py:665
  140.0 11.8 %collective-permute-start.11 = (bf16[400,256]{1,0:T(8,128)(2,1)S(1)}, bf16[400,256]{1,0:T(8,128)(2,1)S(1)}, u32[]{:S(2)}, u32[]{:S(2)}) collective-permute-start(bf16[400,256]{1,0:T(8,128)(2,1)S(1)} %sum_split.11.refs_0_.refs_2_), channel_id=1, source_target_pairs={{0,8},{1,9},{2,10},{3,11},{4,12},{5,13},{6,14},{7,15},{8,0},{9,1},... | collective-permute-start | bytes 614408 | tf_op jit(solution)/shard_map/ppermute | solution.py:665
  142.5 9.3 %collective-permute-start.17 = (bf16[384,256]{1,0:T(8,128)(2,1)S(1)}, bf16[384,256]{1,0:T(8,128)(2,1)S(1)}, u32[]{:S(2)}, u32[]{:S(2)}) collective-permute-start(bf16[384,256]{1,0:T(8,128)(2,1)S(1)} %get-tuple-element.111.refs_2_.refs_0_), channel_id=1, source_target_pairs={{0,18},{1,19},{2,16},{3,17},{4,22},{5,23},{6,20},{7,21},{8,26},{9,... | collective-permute-start | bytes 589832 | tf_op jit(solution)/shard_map/ppermute | solution.py:665
  143.3 9.9 %collective-permute-start.16 = (bf16[384,256]{1,0:T(8,128)(2,1)S(1)}, bf16[384,256]{1,0:T(8,128)(2,1)S(1)}, u32[]{:S(2)}, u32[]{:S(2)}) collective-permute-start(bf16[384,256]{1,0:T(8,128)(2,1)S(1)} %get-tuple-element.111.refs_2_.refs_0_), channel_id=1, source_target_pairs={{0,2},{1,3},{2,0},{3,1},{4,6},{5,7},{6,4},{7,5},{8,10},{9,11},{10,... | collective-permute-start | bytes 589832 | tf_op jit(solution)/shard_map/ppermute | solution.py:665
  144.8 8.4 %collective-permute-start.15 = (bf16[384,256]{1,0:T(8,128)(2,1)S(1)}, bf16[384,256]{1,0:T(8,128)(2,1)S(1)}, u32[]{:S(2)}, u32[]{:S(2)}) collective-permute-start(bf16[384,256]{1,0:T(8,128)(2,1)S(1)} %get-tuple-element.111.refs_2_.refs_0_), channel_id=1, source_target_pairs={{0,16},{1,17},{2,18},{3,19},{4,20},{5,21},{6,22},{7,23},{8,24},{9,... | collective-permute-start | bytes 589832 | tf_op jit(solution)/shard_map/ppermute | solution.py:665
  153.2 3.6 %collective-permute-start.18 = (bf16[1536,256]{1,0:T(8,128)(2,1)S(1)}, bf16[1536,256]{1,0:T(8,128)(2,1)S(1)}, u32[]{:S(2)}, u32[]{:S(2)}) collective-permute-start(bf16[1536,256]{1,0:T(8,128)(2,1)S(1)} %bitcast.16), channel_id=1, source_target_pairs={{0,1},{1,0},{2,3},{3,2},{4,5},{5,4},{6,7},{7,6},{8,9},{9,8},{10,11... | collective-permute-start | bytes 2359304 | tf_op jit(solution)/shard_map/ppermute | solution.py:665
  153.3 8.7 %collective-permute-start.14 = (bf16[384,256]{1,0:T(8,128)(2,1)S(1)}, bf16[384,256]{1,0:T(8,128)(2,1)S(1)}, u32[]{:S(2)}, u32[]{:S(2)}) collective-permute-start(bf16[384,256]{1,0:T(8,128)(2,1)S(1)} %get-tuple-element.112.refs_4_.refs_0_), channel_id=1, source_target_pairs={{0,18},{1,19},{2,16},{3,17},{4,22},{5,23},{6,20},{7,21},{8,26},{9,... | collective-permute-start | bytes 589832 | tf_op jit(solution)/shard_map/ppermute | solution.py:665
  154.9 10.9 %collective-permute-start.13 = (bf16[384,256]{1,0:T(8,128)(2,1)S(1)}, bf16[384,256]{1,0:T(8,128)(2,1)S(1)}, u32[]{:S(2)}, u32[]{:S(2)}) collective-permute-start(bf16[384,256]{1,0:T(8,128)(2,1)S(1)} %get-tuple-element.112.refs_4_.refs_0_), channel_id=1, source_target_pairs={{0,2},{1,3},{2,0},{3,1},{4,6},{5,7},{6,4},{7,5},{8,10},{9,11},{10,... | collective-permute-start | bytes 589832 | tf_op jit(solution)/shard_map/ppermute | solution.py:665
  156.1 9.7 %collective-permute-start.12 = (bf16[384,256]{1,0:T(8,128)(2,1)S(1)}, bf16[384,256]{1,0:T(8,128)(2,1)S(1)}, u32[]{:S(2)}, u32[]{:S(2)}) collective-permute-start(bf16[384,256]{1,0:T(8,128)(2,1)S(1)} %get-tuple-element.112.refs_4_.refs_0_), channel_id=1, source_target_pairs={{0,16},{1,17},{2,18},{3,19},{4,20},{5,21},{6,22},{7,23},{8,24},{9,... | collective-permute-start | bytes 589832 | tf_op jit(solution)/shard_map/ppermute | solution.py:665
  165.8 2.4 %collective-permute-start.19 = (bf16[1536,256]{1,0:T(8,128)(2,1)S(1)}, bf16[1536,256]{1,0:T(8,128)(2,1)S(1)}, u32[]{:S(2)}, u32[]{:S(2)}) collective-permute-start(bf16[1536,256]{1,0:T(8,128)(2,1)S(1)} %bitcast.19), channel_id=1, source_target_pairs={{0,1},{1,0},{2,3},{3,2},{4,5},{5,4},{6,7},{7,6},{8,9},{9,8},{10,11... | collective-permute-start | bytes 2359304 | tf_op jit(solution)/shard_map/ppermute | solution.py:665
  (4 other events, 99.7 us)

commit v7 on v6

--- a/solution.py
+++ b/solution.py
@@ -753,8 +753,8 @@
     stream_grad, token = rows_rest(grads, inputs, rows_gains[0], (wq, wk, wv), token)
     while columns.others:
         token = columns.add(token)
+    token = rows_chain.add(token)
     final, token = unpack(final, inputs.shape, token)
-    token = rows_chain.add(token)
     token = columns.last(token)
     columns.spread()
     while rows_chain.others:

time: 171 us -> 171 us (level)
  no operation moved by 1% of the time
where the time goes in v7:
time: 171 us; the launch traced here: 170 us
  waiting for transfers between devices  65.2 us (38%)
  Pallas kernels  53.7 us (31%)
  starting transfers between devices  47.9 us (28%)
  local copies, waits for them, and re-layouts  2.78 us (2%)
    ppermute x20, waiting for transfers between devices, swap(): lax.ppermute(array, ALL, [(i, i ^ mask) for i in range(self.devices)])  42.2 us
    ppermute x20, starting transfers between devices, swap(): lax.ppermute(array, ALL, [(i, i ^ mask) for i in range(self.devices)])  24 us
    all_to_all x4, starting transfers between devices, trade(): return lax.all_to_all(array, 'row', 0, 0, tiled=True)  23.9 us
    all_to_all x4, waiting for transfers between devices, trade(): return lax.all_to_all(array, 'row', 0, 0, tiled=True)  23 us
    pallas_call x1, Pallas kernels, columns_both(): pl.pallas_call(columns_kernel, in_specs=[SCALAR] + [HELD] * 4 + [UNREAD]...  16.4 us
    pallas_call x1, Pallas kernels, rows_forward(): pl.pallas_call(rows_forward_kernel, grid=(1,), in_specs=[whole(array) for...  14.4 us
    pallas_call x1, Pallas kernels, rows_backward(): pl.pallas_call(rows_backward_kernel, in_specs=[SCALAR, HELD] + [UNREAD] *...  12.7 us
    pallas_call x1, Pallas kernels, rows_rest(): pl.pallas_call(rows_rest_kernel, grid=(1,), in_specs=[HELD] * 4 + [whole(...  3.92 us
  transfers between devices with their start and end apart: 24, of which 15 were waited for; matrix products, arithmetic and copies ran while one was open for 0% of the time, Pallas kernels for 21%

profile of v7, /device:TPU:0, one launch (start us, length us, event | category | flops | bytes accessed | tf_op | source)
XLA Modules:
  0.0 170.4 jit_solution(12614349165780630980)
XLA Ops:
  0.7 2.1 %copy.38 = bf16[2,16,48,256]{3,2,0,1:T(8,128)(2,1)} copy(bf16[2,16,48,256]{3,2,1,0:T(8,128)(2,1)} %bitcast.24) | data formatting | bytes 1572864 | tf_op jit(solution)/shard_map/reshape | solution.py:734
  2.7 7.4 %all-to-all-start = ((bf16[16,2,48,256]{3,2,1,0:T(8,128)(2,1)}), bf16[16,2,48,256]{3,2,1,0:T(8,128)(2,1)S(1)}, u32[]{:S(2)}, u32[]{:S(2)}) async-start(bf16[16,2,48,256]{3,2,1,0:T(8,128)(2,1)} %bitcast.15), calls=%async_computation | async-start | bytes 1572864 | tf_op jit(solution)/shard_map/all_to_all | solution.py:729
  10.2 14.4 %rows_forward.1 = (bf16[16,2,48,256]{3,2,1,0:T(8,128)(2,1)}, bf16[2,8,96,256]{3,2,1,0:T(8,128)(2,1)}, bf16[2,8,96,256]{3,2,1,0:T(8,128)(2,1)}, bf16[2,8,96,256]{...) custom-call(bf16[2,8,96,256]{3,2,1,0:T(8,128)(2,1)} %x_ref.3, ...), custom_call_target="tpu_custom_call" | custom-call | flops 1 | bytes 1 | tf_op jit(solution)/shard_map/rows_forward/pallas_call | solution.py:442
  24.5 4.3 %all-to-all-done.up_ref = bf16[16,2,48,256]{3,2,1,0:T(8,128)(2,1)S(1)} async-done(((bf16[16,2,48,256]{3,2,1,0:T(8,128)(2,1)}), bf16[16,2,48,256]{3,2,1,0:T(8,128)(2,1)S(1)}, u32[]{:S(2)}, u32[]{:S(2)}) %all-to-all-start) | async-done | bytes 786464 | tf_op jit(solution)/shard_map/all_to_all | solution.py:729
  28.8 5.5 %all-to-all-start.1 = ((bf16[16,2,48,256]{3,2,1,0:T(8,128)(2,1)}), bf16[16,2,48,256]{3,2,1,0:T(8,128)(2,1)S(1)}, u32[]{:S(2)}, u32[]{:S(2)}) async-start(bf16[16,2,48,256]{3,2,1,0:T(8,128)(2,1)} %get-tuple-element.76), calls=%async_computation.1 | async-start | bytes 1572864 | tf_op jit(solution)/shard_map/all_to_all | solution.py:729
  34.3 18.7 %all-to-all-done.1.x_ref = bf16[16,2,48,256]{3,2,1,0:T(8,128)(2,1)S(1)} async-done(((bf16[16,2,48,256]{3,2,1,0:T(8,128)(2,1)}), bf16[16,2,48,256]{3,2,1,0:T(8,128)(2,1)S(1)}, u32[]{:S(2)}, u32[]{:S(2)}) %all-to-all-start.1) | async-done | bytes 786464 | tf_op jit(solution)/shard_map/all_to_all | solution.py:729
  53.0 16.4 %columns_both.1 = (bf16[16,2,48,256]{3,2,1,0:T(8,128)(2,1)}, bf16[16,2,48,256]{3,2,1,0:T(8,128)(2,1)}, bf16[1552,256]{1,0:T(8,128)(2,1)S(1)}, bf16[1552,256]{1,0:T(8,128)(2,1)S(1)}) custom-call(s32[1]{0:T(128)} %bitcast.core_ref.at_ref, bf16[16,2,48,256]{3,2,1,0:T(8,128)(2,1)S(1)} %all-to-all-done.1.x_ref, bf16[16,2,48,256]{3,2,1,0:T(8,128)(2,1)S(1)} %all-to-all-done.up_ref, ...), custom_call_target="tpu_custom_call" | custom-call | flops 1 | bytes 1 | tf_op jit(solution)/shard_map/columns_both/pallas_call | solution.py:507
  69.5 5.5 %all-to-all-start.2 = ((bf16[16,2,48,256]{3,2,1,0:T(8,128)(2,1)}), bf16[16,2,48,256]{3,2,1,0:T(8,128)(2,1)S(1)}, u32[]{:S(2)}, u32[]{:S(2)}) async-start(bf16[16,2,48,256]{3,2,1,0:T(8,128)(2,1)} %get-tuple-element.78), calls=%async_computation.2 | async-start | bytes 1572864 | tf_op jit(solution)/shard_map/all_to_all | solution.py:729
  81.4 4.4 %collective-permute-done.1.refs_1_ = bf16[400,256]{1,0:T(8,128)(2,1)S(1)} collective-permute-done((bf16[400,256]{1,0:T(8,128)(2,1)S(1)}, bf16[400,256]{1,0:T(8,128)(2,1)S(1)}, u32[]{:S(2)}, u32[]{:S(2)}) %collective-permute-start.1) | collective-permute-done | bytes 204832 | tf_op jit(solution)/shard_map/ppermute | solution.py:665
  85.8 9.7 %collective-permute-done.2.refs_2_ = bf16[400,256]{1,0:T(8,128)(2,1)S(1)} collective-permute-done((bf16[400,256]{1,0:T(8,128)(2,1)S(1)}, bf16[400,256]{1,0:T(8,128)(2,1)S(1)}, u32[]{:S(2)}, u32[]{:S(2)}) %collective-permute-start.2) | collective-permute-done | bytes 204832 | tf_op jit(solution)/shard_map/ppermute | solution.py:665
  96.3 5.5 %all-to-all-start.3 = ((bf16[16,2,48,256]{3,2,1,0:T(8,128)(2,1)}), bf16[16,2,48,256]{3,2,1,0:T(8,128)(2,1)S(1)}, u32[]{:S(2)}, u32[]{:S(2)}) async-start(bf16[16,2,48,256]{3,2,1,0:T(8,128)(2,1)} %get-tuple-element.86), calls=%async_computation.3 | async-start | bytes 1572864 | tf_op jit(solution)/shard_map/all_to_all | solution.py:729
  101.8 12.7 %rows_backward.1 = (f32[1536,256]{1,0:T(8,128)S(1)}, bf16[1536,256]{1,0:T(8,128)(2,1)S(1)}, bf16[1536,256]{1,0:T(8,128)(2,1)S(1)}, bf16[1536,256]{1,0:T(8,128)(2...) custom-call(s32[1]{0:T(128)} %bitcast.core_ref.at_ref, ...), custom_call_target="tpu_custom_call" | custom-call | flops 1 | bytes 1 | tf_op jit(solution)/shard_map/rows_backward/pallas_call | solution.py:461
  121.0 3.9 %rows_rest.1 = (f32[2,8,96,256]{3,2,1,0:T(8,128)}, f32[8,128]{1,0:T(8,128)S(1)}) custom-call(f32[1536,256]{1,0:T(8,128)S(1)} %get-tuple-element.103.mid_grad_ref, bf16[1536,256]{1,0:T(8,128)(2,1)S(1)} %get-tuple-element.104.dq_ref, bf16[1536,256]{1,0:T(8,128)(2,1)S(1)} %get-tuple-element.105.dk_ref, bf16[1536,256]{1,0:T(8,128)(2,1)S(1)} %get-tuple-element.106.dv_ref, ...), custom_call_target="tpu_custom_call" | custom-call | flops 1 | bytes 1 | tf_op jit(solution)/shard_map/rows_rest/pallas_call | solution.py:477
  124.9 2.8 %collective-permute-start.10 = (bf16[400,256]{1,0:T(8,128)(2,1)S(1)}, bf16[400,256]{1,0:T(8,128)(2,1)S(1)}, u32[]{:S(2)}, u32[]{:S(2)}) collective-permute-start(bf16[400,256]{1,0:T(8,128)(2,1)S(1)} %sum_split.9.refs_4_.refs_0_), channel_id=1, source_target_pairs={{0,8},{1,9},{2,10},{3,11},{4,12},{5,13},{6,14},{7,15},{8,0},{9,1},... | collective-permute-start | bytes 614408 | tf_op jit(solution)/shard_map/ppermute | solution.py:665
  133.1 3.8 %collective-permute-done.10.refs_1_ = bf16[400,256]{1,0:T(8,128)(2,1)S(1)} collective-permute-done((bf16[400,256]{1,0:T(8,128)(2,1)S(1)}, bf16[400,256]{1,0:T(8,128)(2,1)S(1)}, u32[]{:S(2)}, u32[]{:S(2)}) %collective-permute-start.10) | collective-permute-done | bytes 204832 | tf_op jit(solution)/shard_map/ppermute | solution.py:665
  137.0 3.0 %collective-permute-done.9.refs_1_ = bf16[400,256]{1,0:T(8,128)(2,1)S(1)} collective-permute-done((bf16[400,256]{1,0:T(8,128)(2,1)S(1)}, bf16[400,256]{1,0:T(8,128)(2,1)S(1)}, u32[]{:S(2)}, u32[]{:S(2)}) %collective-permute-start.9) | collective-permute-done | bytes 204832 | tf_op jit(solution)/shard_map/ppermute | solution.py:665
  140.0 2.5 %collective-permute-start.11 = (bf16[400,256]{1,0:T(8,128)(2,1)S(1)}, bf16[400,256]{1,0:T(8,128)(2,1)S(1)}, u32[]{:S(2)}, u32[]{:S(2)}) collective-permute-start(bf16[400,256]{1,0:T(8,128)(2,1)S(1)} %sum_split.11.refs_0_.refs_2_), channel_id=1, source_target_pairs={{0,8},{1,9},{2,10},{3,11},{4,12},{5,13},{6,14},{7,15},{8,0},{9,1},... | collective-permute-start | bytes 614408 | tf_op jit(solution)/shard_map/ppermute | solution.py:665
  143.9 2.1 %collective-permute-start.17 = (bf16[384,256]{1,0:T(8,128)(2,1)S(1)}, bf16[384,256]{1,0:T(8,128)(2,1)S(1)}, u32[]{:S(2)}, u32[]{:S(2)}) collective-permute-start(bf16[384,256]{1,0:T(8,128)(2,1)S(1)} %get-tuple-element.111.refs_2_.refs_0_), channel_id=1, source_target_pairs={{0,18},{1,19},{2,16},{3,17},{4,22},{5,23},{6,20},{7,21},{8,26},{9,... | collective-permute-start | bytes 589832 | tf_op jit(solution)/shard_map/ppermute | solution.py:665
  146.0 5.8 %collective-permute-done.11.refs_1_ = bf16[400,256]{1,0:T(8,128)(2,1)S(1)} collective-permute-done((bf16[400,256]{1,0:T(8,128)(2,1)S(1)}, bf16[400,256]{1,0:T(8,128)(2,1)S(1)}, u32[]{:S(2)}, u32[]{:S(2)}) %collective-permute-start.11) | collective-permute-done | bytes 204832 | tf_op jit(solution)/shard_map/ppermute | solution.py:665
  157.2 1.9 %finish.2 = (f32[1,256]{1,0:T(1,128)}, f32[256,256]{1,0:T(8,128)}, f32[256,256]{1,0:T(8,128)}, f32[256,256]{1,0:T(8,128)}, f32[256,256]{1,0:T(8,128)}, /*index=5...) custom-call(s32[1]{0:T(128)} %bitcast.core_ref.at_ref, ...), custom_call_target="tpu_custom_call" | custom-call | flops 1 | bytes 1 | tf_op jit(solution)/shard_map/finish/pallas_call | solution.py:637
  159.1 2.3 %collective-permute-done.12.refs_1_ = bf16[384,256]{1,0:T(8,128)(2,1)S(1)} collective-permute-done((bf16[384,256]{1,0:T(8,128)(2,1)S(1)}, bf16[384,256]{1,0:T(8,128)(2,1)S(1)}, u32[]{:S(2)}, u32[]{:S(2)}) %collective-permute-start.12) | collective-permute-done | bytes 196640 | tf_op jit(solution)/shard_map/ppermute | solution.py:665
  161.4 4.7 %collective-permute-done.13.refs_2_ = bf16[384,256]{1,0:T(8,128)(2,1)S(1)} collective-permute-done((bf16[384,256]{1,0:T(8,128)(2,1)S(1)}, bf16[384,256]{1,0:T(8,128)(2,1)S(1)}, u32[]{:S(2)}, u32[]{:S(2)}) %collective-permute-start.13) | collective-permute-done | bytes 196640 | tf_op jit(solution)/shard_map/ppermute | solution.py:665
  166.2 2.3 %collective-permute-done.19.other_ref = bf16[1536,256]{1,0:T(8,128)(2,1)S(1)} collective-permute-done((bf16[1536,256]{1,0:T(8,128)(2,1)S(1)}, bf16[1536,256]{1,0:T(8,128)(2,1)S(1)}, u32[]{:S(2)}, u32[]{:S(2)}) %collective-permute-start.19) | collective-permute-done | bytes 786464 | tf_op jit(solution)/shard_map/ppermute | solution.py:665
  168.5 1.9 %finish.3 = (f32[1,256]{1,0:T(1,128)}, f32[256,256]{1,0:T(8,128)}, f32[256,256]{1,0:T(8,128)}, f32[256,256]{1,0:T(8,128)}, f32[256,256]{1,0:T(8,128)}, /*index=5...) custom-call(s32[1]{0:T(128)} %bitcast.core_ref.at_ref, ...), custom_call_target="tpu_custom_call" | custom-call | flops 1 | bytes 1 | tf_op jit(solution)/shard_map/finish/pallas_call | solution.py:637
  (50 shorter events, 25.9 us)
Async XLA Ops:
  2.7 26.1 %all-to-all-start = ((bf16[16,2,48,256]{3,2,1,0:T(8,128)(2,1)}), bf16[16,2,48,256]{3,2,1,0:T(8,128)(2,1)S(1)}, u32[]{:S(2)}, u32[]{:S(2)}) async-start(bf16[16,2,48,256]{3,2,1,0:T(8,128)(2,1)} %bitcast.15), calls=%async_computation | async-start | bytes 1572864 | tf_op jit(solution)/shard_map/all_to_all | solution.py:729
  28.8 24.2 %all-to-all-start.1 = ((bf16[16,2,48,256]{3,2,1,0:T(8,128)(2,1)}), bf16[16,2,48,256]{3,2,1,0:T(8,128)(2,1)S(1)}, u32[]{:S(2)}, u32[]{:S(2)}) async-start(bf16[16,2,48,256]{3,2,1,0:T(8,128)(2,1)} %get-tuple-element.76), calls=%async_computation.1 | async-start | bytes 1572864 | tf_op jit(solution)/shard_map/all_to_all | solution.py:729
  69.5 26.8 %all-to-all-start.2 = ((bf16[16,2,48,256]{3,2,1,0:T(8,128)(2,1)}), bf16[16,2,48,256]{3,2,1,0:T(8,128)(2,1)S(1)}, u32[]{:S(2)}, u32[]{:S(2)}) async-start(bf16[16,2,48,256]{3,2,1,0:T(8,128)(2,1)} %get-tuple-element.78), calls=%async_computation.2 | async-start | bytes 1572864 | tf_op jit(solution)/shard_map/all_to_all | solution.py:729
  75.0 2.4 %collective-permute-start = (bf16[1552,256]{1,0:T(8,128)(2,1)S(1)}, bf16[1552,256]{1,0:T(8,128)(2,1)S(1)}, u32[]{:S(2)}, u32[]{:S(2)}) collective-permute-start(bf16[1552,256]{1,0:T(8,128)(2,1)S(1)} %get-tuple-element.81), channel_id=1, source_target_pairs={{0,1},{1,0},{2,3},{3,2},{4,5},{5,4},{6,7},{7,6},{8,9},{9,8},{10,11... | collective-permute-start | bytes 2383880 | tf_op jit(solution)/shard_map/ppermute | solution.py:665
  77.8 8.0 %collective-permute-start.1 = (bf16[400,256]{1,0:T(8,128)(2,1)S(1)}, bf16[400,256]{1,0:T(8,128)(2,1)S(1)}, u32[]{:S(2)}, u32[]{:S(2)}) collective-permute-start(bf16[400,256]{1,0:T(8,128)(2,1)S(1)} %get-tuple-element.83), channel_id=1, source_target_pairs={{0,16},{1,17},{2,18},{3,19},{4,20},{5,21},{6,22},{7,23},{8,24},{9,... | collective-permute-start | bytes 614408 | tf_op jit(solution)/shard_map/ppermute | solution.py:665
  79.4 16.1 %collective-permute-start.2 = (bf16[400,256]{1,0:T(8,128)(2,1)S(1)}, bf16[400,256]{1,0:T(8,128)(2,1)S(1)}, u32[]{:S(2)}, u32[]{:S(2)}) collective-permute-start(bf16[400,256]{1,0:T(8,128)(2,1)S(1)} %get-tuple-element.84), channel_id=1, source_target_pairs={{0,2},{1,3},{2,0},{3,1},{4,6},{5,7},{6,4},{7,5},{8,10},{9,11},{10,... | collective-permute-start | bytes 614408 | tf_op jit(solution)/shard_map/ppermute | solution.py:665
  81.3 14.2 %collective-permute-start.3 = (bf16[400,256]{1,0:T(8,128)(2,1)S(1)}, bf16[400,256]{1,0:T(8,128)(2,1)S(1)}, u32[]{:S(2)}, u32[]{:S(2)}) collective-permute-start(bf16[400,256]{1,0:T(8,128)(2,1)S(1)} %get-tuple-element.85), channel_id=1, source_target_pairs={{0,18},{1,19},{2,16},{3,17},{4,22},{5,23},{6,20},{7,21},{8,26},{9,... | collective-permute-start | bytes 614408 | tf_op jit(solution)/shard_map/ppermute | solution.py:665
  96.3 35.8 %all-to-all-start.3 = ((bf16[16,2,48,256]{3,2,1,0:T(8,128)(2,1)}), bf16[16,2,48,256]{3,2,1,0:T(8,128)(2,1)S(1)}, u32[]{:S(2)}, u32[]{:S(2)}) async-start(bf16[16,2,48,256]{3,2,1,0:T(8,128)(2,1)} %get-tuple-element.86), calls=%async_computation.3 | async-start | bytes 1572864 | tf_op jit(solution)/shard_map/all_to_all | solution.py:729
  114.5 2.4 %collective-permute-start.4 = (bf16[1552,256]{1,0:T(8,128)(2,1)S(1)}, bf16[1552,256]{1,0:T(8,128)(2,1)S(1)}, u32[]{:S(2)}, u32[]{:S(2)}) collective-permute-start(bf16[1552,256]{1,0:T(8,128)(2,1)S(1)} %get-tuple-element.98), channel_id=1, source_target_pairs={{0,1},{1,0},{2,3},{3,2},{4,5},{5,4},{6,7},{7,6},{8,9},{9,8},{10,11... | collective-permute-start | bytes 2383880 | tf_op jit(solution)/shard_map/ppermute | solution.py:665
  115.0 9.9 %collective-permute-start.8 = (bf16[400,256]{1,0:T(8,128)(2,1)S(1)}, bf16[400,256]{1,0:T(8,128)(2,1)S(1)}, u32[]{:S(2)}, u32[]{:S(2)}) collective-permute-start(bf16[400,256]{1,0:T(8,128)(2,1)S(1)} %copy-done.1), channel_id=1, source_target_pairs={{0,4},{1,5},{2,6},{3,7},{4,0},{5,1},{6,2},{7,3},{8,12},{9,13},{10,... | collective-permute-start | bytes 614408 | tf_op jit(solution)/shard_map/ppermute | solution.py:665
  117.4 10.4 %collective-permute-start.5 = (bf16[400,256]{1,0:T(8,128)(2,1)S(1)}, bf16[400,256]{1,0:T(8,128)(2,1)S(1)}, u32[]{:S(2)}, u32[]{:S(2)}) collective-permute-start(bf16[400,256]{1,0:T(8,128)(2,1)S(1)} %get-tuple-element.100), channel_id=1, source_target_pairs={{0,16},{1,17},{2,18},{3,19},{4,20},{5,21},{6,22},{7,23},{8,24},{9,... | collective-permute-start | bytes 614408 | tf_op jit(solution)/shard_map/ppermute | solution.py:665
  118.2 10.7 %collective-permute-start.6 = (bf16[400,256]{1,0:T(8,128)(2,1)S(1)}, bf16[400,256]{1,0:T(8,128)(2,1)S(1)}, u32[]{:S(2)}, u32[]{:S(2)}) collective-permute-start(bf16[400,256]{1,0:T(8,128)(2,1)S(1)} %get-tuple-element.101), channel_id=1, source_target_pairs={{0,2},{1,3},{2,0},{3,1},{4,6},{5,7},{6,4},{7,5},{8,10},{9,11},{10,... | collective-permute-start | bytes 614408 | tf_op jit(solution)/shard_map/ppermute | solution.py:665
  120.1 10.2 %collective-permute-start.7 = (bf16[400,256]{1,0:T(8,128)(2,1)S(1)}, bf16[400,256]{1,0:T(8,128)(2,1)S(1)}, u32[]{:S(2)}, u32[]{:S(2)}) collective-permute-start(bf16[400,256]{1,0:T(8,128)(2,1)S(1)} %get-tuple-element.102), channel_id=1, source_target_pairs={{0,18},{1,19},{2,16},{3,17},{4,22},{5,23},{6,20},{7,21},{8,26},{9,... | collective-permute-start | bytes 614408 | tf_op jit(solution)/shard_map/ppermute | solution.py:665
  124.9 12.0 %collective-permute-start.10 = (bf16[400,256]{1,0:T(8,128)(2,1)S(1)}, bf16[400,256]{1,0:T(8,128)(2,1)S(1)}, u32[]{:S(2)}, u32[]{:S(2)}) collective-permute-start(bf16[400,256]{1,0:T(8,128)(2,1)S(1)} %sum_split.9.refs_4_.refs_0_), channel_id=1, source_target_pairs={{0,8},{1,9},{2,10},{3,11},{4,12},{5,13},{6,14},{7,15},{8,0},{9,1},... | collective-permute-start | bytes 614408 | tf_op jit(solution)/shard_map/ppermute | solution.py:665
  130.4 9.6 %collective-permute-start.9 = (bf16[400,256]{1,0:T(8,128)(2,1)S(1)}, bf16[400,256]{1,0:T(8,128)(2,1)S(1)}, u32[]{:S(2)}, u32[]{:S(2)}) collective-permute-start(bf16[400,256]{1,0:T(8,128)(2,1)S(1)} %sum_split.10._.refs_0_), channel_id=1, source_target_pairs={{0,4},{1,5},{2,6},{3,7},{4,0},{5,1},{6,2},{7,3},{8,12},{9,13},{10,... | collective-permute-start | bytes 614408 | tf_op jit(solution)/shard_map/ppermute | solution.py:665
  140.0 11.8 %collective-permute-start.11 = (bf16[400,256]{1,0:T(8,128)(2,1)S(1)}, bf16[400,256]{1,0:T(8,128)(2,1)S(1)}, u32[]{:S(2)}, u32[]{:S(2)}) collective-permute-start(bf16[400,256]{1,0:T(8,128)(2,1)S(1)} %sum_split.11.refs_0_.refs_2_), channel_id=1, source_target_pairs={{0,8},{1,9},{2,10},{3,11},{4,12},{5,13},{6,14},{7,15},{8,0},{9,1},... | collective-permute-start | bytes 614408 | tf_op jit(solution)/shard_map/ppermute | solution.py:665
  142.5 9.3 %collective-permute-start.15 = (bf16[384,256]{1,0:T(8,128)(2,1)S(1)}, bf16[384,256]{1,0:T(8,128)(2,1)S(1)}, u32[]{:S(2)}, u32[]{:S(2)}) collective-permute-start(bf16[384,256]{1,0:T(8,128)(2,1)S(1)} %get-tuple-element.111.refs_2_.refs_0_), channel_id=1, source_target_pairs={{0,16},{1,17},{2,18},{3,19},{4,20},{5,21},{6,22},{7,23},{8,24},{9,... | collective-permute-start | bytes 589832 | tf_op jit(solution)/shard_map/ppermute | solution.py:665
  143.3 10.1 %collective-permute-start.16 = (bf16[384,256]{1,0:T(8,128)(2,1)S(1)}, bf16[384,256]{1,0:T(8,128)(2,1)S(1)}, u32[]{:S(2)}, u32[]{:S(2)}) collective-permute-start(bf16[384,256]{1,0:T(8,128)(2,1)S(1)} %get-tuple-element.111.refs_2_.refs_0_), channel_id=1, source_target_pairs={{0,2},{1,3},{2,0},{3,1},{4,6},{5,7},{6,4},{7,5},{8,10},{9,11},{10,... | collective-permute-start | bytes 589832 | tf_op jit(solution)/shard_map/ppermute | solution.py:665
  143.9 9.6 %collective-permute-start.17 = (bf16[384,256]{1,0:T(8,128)(2,1)S(1)}, bf16[384,256]{1,0:T(8,128)(2,1)S(1)}, u32[]{:S(2)}, u32[]{:S(2)}) collective-permute-start(bf16[384,256]{1,0:T(8,128)(2,1)S(1)} %get-tuple-element.111.refs_2_.refs_0_), channel_id=1, source_target_pairs={{0,18},{1,19},{2,16},{3,17},{4,22},{5,23},{6,20},{7,21},{8,26},{9,... | collective-permute-start | bytes 589832 | tf_op jit(solution)/shard_map/ppermute | solution.py:665
  153.5 3.6 %collective-permute-start.18 = (bf16[1536,256]{1,0:T(8,128)(2,1)S(1)}, bf16[1536,256]{1,0:T(8,128)(2,1)S(1)}, u32[]{:S(2)}, u32[]{:S(2)}) collective-permute-start(bf16[1536,256]{1,0:T(8,128)(2,1)S(1)} %bitcast.16), channel_id=1, source_target_pairs={{0,1},{1,0},{2,3},{3,2},{4,5},{5,4},{6,7},{7,6},{8,9},{9,8},{10,11... | collective-permute-start | bytes 2359304 | tf_op jit(solution)/shard_map/ppermute | solution.py:665
  153.6 7.8 %collective-permute-start.12 = (bf16[384,256]{1,0:T(8,128)(2,1)S(1)}, bf16[384,256]{1,0:T(8,128)(2,1)S(1)}, u32[]{:S(2)}, u32[]{:S(2)}) collective-permute-start(bf16[384,256]{1,0:T(8,128)(2,1)S(1)} %get-tuple-element.112.refs_4_.refs_0_), channel_id=1, source_target_pairs={{0,16},{1,17},{2,18},{3,19},{4,20},{5,21},{6,22},{7,23},{8,24},{9,... | collective-permute-start | bytes 589832 | tf_op jit(solution)/shard_map/ppermute | solution.py:665
  154.9 11.2 %collective-permute-start.13 = (bf16[384,256]{1,0:T(8,128)(2,1)S(1)}, bf16[384,256]{1,0:T(8,128)(2,1)S(1)}, u32[]{:S(2)}, u32[]{:S(2)}) collective-permute-start(bf16[384,256]{1,0:T(8,128)(2,1)S(1)} %get-tuple-element.112.refs_4_.refs_0_), channel_id=1, source_target_pairs={{0,2},{1,3},{2,0},{3,1},{4,6},{5,7},{6,4},{7,5},{8,10},{9,11},{10,... | collective-permute-start | bytes 589832 | tf_op jit(solution)/shard_map/ppermute | solution.py:665
  155.4 10.7 %collective-permute-start.14 = (bf16[384,256]{1,0:T(8,128)(2,1)S(1)}, bf16[384,256]{1,0:T(8,128)(2,1)S(1)}, u32[]{:S(2)}, u32[]{:S(2)}) collective-permute-start(bf16[384,256]{1,0:T(8,128)(2,1)S(1)} %get-tuple-element.112.refs_4_.refs_0_), channel_id=1, source_target_pairs={{0,18},{1,19},{2,16},{3,17},{4,22},{5,23},{6,20},{7,21},{8,26},{9,... | collective-permute-start | bytes 589832 | tf_op jit(solution)/shard_map/ppermute | solution.py:665
  166.1 2.4 %collective-permute-start.19 = (bf16[1536,256]{1,0:T(8,128)(2,1)S(1)}, bf16[1536,256]{1,0:T(8,128)(2,1)S(1)}, u32[]{:S(2)}, u32[]{:S(2)}) collective-permute-start(bf16[1536,256]{1,0:T(8,128)(2,1)S(1)} %bitcast.19), channel_id=1, source_target_pairs={{0,1},{1,0},{2,3},{3,2},{4,5},{5,4},{6,7},{7,6},{8,9},{9,8},{10,11... | collective-permute-start | bytes 2359304 | tf_op jit(solution)/shard_map/ppermute | solution.py:665
  (4 other events, 99.7 us)
